TPU v7x, 32 devices: a whole 2x2x4 slice. The times are simulated.
32 devices in a mesh: seq: 4 (over y, x), fsdp: 8 (over z, core).
Axes of the slice: x: 2, y: 2, z: 4, core: 2. Of those that a mesh axis runs over, the one named last changes fastest.
Arguments:
- inputs: bfloat16 [8, 1024, 2048], P('fsdp', 'seq'), may hold values from -6 to 6
- doc_starts: int32 [8, 8], P('fsdp'), may hold values from 0 to 1023, as said below
- ln_gain: bfloat16 [2048], P('fsdp'), may hold values from 0.5 to 1.5
- ln_bias: bfloat16 [2048], P('fsdp'), may hold values from -0.5 to 0.5
- w_qkv: bfloat16 [2048, 6144], P('fsdp'), may hold values from -0.125 to 0.125
- b_qkv: bfloat16 [6144], P('fsdp'), may hold values from -0.5 to 0.5
- w_out: bfloat16 [2048, 2048], P('fsdp'), may hold values from -0.75 to 0.75
- b_out: bfloat16 [2048], P('fsdp'), may hold values from -0.5 to 0.5
- w_fc1: bfloat16 [2048, 8192], P('fsdp'), may hold values from -0.125 to 0.125
- b_fc1: bfloat16 [8192], P('fsdp'), may hold values from -0.5 to 0.5
- w_fc2: bfloat16 [8192, 2048], P('fsdp'), may hold values from -0.0625 to 0.0625
- b_fc2: bfloat16 [2048], P('fsdp'), may hold values from -0.5 to 0.5
- cotangent: bfloat16 [8, 1024, 2048], P('fsdp', 'seq'), may hold values from -6 to 6
Outputs:
- output: bfloat16 [8, 1024, 2048], P('fsdp', 'seq')
- grad_inputs: float32 [8, 1024, 2048], P('fsdp', 'seq')
- grad_ln_gain: float32 [2048], P('fsdp')
- grad_ln_bias: float32 [2048], P('fsdp')
- grad_w_qkv: float32 [2048, 6144], P('fsdp')
- grad_b_qkv: float32 [6144], P('fsdp')
- grad_w_out: float32 [2048, 2048], P('fsdp')
- grad_b_out: float32 [2048], P('fsdp')
- grad_w_fc1: float32 [2048, 8192], P('fsdp')
- grad_b_fc1: float32 [8192], P('fsdp')
- grad_w_fc2: float32 [8192, 2048], P('fsdp')
- grad_b_fc2: float32 [2048], P('fsdp')
Inputs may be any that keep to these rules, and one draw needn't show every extreme that they name: `doc_starts`: in every sequence the starts rise strictly, the first is 0 and the last is 1023; document k covers the positions from its start up to the next start, the last one only position 1023.
All inputs are finite; a program needn't handle non-finite values.
Results may differ from a plain program's by a relative error of at most 0.009.
Values may be sent and summed in bfloat16 or wider, within the bound.
No kernel may reach another device: no remote copies, remote signals or barrier semaphores. Data moves between devices by JAX's collectives and lax.ppermute only.
A program may use at most 704 MiB of HBM per device.

v0:
```python
import jax
import jax.numpy as jnp
from jax import lax
from jax.sharding import PartitionSpec as P

HEADS = 32
HEAD_DIM = 64
ROT = 32


eps_norm = 1e-05


def gelu_tanh(values):
    return (
        0.5
        * values
        * (1.0 + jnp.tanh(0.7978845608028654 * (values + 0.044715 * values * values * values)))
    )


def rotate(pairs, cosine, sine):
    half_rot = cosine.shape[-1]
    leading = pairs[..., :half_rot]
    trailing = pairs[..., half_rot : 2 * half_rot]
    return jnp.concatenate(
        [
            leading * cosine - trailing * sine,
            trailing * cosine + leading * sine,
            pairs[..., 2 * half_rot :],
        ],
        axis=-1,
    )


def unrotate(pairs, cosine, sine):
    half_rot = cosine.shape[-1]
    leading = pairs[..., :half_rot]
    trailing = pairs[..., half_rot : 2 * half_rot]
    return jnp.concatenate(
        [
            leading * cosine + trailing * sine,
            trailing * cosine - leading * sine,
            pairs[..., 2 * half_rot :],
        ],
        axis=-1,
    )


def segments(starts_row, positions):
    before = starts_row[None, :] <= positions[:, None]
    opening = jnp.max(jnp.where(before, starts_row[None, :], 0), axis=1)
    return (opening, jnp.sum(before.astype(jnp.int32), axis=1))


def turning(starts_row, positions):
    opening, unused = segments(starts_row, positions)
    rates = 10000.0 ** (-2.0 * jnp.arange(ROT // 2, dtype=jnp.float32) / ROT)
    angle = (positions - opening).astype(jnp.float32)[:, None] * rates[None, :]
    return (jnp.cos(angle), jnp.sin(angle))


def masked_scores(query_rows, query_pos, query_seg, key_all, key_pos, key_seg, score_scale):
    raw = (
        jnp.einsum("qhd,khd->hqk", query_rows, key_all, preferred_element_type=jnp.float32)
        * score_scale
    )
    allowed = (key_pos[None, :] <= query_pos[:, None]) & (key_seg[None, :] == query_seg[:, None])
    return jnp.where(allowed[None], raw, -1000000000.0)


def contract_rows(left, right):
    return lax.dot_general(
        left, right, (((0,), (0,)), ((), ())), preferred_element_type=jnp.float32
    )


def contract_cols(left, right):
    return lax.dot_general(
        left, right, (((1,), (1,)), ((), ())), preferred_element_type=jnp.float32
    )


def rows_term(left, right):
    return contract_rows(left, right)


def per_device(
    inputs,
    doc_starts,
    ln_gain,
    ln_bias,
    w_qkv,
    b_qkv,
    w_out,
    b_out,
    w_fc1,
    b_fc1,
    w_fc2,
    b_fc2,
    cotangent,
):
    gathered = (
        lax.all_gather(ln_gain, "fsdp", axis=0, tiled=True),
        lax.all_gather(ln_bias, "fsdp", axis=0, tiled=True),
        lax.all_gather(b_qkv, "fsdp", axis=0, tiled=True),
        lax.all_gather(b_out, "fsdp", axis=0, tiled=True),
        lax.all_gather(b_fc1, "fsdp", axis=0, tiled=True),
        lax.all_gather(b_fc2, "fsdp", axis=0, tiled=True),
        lax.all_gather(w_qkv, "fsdp", axis=0, tiled=True),
        lax.all_gather(w_out, "fsdp", axis=0, tiled=True),
        lax.all_gather(w_fc1, "fsdp", axis=0, tiled=True),
        lax.all_gather(w_fc2, "fsdp", axis=0, tiled=True),
    )
    gain_all, shift_all, bias_qkv, bias_out, bias_fc1, bias_fc2 = [
        vector.astype(jnp.float32) for vector in gathered[:6]
    ]
    whole_qkv, whole_out, whole_fc1, whole_fc2 = gathered[6:]
    tok_count = inputs.shape[1]
    feature_count = inputs.shape[2]
    seq_parts = lax.axis_size("seq")
    heads_here = HEADS // seq_parts
    seq_length = tok_count * seq_parts
    block_rows = min(512, seq_length)
    block_count = seq_length // block_rows
    score_scale = HEAD_DIM ** (-0.5)
    starts_row = doc_starts[0]
    rows_in = inputs[0].astype(jnp.float32)
    centred = rows_in - jnp.mean(rows_in, axis=-1, keepdims=True)
    inv_std = lax.rsqrt(jnp.mean(centred * centred, axis=-1, keepdims=True) + eps_norm)
    normal_hat = centred * inv_std
    normed = (normal_hat * gain_all + shift_all).astype(jnp.bfloat16)
    own_pos = lax.axis_index("seq") * tok_count + jnp.arange(tok_count, dtype=jnp.int32)
    cosine, sine = turning(starts_row, own_pos)
    cosine = cosine[:, None, None, :]
    sine = sine[:, None, None, :]
    qkv_pre = jnp.dot(normed, whole_qkv, preferred_element_type=jnp.float32) + bias_qkv
    qkv_pre = qkv_pre.reshape(tok_count, HEADS, 3, HEAD_DIM)
    packed = jnp.concatenate([rotate(qkv_pre[:, :, :2], cosine, sine), qkv_pre[:, :, 2:]], axis=2)
    packed = packed.astype(jnp.bfloat16).reshape(tok_count, 3 * feature_count)
    by_heads = lax.all_to_all(packed, "seq", split_axis=1, concat_axis=0, tiled=True).reshape(
        seq_length, heads_here, 3, HEAD_DIM
    )
    query_all = by_heads[:, :, 0]
    key_all = by_heads[:, :, 1]
    value_all = by_heads[:, :, 2]
    all_pos = jnp.arange(seq_length, dtype=jnp.int32)
    unused_open, all_seg = segments(starts_row, all_pos)

    def block_scores(index):
        begin = index * block_rows
        return masked_scores(
            lax.dynamic_slice_in_dim(query_all, begin, block_rows, 0),
            lax.dynamic_slice_in_dim(all_pos, begin, block_rows, 0),
            lax.dynamic_slice_in_dim(all_seg, begin, block_rows, 0),
            key_all,
            all_pos,
            all_seg,
            score_scale,
        )

    def forward_block(index):
        scores = block_scores(index)
        top_score = jnp.max(scores, axis=-1, keepdims=True)
        expo = jnp.exp(scores - top_score)
        row_totals = jnp.sum(expo, axis=-1, keepdims=True)
        probs = (expo / row_totals).astype(jnp.bfloat16)
        mixed_block = jnp.einsum(
            "hqk,khd->qhd", probs, value_all, preferred_element_type=jnp.float32
        )
        return (mixed_block, top_score + jnp.log(row_totals))

    mixed_all, log_norms = lax.map(forward_block, jnp.arange(block_count, dtype=jnp.int32))
    mixed_heads = mixed_all.reshape(seq_length, heads_here * HEAD_DIM).astype(jnp.bfloat16)
    mixed_tok = lax.all_to_all(mixed_heads, "seq", split_axis=0, concat_axis=1, tiled=True)
    attn_out = jnp.dot(mixed_tok, whole_out, preferred_element_type=jnp.float32) + bias_out
    hidden_pre = jnp.dot(normed, whole_fc1, preferred_element_type=jnp.float32) + bias_fc1
    active, gelu_pull = jax.vjp(gelu_tanh, hidden_pre)
    active = active.astype(jnp.bfloat16)
    result = (
        rows_in
        + attn_out
        + jnp.dot(active, whole_fc2, preferred_element_type=jnp.float32)
        + bias_fc2
    )
    output = result.astype(jnp.bfloat16)[None]
    whole_qkv, whole_out, whole_fc1, whole_fc2 = (
        lax.all_gather(w_qkv, "fsdp", axis=0, tiled=True),
        lax.all_gather(w_out, "fsdp", axis=0, tiled=True),
        lax.all_gather(w_fc1, "fsdp", axis=0, tiled=True),
        lax.all_gather(w_fc2, "fsdp", axis=0, tiled=True),
    )
    grad_rows = cotangent[0]
    grad_mixed = contract_cols(grad_rows, whole_out).astype(jnp.bfloat16)
    grad_hidden = gelu_pull(contract_cols(grad_rows, whole_fc2))[0].astype(jnp.bfloat16)
    grad_heads = lax.all_to_all(grad_mixed, "seq", split_axis=1, concat_axis=0, tiled=True).reshape(
        seq_length, heads_here, HEAD_DIM
    )

    def backward_block(carry, item):
        grad_key, grad_value = carry
        index, log_norm = item
        begin = index * block_rows
        query_rows = lax.dynamic_slice_in_dim(query_all, begin, block_rows, 0)
        grad_block = lax.dynamic_slice_in_dim(grad_heads, begin, block_rows, 0)
        probs = jnp.exp(block_scores(index) - log_norm)
        grad_probs = jnp.einsum(
            "qhd,khd->hqk", grad_block, value_all, preferred_element_type=jnp.float32
        )
        row_dots = jnp.sum(probs * grad_probs, axis=-1, keepdims=True)
        grad_scores = (probs * (grad_probs - row_dots)).astype(jnp.bfloat16)
        grad_query = (
            jnp.einsum("hqk,khd->qhd", grad_scores, key_all, preferred_element_type=jnp.float32)
            * score_scale
        )
        grad_key = (
            grad_key
            + jnp.einsum(
                "hqk,qhd->khd", grad_scores, query_rows, preferred_element_type=jnp.float32
            )
            * score_scale
        )
        grad_value = grad_value + jnp.einsum(
            "hqk,qhd->khd",
            probs.astype(jnp.bfloat16),
            grad_block,
            preferred_element_type=jnp.float32,
        )
        return ((grad_key, grad_value), grad_query)

    zero_grads = jnp.zeros((seq_length, heads_here, HEAD_DIM), jnp.float32)
    (grad_key, grad_value), grad_query = lax.scan(
        backward_block,
        (zero_grads, zero_grads),
        (jnp.arange(block_count, dtype=jnp.int32), log_norms),
    )
    grad_query = grad_query.reshape(seq_length, heads_here, HEAD_DIM)
    grad_packed = jnp.stack([grad_query, grad_key, grad_value], axis=2).astype(jnp.bfloat16)
    grad_packed = grad_packed.reshape(seq_length, heads_here * 3 * HEAD_DIM)
    grad_tok = lax.all_to_all(grad_packed, "seq", split_axis=0, concat_axis=1, tiled=True)
    grad_tok = grad_tok.reshape(tok_count, HEADS, 3, HEAD_DIM).astype(jnp.float32)
    grad_qkv = jnp.concatenate(
        [unrotate(grad_tok[:, :, :2], cosine, sine), grad_tok[:, :, 2:]], axis=2
    )
    grad_qkv = grad_qkv.astype(jnp.bfloat16).reshape(tok_count, 3 * feature_count)
    part_qkv = lax.psum_scatter(
        rows_term(normed, grad_qkv), "fsdp", scatter_dimension=0, tiled=True
    )
    part_out = lax.psum_scatter(
        rows_term(mixed_tok, grad_rows), "fsdp", scatter_dimension=0, tiled=True
    )
    part_fc1 = lax.psum_scatter(
        rows_term(normed, grad_hidden), "fsdp", scatter_dimension=0, tiled=True
    )
    part_fc2 = lax.psum_scatter(
        rows_term(active, grad_rows), "fsdp", scatter_dimension=0, tiled=True
    )
    grad_normed = contract_cols(grad_qkv, whole_qkv) + contract_cols(grad_hidden, whole_fc1)
    grad_gain = jnp.sum(grad_normed * normal_hat, axis=0)
    grad_shift = jnp.sum(grad_normed, axis=0)
    scaled = grad_normed * gain_all
    grad_in = grad_rows.astype(jnp.float32) + inv_std * (
        scaled
        - jnp.mean(scaled, axis=-1, keepdims=True)
        - normal_hat * jnp.mean(scaled * normal_hat, axis=-1, keepdims=True)
    )
    sum_qkv_bias = jnp.sum(grad_qkv.astype(jnp.float32), axis=0)
    sum_out_bias = jnp.sum(grad_rows.astype(jnp.float32), axis=0)
    sum_fc1_bias = jnp.sum(grad_hidden.astype(jnp.float32), axis=0)
    shard_gain, shard_shift, shard_bqkv, shard_bout, shard_bfc1 = (
        lax.psum_scatter(grad_gain, "fsdp", scatter_dimension=0, tiled=True),
        lax.psum_scatter(grad_shift, "fsdp", scatter_dimension=0, tiled=True),
        lax.psum_scatter(sum_qkv_bias, "fsdp", scatter_dimension=0, tiled=True),
        lax.psum_scatter(sum_out_bias, "fsdp", scatter_dimension=0, tiled=True),
        lax.psum_scatter(sum_fc1_bias, "fsdp", scatter_dimension=0, tiled=True),
    )
    (
        total_gain,
        total_shift,
        total_bqkv,
        total_bout,
        total_bfc1,
        total_wqkv,
        total_wout,
        total_wfc1,
        total_wfc2,
    ) = lax.psum(
        (
            shard_gain,
            shard_shift,
            shard_bqkv,
            shard_bout,
            shard_bfc1,
            part_qkv,
            part_out,
            part_fc1,
            part_fc2,
        ),
        "seq",
    )
    return (
        output,
        grad_in[None],
        total_gain,
        total_shift,
        total_wqkv,
        total_bqkv,
        total_wout,
        total_bout,
        total_wfc1,
        total_bfc1,
        total_wfc2,
        total_bout,
    )


def solution(mesh):
    return jax.shard_map(
        per_device,
        mesh=mesh,
        in_specs=(
            P("fsdp", "seq", None),
            P("fsdp", None),
            P("fsdp"),
            P("fsdp"),
            P("fsdp", None),
            P("fsdp"),
            P("fsdp", None),
            P("fsdp"),
            P("fsdp", None),
            P("fsdp"),
            P("fsdp", None),
            P("fsdp"),
            P("fsdp", "seq", None),
        ),
        out_specs=(
            P("fsdp", "seq", None),
            P("fsdp", "seq", None),
            P("fsdp"),
            P("fsdp"),
            P("fsdp", None),
            P("fsdp"),
            P("fsdp", None),
            P("fsdp"),
            P("fsdp", None),
            P("fsdp"),
            P("fsdp", None),
            P("fsdp"),
        ),
        check_vma=False,
    )
```

profile of v0, /device:TPU:0, one launch (start us, length us, event | category | flops | bytes accessed | tf_op | source)
XLA Modules:
  0.0 3358.0 jit_solution(4762439200795551928)
XLA Ops:
  10.1 13.4 all-gather.1
  32.4 16.7 all-gather.2
  50.1 182.5 %all-gather.10.cloned.1.call-done = bf16[2048,6144]{1,0:T(8,128)(2,1)} async-done(((bf16[256,6144]{1,0:T(8,128)(2,1)}), bf16[2048,6144]{1,0:T(8,128)(2,1)}) %all-gather.10.cloned.1.call-update) | async-done | bytes 25165840 | tf_op jit(solution)/shard_map/all_gather | solution.py:110
  232.6 14.0 convolution_add_fusion.1
  264.4 36.6 %all-to-all-done = bf16[256,4,1536]{0,2,1:T(8,128)(2,1)S(1)} async-done(((bf16[256,4,1536]{0,2,1:T(8,128)(2,1)}), bf16[256,4,1536]{0,2,1:T(8,128)(2,1)S(1)}, u32[]{:S(2)}, u32[]{:S(2)}) %all-to-all-start) | async-done | bytes 3145760 | tf_op jit(solution)/shard_map/all_to_all | solution.py:141
  301.0 13.1 copy.53
  324.3 34.1 %while.29 = (s32[]{:T(128)}, bf16[2,512,8,64]{1,3,2,0:T(8,128)(2,1)S(1)}, f32[2,8,512,1]{2,1,3,0:T(8,128)}, s32[1024]{0:T(1024)S(1)}, s32[2]{0:T(128)S(1)}, /*in...) while((s32[]{:T(128)}, ...), condition=%wide.region_7.8_spmd.clone, body=%wide.region_4.7_spmd.clone.sunk | while | flops 1125642240 | bytes 56250576 | solution.py:173
  363.8 16.2 all_to_all.55
  399.7 12.0 all-to-all-done.2
  415.1 91.5 %while.30 = (s32[]{:T(128)}, f32[1024,8,64]{0,2,1:T(8,128)}, f32[1024,8,64]{0,2,1:T(8,128)}, bf16[2,512,8,64]{1,3,2,0:T(8,128)(2,1)}, s32[2]{0:T(128)S(1)}, /*in...) while((s32[]{:T(128)}, f32[1024,8,64]{0,2,1:T(8,128)}, ...), condition=%wide.region_10.11_spmd.clone.clone, body=%wide.region_8.10_spmd.clone.clone.sunk | while | flops 2726555648 | bytes 187797872 | solution.py:232
  422.8 11.6 multiply_reduce_fusion.3
  434.4 9.4 multiply_convert_fusion.5
  467.8 11.6 multiply_reduce_fusion.3
  488.8 9.8 bitcast_add_fusion.5
  519.3 38.8 %all_to_all.56 = bf16[4,256,1536]{1,2,0:T(8,128)(2,1)S(1)} all-to-all(bf16[4,256,1536]{1,2,0:T(8,128)(2,1)S(1)} %copy.60), channel_id=1, replica_groups=mesh['seq'=4,'fsdp'=8] {'seq'}, dimensions={0} | all-to-all | bytes 6291456 | tf_op jit(solution)/shard_map/all_to_all | solution.py:240
  562.0 21.7 fusion.55
  584.4 12.8 all_gather.41
  603.3 21.4 convolution_add_fusion
  624.7 27.8 fusion.57
  652.6 239.0 %all-gather.16.cloned.1.call-done = bf16[8192,2048]{1,0:T(8,128)(2,1)} async-done(((bf16[1024,2048]{1,0:T(8,128)(2,1)}), bf16[8192,2048]{1,0:T(8,128)(2,1)}) %all-gather.16.cloned.1.call-update) | async-done | bytes 33554448 | tf_op jit(solution)/shard_map/all_gather | solution.py:113
  891.6 23.2 convert_reduce_fusion
  914.8 26.0 fusion.70
  942.4 13.9 fusion.74
  956.3 18.9 fusion.47
  980.0 80.3 %reduce-scatter.7.cloned.1.call-done = f32[256,2048]{1,0:T(8,128)} async-done(((f32[2048,2048]{1,0:T(8,128)}), f32[256,2048]{1,0:T(8,128)}) %reduce-scatter.7.cloned.1.call-update) | async-done | bytes 2097168 | tf_op jit(solution)/shard_map/reduce_scatter | solution.py:249
  1060.3 483.8 %reduce-scatter.5.cloned.1.call-done = f32[256,6144]{1,0:T(8,128)} async-done(((f32[2048,6144]{1,0:T(8,128)}), f32[256,6144]{1,0:T(8,128)}) %reduce-scatter.5.cloned.1.call-update) | async-done | bytes 6291472 | tf_op jit(solution)/shard_map/reduce_scatter | solution.py:246
  1544.1 641.0 %reduce-scatter.11.cloned.1.call-done = f32[1024,2048]{1,0:T(8,128)} async-done(((f32[8192,2048]{1,0:T(8,128)}), f32[1024,2048]{1,0:T(8,128)}) %reduce-scatter.11.cloned.1.call-update) | async-done | bytes 8388624 | tf_op jit(solution)/shard_map/reduce_scatter | solution.py:255
  2185.1 640.9 %reduce-scatter.9.cloned.1.call-done = f32[256,8192]{1,0:T(8,128)} async-done(((f32[2048,8192]{1,0:T(8,128)}), f32[256,8192]{1,0:T(8,128)}) %reduce-scatter.9.cloned.1.call-update) | async-done | bytes 8388624 | tf_op jit(solution)/shard_map/reduce_scatter | solution.py:252
  2838.4 9.7 all-gather.3
  2855.1 20.1 fusion.41
  2882.8 16.8 all-reduce.6
  2899.6 433.4 %all-reduce.13.cloned.1.call-done = (f32[256,6144]{1,0:T(8,128)}, f32[256,2048]{1,0:T(8,128)}, f32[256,8192]{1,0:T(8,128)}, f32[1024,2048]{1,0:T(8,128)}) async-done(((f32[256,6144]{1,0:T(8,128)}, f32[256,2048]{1,0:T(8,128)}, f32[256,8192]{1,0:T(8,128)}, f32[1024,2048]{1,0:T(8,128)}), (f32[256,6144]{1,0:T(8,128)}, f32[256,2048]{1,0:T(8,128)}, f32[256,8192]{1,0:T(8,128)}, ...) | async-done | bytes 25165840 | tf_op jit(solution)/shard_map/psum | solution.py:287
  (219 shorter events, 221.6 us)
Async XLA Ops:
  7.2 41.9 %copy-start.25 = (s32[1,8]{1,0:T(1,128)S(1)}, s32[1,8]{1,0:T(1,128)}, u32[]{:S(2)}) copy-start(s32[1,8]{1,0:T(1,128)} %param.18) | copy-start | bytes 100
  7.2 42.0 %copy-start.1 = (bf16[1,256,2048]{2,1,0:T(8,128)(2,1)S(1)}, bf16[1,256,2048]{2,1,0:T(8,128)(2,1)}, u32[]{:S(2)}) copy-start(bf16[1,256,2048]{2,1,0:T(8,128)(2,1)} %param.17) | copy-start | bytes 3145732
  7.2 225.3 %all-gather.10.cloned.1.call-start = ((), (), s32[]{:S(2)}) async-start(), calls=%async_computation.8 | async-start | bytes 28311552 | tf_op jit(solution)/shard_map/all_gather | solution.py:110
  8.0 381.2 %all-gather.12.cloned.1.call-start = ((), (), s32[]{:S(2)}) async-start(), calls=%async_computation.9 | async-start | bytes 9437184 | tf_op jit(solution)/shard_map/all_gather | solution.py:111
  8.7 594.6 %all-gather.14.cloned.1.call-start = ((), (), s32[]{:S(2)}) async-start(), calls=%async_computation.10 | async-start | bytes 37748736 | tf_op jit(solution)/shard_map/all_gather | solution.py:112
  9.4 882.2 %all-gather.16.cloned.1.call-start = ((), (), s32[]{:S(2)}) async-start(), calls=%async_computation.11 | async-start | bytes 37748736 | tf_op jit(solution)/shard_map/all_gather | solution.py:113
  23.6 223.0 %copy-start.13 = (f32[8,1,256]{2,1,0:T(1,128)}, f32[8,1,256]{2,1,0:T(1,128)S(1)}, u32[]{:S(2)}) copy-start(f32[8,1,256]{2,1,0:T(1,128)S(1)} %convert_element_type.153) | copy-start | bytes 24580
  32.4 214.2 %copy-start.11 = (f32[8,1,256]{2,1,0:T(1,128)}, f32[8,1,256]{2,1,0:T(1,128)S(1)}, u32[]{:S(2)}) copy-start(f32[8,1,256]{2,1,0:T(1,128)S(1)} %convert_element_type.152) | copy-start | bytes 24580
  49.5 197.1 %copy-start.16 = (f32[256]{0:T(256)}, f32[256]{0:T(256)S(1)}, u32[]{:S(2)}) copy-start(f32[256]{0:T(256)S(1)} %broadcast_multiply_fusion.2) | copy-start | bytes 3076
  49.9 196.7 %copy-start.22 = (f32[256]{0:T(256)}, f32[256]{0:T(256)S(1)}, u32[]{:S(2)}) copy-start(f32[256]{0:T(256)S(1)} %add_rsqrt_fusion) | copy-start | bytes 3076
  50.1 206.6 %copy-start.18 = (f32[256,16]{0,1:T(8,128)}, f32[256,16]{0,1:T(8,128)S(1)}, u32[]{:S(2)}) copy-start(f32[256,16]{0,1:T(8,128)S(1)} %get-tuple-element.311) | copy-start | bytes 49156
  50.1 206.6 %copy-start.20 = (f32[256,16]{0,1:T(8,128)}, f32[256,16]{0,1:T(8,128)S(1)}, u32[]{:S(2)}) copy-start(f32[256,16]{0,1:T(8,128)S(1)} %get-tuple-element.312) | copy-start | bytes 49156
  260.5 40.4 %all-to-all-start = ((bf16[256,4,1536]{0,2,1:T(8,128)(2,1)}), bf16[256,4,1536]{0,2,1:T(8,128)(2,1)S(1)}, u32[]{:S(2)}, u32[]{:S(2)}) async-start(bf16[256,4,1536]{0,2,1:T(8,128)(2,1)} %bitcast.186), calls=%async_computation | async-start | bytes 6291456 | tf_op jit(solution)/shard_map/all_to_all | solution.py:141
  264.2 796.1 %reduce-scatter.7.cloned.1.call-start = ((), (), s32[]{:S(2)}) async-start(), calls=%async_computation.13 | async-start | bytes 18874368 | tf_op jit(solution)/shard_map/reduce_scatter | solution.py:249
  358.4 22.5 copy-start.6
  396.1 15.5 all-to-all-start.2
  399.6 1144.5 %reduce-scatter.5.cloned.1.call-start = ((), (), s32[]{:S(2)}) async-start(), calls=%async_computation.12 | async-start | bytes 56623104 | tf_op jit(solution)/shard_map/reduce_scatter | solution.py:246
  434.4 9.4 copy-start.3
  443.9 9.2 copy-start
  443.9 9.2 copy-start.8
  479.4 9.4 copy-start.3
  488.8 9.8 copy-start
  488.8 9.8 copy-start.8
  583.8 1601.3 %reduce-scatter.11.cloned.1.call-start = ((), (), s32[]{:S(2)}) async-start(), calls=%async_computation.15 | async-start | bytes 75497472 | tf_op jit(solution)/shard_map/reduce_scatter | solution.py:255
  597.2 27.6 copy-start.7
  652.6 2173.4 %reduce-scatter.9.cloned.1.call-start = ((), (), s32[]{:S(2)}) async-start(), calls=%async_computation.14 | async-start | bytes 75497472 | tf_op jit(solution)/shard_map/reduce_scatter | solution.py:252
  940.9 1938.2 %all-reduce.11.cloned.1.call-start = ((), (), s32[]{:S(2)}) async-start(), calls=%async_computation.16 | async-start | bytes 163840
  980.0 2353.0 %all-reduce.13.cloned.1.call-start = ((), (), s32[]{:S(2)}) async-start(), calls=%async_computation.17 | async-start | bytes 50331648 | tf_op jit(solution)/shard_map/psum | solution.py:287
  2826.0 22.1 copy-start.5
  2899.6 440.6 %copy-start.27 = (f32[256]{0:T(256)}, f32[256]{0:T(256)S(1)}, u32[]{:S(2)}) copy-start(f32[256]{0:T(256)S(1)} %get-tuple-element.572) | copy-start | bytes 3076
  3333.0 8.5 slice-start.2
  3333.6 7.9 slice-start.3
  (21 other events, 63.9 us)
Sparse Core Ops, SparseCore 0:
  9.7 222.7 all-gather.9
  234.1 80.2 all-gather.11
  316.0 287.2 all-gather.13
  604.8 286.8 all-gather.15
  893.8 166.4 reduce-scatter.6
  1062.5 481.4 reduce-scatter.4
  1546.5 638.4 reduce-scatter.10
  2187.4 638.4 reduce-scatter.8
  2830.0 49.0 all-reduce.10
  2882.9 450.0 all-reduce.12
where the time goes:
time: 3370 us; the launch traced here: 3360 us
  waiting for transfers between devices  2760 us (82%)
  matrix products  293 us (9%)
  blocking collectives  142 us (4%)
  local copies, waits for them, and re-layouts  81.5 us (2%)
  other arithmetic  51.5 us (2%)
    reduce_scatter x1, waiting for transfers between devices, per_device(): lax.psum_scatter(rows_term(active, grad_rows), 'fsdp', scatter_dimension=...  641 us
    reduce_scatter x1, waiting for transfers between devices, per_device(): lax.psum_scatter(rows_term(normed, grad_hidden), 'fsdp', scatter_dimensio...  641 us
    reduce_scatter x1, waiting for transfers between devices, per_device(): lax.psum_scatter(rows_term(normed, grad_qkv), 'fsdp', scatter_dimension=0...  484 us
    psum x1, waiting for transfers between devices, per_device(): lax.psum((shard_gain, shard_shift, shard_bqkv, shard_bout, shard_bfc1, pa...  433 us
    all_gather x1, waiting for transfers between devices, per_device(): lax.all_gather(w_fc2, 'fsdp', axis=0, tiled=True)  239 us
    all_gather x1, waiting for transfers between devices, per_device(): lax.all_gather(w_qkv, 'fsdp', axis=0, tiled=True)  182 us
    dot_general x4, matrix products, contract_rows(): lax.dot_general(left, right, (((0,), (0,)), ((), ())), preferred_element_...  83.7 us
    reduce_scatter x1, waiting for transfers between devices, per_device(): lax.psum_scatter(rows_term(mixed_tok, grad_rows), 'fsdp', scatter_dimensi...  80.3 us
  transfers between devices with their start and end apart: 12, of which 11 were waited for; matrix products, arithmetic and copies ran while one was open for 12% of the time, Pallas kernels for 0%

commit v1 on v0

v1 whole, which is shorter than its diff:
```python
import jax
import jax.numpy as jnp
from jax import lax
from jax.sharding import PartitionSpec as P

HEADS = 32
HEAD_DIM = 64
ROT = 32
EPS = 1e-05
BF = jnp.bfloat16
F32 = jnp.float32


def gelu_tanh(values):
    return (
        0.5
        * values
        * (1.0 + jnp.tanh(0.7978845608028654 * (values + 0.044715 * values * values * values)))
    )


def segments(starts_row, positions):
    before = starts_row[None, :] <= positions[:, None]
    opening = jnp.max(jnp.where(before, starts_row[None, :], 0), axis=1)
    return (opening, jnp.sum(before.astype(jnp.int32), axis=1))


def turning(starts_row, positions):
    opening, unused = segments(starts_row, positions)
    rates = 10000.0 ** (-2.0 * jnp.arange(ROT // 2, dtype=F32) / ROT)
    angle = (positions - opening).astype(F32)[:, None] * rates[None, :]
    return (jnp.cos(angle), jnp.sin(angle))


def rotate(pairs, cosine, sine):
    half = cosine.shape[-1]
    lead, trail = pairs[..., :half], pairs[..., half : 2 * half]
    return jnp.concatenate(
        [lead * cosine - trail * sine, trail * cosine + lead * sine, pairs[..., 2 * half :]],
        axis=-1,
    )


def mm(left, right, left_dim=1, right_dim=0):
    return lax.dot_general(
        left, right, (((left_dim,), (right_dim,)), ((), ())), preferred_element_type=F32
    )


def pick(array, index, axis=0):
    return lax.dynamic_index_in_dim(array, index, axis, keepdims=False)


def swap_seq(array, step):
    count = lax.axis_size("seq")
    return lax.ppermute(array, "seq", [(i, i ^ step) for i in range(count)])


def seq_gather(block):
    count = lax.axis_size("seq")
    me = lax.axis_index("seq")
    whole = jnp.zeros((count,) + block.shape, block.dtype)
    whole = lax.dynamic_update_index_in_dim(whole, block, me, 0)
    for step in range(1, count):
        whole = lax.dynamic_update_index_in_dim(whole, swap_seq(block, step), me ^ step, 0)
    return whole


def seq_sum(blocks):
    count = lax.axis_size("seq")
    me = lax.axis_index("seq")
    total = pick(blocks, me).astype(F32)
    for step in range(1, count):
        total = total + swap_seq(pick(blocks, me ^ step), step).astype(F32)
    return total


def line_sum(parts):
    count = parts.shape[0]
    chips = count // 2
    me = lax.axis_index("fsdp")
    chip, core = me // 2, me % 2
    parts = parts.reshape((chips, 2) + parts.shape[1:])
    got = lax.ppermute(pick(parts, 1 - core, 1), "fsdp", [(i, i ^ 1) for i in range(count)])
    own = (pick(parts, core, 1).astype(F32) + got.astype(F32)).astype(parts.dtype)

    def of(index):
        return pick(own, jnp.clip(index, 0, chips - 1))

    total = of(chip).astype(F32)
    down, up = of(chip - (chips - 1)), of(chip + (chips - 1))
    for step in range(1, chips):
        down_pairs = [(2 * a + c, 2 * (a - 1) + c) for a in range(chips - step, chips) for c in (0, 1)]
        up_pairs = [(2 * a + c, 2 * (a + 1) + c) for a in range(0, step) for c in (0, 1)]
        got_down = lax.ppermute(down, "fsdp", down_pairs).astype(F32)
        got_up = lax.ppermute(up, "fsdp", up_pairs).astype(F32)
        if step < chips - 1:
            down = (got_down + of(chip - (chips - step - 1)).astype(F32)).astype(parts.dtype)
            up = (got_up + of(chip + (chips - step - 1)).astype(F32)).astype(parts.dtype)
    return total + got_down + got_up


def fsdp_gather(block):
    return lax.all_gather(block, "fsdp", axis=0, tiled=True)


def attention(query, key, value, grad_of, seg, score_scale):
    length = query.shape[0]
    rows = min(512, length)
    blocks = length // rows
    pos = jnp.arange(length, dtype=jnp.int32)

    def block_scores(index):
        begin = index * rows
        raw = (
            jnp.einsum(
                "qhd,khd->hqk",
                lax.dynamic_slice_in_dim(query, begin, rows, 0),
                key,
                preferred_element_type=F32,
            )
            * score_scale
        )
        q_pos = lax.dynamic_slice_in_dim(pos, begin, rows, 0)
        q_seg = lax.dynamic_slice_in_dim(seg, begin, rows, 0)
        allowed = (pos[None, :] <= q_pos[:, None]) & (seg[None, :] == q_seg[:, None])
        return jnp.where(allowed[None], raw, -1000000000.0)

    def forward_block(index):
        scores = block_scores(index)
        top = jnp.max(scores, axis=-1, keepdims=True)
        expo = jnp.exp(scores - top)
        totals = jnp.sum(expo, axis=-1, keepdims=True)
        probs = (expo / totals).astype(BF)
        return (
            jnp.einsum("hqk,khd->qhd", probs, value, preferred_element_type=F32),
            top + jnp.log(totals),
        )

    mixed, log_norms = lax.map(forward_block, jnp.arange(blocks, dtype=jnp.int32))
    mixed = mixed.reshape(query.shape).astype(BF)
    grad_heads = grad_of()

    def backward_block(carry, item):
        grad_key, grad_value = carry
        index, log_norm = item
        begin = index * rows
        q_rows = lax.dynamic_slice_in_dim(query, begin, rows, 0)
        g_rows = lax.dynamic_slice_in_dim(grad_heads, begin, rows, 0)
        probs = jnp.exp(block_scores(index) - log_norm)
        grad_probs = jnp.einsum("qhd,khd->hqk", g_rows, value, preferred_element_type=F32)
        dots = jnp.sum(probs * grad_probs, axis=-1, keepdims=True)
        grad_scores = (probs * (grad_probs - dots)).astype(BF)
        grad_query = (
            jnp.einsum("hqk,khd->qhd", grad_scores, key, preferred_element_type=F32) * score_scale
        )
        grad_key = (
            grad_key
            + jnp.einsum("hqk,qhd->khd", grad_scores, q_rows, preferred_element_type=F32)
            * score_scale
        )
        grad_value = grad_value + jnp.einsum(
            "hqk,qhd->khd", probs.astype(BF), g_rows, preferred_element_type=F32
        )
        return ((grad_key, grad_value), grad_query)

    zero = jnp.zeros(query.shape, F32)
    (grad_key, grad_value), grad_query = lax.scan(
        backward_block, (zero, zero), (jnp.arange(blocks, dtype=jnp.int32), log_norms)
    )
    return mixed, grad_query.reshape(query.shape), grad_key, grad_value


def per_device(
    inputs,
    doc_starts,
    ln_gain,
    ln_bias,
    w_qkv,
    b_qkv,
    w_out,
    b_out,
    w_fc1,
    b_fc1,
    w_fc2,
    b_fc2,
    cotangent,
):
    seqs = lax.axis_size("seq")
    shards = lax.axis_size("fsdp")
    me = lax.axis_index("seq")
    tok, width = inputs.shape[1:]
    length = tok * seqs
    rows_here = w_qkv.shape[0]
    heads = HEADS // seqs
    head_cols = heads * HEAD_DIM
    shard_heads = w_out.shape[0] // HEAD_DIM
    strided = shard_heads % seqs == 0
    unit = w_fc2.shape[0] // seqs
    hidden_cols = unit * shards
    score_scale = HEAD_DIM ** (-0.5)

    fc1_here = pick(w_fc1.reshape(rows_here, shards, seqs, unit), me, 2).reshape(
        rows_here, hidden_cols
    )
    fc2_here = pick(w_fc2.reshape(seqs, unit, width), me)
    if strided:
        each = shard_heads // seqs
        qkv_here = pick(w_qkv.reshape(rows_here, shards, seqs, each, 3, HEAD_DIM), me, 2)
        out_here = pick(w_out.reshape(seqs, each * HEAD_DIM, width), me)
    else:
        qkv_here = pick(w_qkv.reshape(rows_here, seqs, heads, 3, HEAD_DIM), me, 1)
        out_here = w_out
    qkv_here = qkv_here.reshape(rows_here, heads, 3, HEAD_DIM).transpose(0, 2, 1, 3)
    qkv_here = qkv_here.reshape(rows_here, 3 * head_cols)

    fc1 = fsdp_gather(fc1_here)
    fc2 = fsdp_gather(fc2_here)
    qkv_w = fsdp_gather(qkv_here)
    out_w = fsdp_gather(out_here)
    if not strided:
        out_w = pick(out_w.reshape(seqs, head_cols, width), me)

    sizes = [v.shape[0] for v in (ln_gain, ln_bias, b_out, b_fc2, b_qkv, b_fc1)]
    small = fsdp_gather(jnp.concatenate([ln_gain, ln_bias, b_out, b_fc2, b_qkv, b_fc1])[None])
    small = small.astype(F32)
    cuts = [sum(sizes[:i]) for i in range(len(sizes) + 1)]
    gain, shift, bias_out, bias_fc2, bias_qkv, bias_fc1 = [
        small[:, a:b].reshape(-1) for a, b in zip(cuts[:-1], cuts[1:])
    ]
    bias_fc1 = pick(bias_fc1.reshape(shards, seqs, unit), me, 1).reshape(hidden_cols)
    if strided:
        bias_qkv = pick(bias_qkv.reshape(shards, seqs, each, 3, HEAD_DIM), me, 1)
    else:
        bias_qkv = pick(bias_qkv.reshape(seqs, heads, 3, HEAD_DIM), me)
    bias_qkv = bias_qkv.reshape(heads, 3, HEAD_DIM).transpose(1, 0, 2).reshape(3 * head_cols)

    rows_all = seq_gather(inputs[0]).reshape(length, width)
    grad_rows = seq_gather(cotangent[0]).reshape(length, width)
    starts_row = doc_starts[0]
    pos = jnp.arange(length, dtype=jnp.int32)
    unused_open, seg = segments(starts_row, pos)
    cosine, sine = turning(starts_row, pos)
    cosine, sine = cosine[:, None, :], sine[:, None, :]

    centred = rows_all.astype(F32)
    centred = centred - jnp.mean(centred, axis=-1, keepdims=True)
    inv_std = lax.rsqrt(jnp.mean(centred * centred, axis=-1, keepdims=True) + EPS)
    normal_hat = centred * inv_std
    normed = (normal_hat * gain + shift).astype(BF)

    hidden = mm(normed, fc1) + bias_fc1
    active, pull = jax.vjp(gelu_tanh, hidden)
    active = active.astype(BF)
    part_fc2 = line_sum(mm(active, grad_rows, 0, 0).astype(BF).reshape(shards, unit, width))
    grad_hidden = pull(mm(grad_rows, fc2, 1, 1))[0].astype(BF)
    part_fc1 = line_sum(
        mm(normed, grad_hidden, 0, 0).astype(BF).reshape(shards, rows_here, hidden_cols)
    )

    qkv = mm(normed, qkv_w) + bias_qkv
    query, key, value = [
        qkv[:, i * head_cols : (i + 1) * head_cols].reshape(length, heads, HEAD_DIM)
        for i in range(3)
    ]
    query = rotate(query, cosine, sine).astype(BF)
    key = rotate(key, cosine, sine).astype(BF)
    value = value.astype(BF)
    mixed, grad_query, grad_key, grad_value = attention(
        query,
        key,
        value,
        lambda: mm(grad_rows, out_w, 1, 1).astype(BF).reshape(length, heads, HEAD_DIM),
        seg,
        score_scale,
    )
    mixed = mixed.reshape(length, head_cols)
    out_grad = mm(mixed, grad_rows, 0, 0).astype(BF)
    if strided:
        part_out = line_sum(out_grad.reshape(shards, each * HEAD_DIM, width))
    else:
        spread = jnp.zeros((seqs, head_cols, width), BF)
        spread = lax.dynamic_update_index_in_dim(spread, out_grad, me, 0)
        part_out = line_sum(spread.reshape(shards, shard_heads * HEAD_DIM, width))
    grad_qkv = jnp.concatenate(
        [rotate(grad_query, cosine, -sine), rotate(grad_key, cosine, -sine), grad_value], axis=1
    )
    grad_qkv = grad_qkv.reshape(length, 3 * head_cols).astype(BF)
    part_qkv = line_sum(
        mm(normed, grad_qkv, 0, 0).astype(BF).reshape(shards, rows_here, 3 * head_cols)
    )

    partial = (mm(mixed, out_w) + mm(active, fc2)).astype(BF)
    result = seq_sum(partial.reshape(seqs, tok, width))
    output = (inputs[0].astype(F32) + result + (bias_out + bias_fc2)).astype(BF)[None]

    grad_partial = mm(grad_qkv, qkv_w, 1, 1) + mm(grad_hidden, fc1, 1, 1)
    sum_gain = jnp.sum(grad_partial * normal_hat, axis=0)
    sum_shift = jnp.sum(grad_partial, axis=0)
    grad_normed = seq_sum(grad_partial.astype(BF).reshape(seqs, tok, width))
    own_hat = pick(normal_hat.reshape(seqs, tok, width), me)
    own_std = pick(inv_std.reshape(seqs, tok, 1), me)
    scaled = grad_normed * gain
    grad_in = cotangent[0].astype(F32) + own_std * (
        scaled
        - jnp.mean(scaled, axis=-1, keepdims=True)
        - own_hat * jnp.mean(scaled * own_hat, axis=-1, keepdims=True)
    )

    sum_fc1 = jnp.sum(grad_hidden.astype(F32), axis=0).reshape(shards, unit)
    sum_fc1 = lax.dynamic_update_index_in_dim(
        jnp.zeros((shards, seqs, unit), F32), sum_fc1, me, 1
    )
    sum_qkv = jnp.sum(grad_qkv.astype(F32), axis=0).reshape(3, heads, HEAD_DIM).transpose(1, 0, 2)
    if strided:
        sum_qkv = lax.dynamic_update_index_in_dim(
            jnp.zeros((shards, seqs, each, 3, HEAD_DIM), F32),
            sum_qkv.reshape(shards, each, 3, HEAD_DIM),
            me,
            1,
        )
    else:
        sum_qkv = lax.dynamic_update_index_in_dim(
            jnp.zeros((seqs, heads, 3, HEAD_DIM), F32), sum_qkv, me, 0
        )
    sum_out = jnp.sum(cotangent[0].astype(F32), axis=0)
    vectors = jnp.concatenate(
        [v.reshape(shards, -1) for v in (sum_gain, sum_shift, sum_out, sum_qkv, sum_fc1)], axis=1
    )
    vectors = line_sum(vectors[:, None, :])[0]
    vectors = jnp.sum(seq_gather(vectors[None]), axis=(0, 1))
    ends = [sizes[0], sizes[1], sizes[2], sizes[4], sizes[5]]
    ends = [sum(ends[:i]) for i in range(len(ends) + 1)]
    total_gain, total_shift, total_bout, total_bqkv, total_bfc1 = [
        vectors[a:b] for a, b in zip(ends[:-1], ends[1:])
    ]

    total_wfc2 = seq_gather(part_fc2.astype(BF)).reshape(seqs * unit, width).astype(F32)
    total_wfc1 = seq_gather(part_fc1.astype(BF)).reshape(seqs, rows_here, shards, unit)
    total_wfc1 = total_wfc1.transpose(1, 2, 0, 3).reshape(rows_here, -1).astype(F32)
    total_qkv = seq_gather(part_qkv.astype(BF))
    if strided:
        total_wout = seq_gather(part_out.astype(BF)).reshape(-1, width).astype(F32)
        total_qkv = total_qkv.reshape(seqs, rows_here, 3, shards, each, HEAD_DIM)
        total_qkv = total_qkv.transpose(1, 3, 0, 4, 2, 5)
    else:
        total_wout = jnp.sum(seq_gather(part_out.astype(BF)).astype(F32), axis=0)
        total_qkv = total_qkv.reshape(seqs, rows_here, 3, heads, HEAD_DIM).transpose(1, 0, 3, 2, 4)
    total_wqkv = total_qkv.reshape(rows_here, -1).astype(F32)
    return (
        output,
        grad_in[None],
        total_gain,
        total_shift,
        total_wqkv,
        total_bqkv,
        total_wout,
        total_bout,
        total_wfc1,
        total_bfc1,
        total_wfc2,
        total_bout,
    )


def solution(mesh):
    rows, vector, matrix = P("fsdp", "seq", None), P("fsdp"), P("fsdp", None)
    return jax.shard_map(
        per_device,
        mesh=mesh,
        in_specs=(
            rows,
            matrix,
            vector,
            vector,
            matrix,
            vector,
            matrix,
            vector,
            matrix,
            vector,
            matrix,
            vector,
            rows,
        ),
        out_specs=(
            rows,
            rows,
            vector,
            vector,
            matrix,
            vector,
            matrix,
            vector,
            matrix,
            vector,
            matrix,
            vector,
        ),
        check_vma=False,
    )
```

time: 3370 us -> 906 us (0.27)
  waiting for transfers between devices: 2760 us -> 235 us
  blocking collectives: 142 us -> 14.1 us
  starting transfers between devices: 7.62 us -> 115 us
  local copies, waits for them, and re-layouts: 81.5 us -> 183 us
  matrix products: 293 us -> 223 us
  other arithmetic: 51.5 us -> 106 us
    reduce_scatter x4 -> x0, waiting for transfers between devices: 1850 us -> none  [the longest x1 641 us: per_device(): lax.psum_scatter(rows_term(active, grad_rows), 'fsdp', scatter_dimension=...]
    psum x1 -> x0, waiting for transfers between devices: 433 us -> none  [per_device(): lax.psum((shard_gain, shard_shift, shard_bqkv, shard_bout, shard_bfc1, pa...]
    all_gather x4, waiting for transfers between devices: 428 us -> 0.01 us  [fsdp_gather(): return lax.all_gather(block, 'fsdp', axis=0, tiled=True)]
    ppermute x0 -> x62, waiting for transfers between devices: none -> 235 us  [the longest x27 159 us: swap_seq(): return lax.ppermute(array, 'seq', [(i, i ^ step) for i in range(count)])]
    ppermute x0 -> x62, starting transfers between devices: none -> 115 us  [the longest x15 65.9 us: line_sum(): got_up = lax.ppermute(up, 'fsdp', up_pairs).astype(F32)]
    dot_general x26, matrix products: 293 us -> 223 us  [the longest x12 143 us: mm(): lax.dot_general(left, right, (((left_dim,), (right_dim,)), ((), ())), pre...]
    dynamic_update_slice x0 -> x30, local copies, waits for them, and re-layouts: none -> 60.7 us  [the longest x4 43.3 us: attention(): lax.map(forward_block, jnp.arange(blocks, dtype=jnp.int32))]
    all_gather x6 -> x1, blocking collectives: 70.5 us -> 14.1 us  [fsdp_gather(): return lax.all_gather(block, 'fsdp', axis=0, tiled=True)]
  transfers between devices with their start and end apart: 12 -> 66, of which waited for: 11 -> 24; matrix products, arithmetic and copies ran while one was open for 12% -> 53% of each run, Pallas kernels for 0% -> 0%
where the time goes in v1:
time: 906 us; the launch traced here: 895 us
  waiting for transfers between devices  235 us (26%)
  matrix products  223 us (25%)
  local copies, waits for them, and re-layouts  183 us (20%)
  starting transfers between devices  115 us (13%)
  other arithmetic  106 us (12%)
  between operations  15.7 us (2%)
  blocking collectives  14.1 us (2%)
    ppermute x27, waiting for transfers between devices, swap_seq(): return lax.ppermute(array, 'seq', [(i, i ^ step) for i in range(count)])  159 us
    dot_general x12, matrix products, mm(): lax.dot_general(left, right, (((left_dim,), (right_dim,)), ((), ())), pre...  143 us
    ppermute x15, waiting for transfers between devices, line_sum(): got_up = lax.ppermute(up, 'fsdp', up_pairs).astype(F32)  76.4 us
    ppermute x15, starting transfers between devices, line_sum(): got_up = lax.ppermute(up, 'fsdp', up_pairs).astype(F32)  65.9 us
    dynamic_update_slice x4, local copies, waits for them, and re-layouts, attention(): lax.map(forward_block, jnp.arange(blocks, dtype=jnp.int32))  43.3 us
    unnamed x137, local copies, waits for them, and re-layouts  39.4 us
    ppermute x27, starting transfers between devices, swap_seq(): return lax.ppermute(array, 'seq', [(i, i ^ step) for i in range(count)])  33.8 us
    dot_general x4, matrix products, block_scores(): jnp.einsum('qhd,khd->hqk', lax.dynamic_slice_in_dim(query, begin, rows, 0...  31.2 us
  transfers between devices with their start and end apart: 66, of which 24 were waited for; matrix products, arithmetic and copies ran while one was open for 53% of the time, Pallas kernels for 0%

profile of v1, /device:TPU:0, one launch (start us, length us, event | category | flops | bytes accessed | tf_op | source)
XLA Modules:
  0.0 895.3 jit_solution(10907983901382192209)
XLA Ops:
  36.9 14.1 %all-gather.3 = bf16[8,1,2816]{2,1,0:T(2,128)(2,1)S(1)} all-gather(bf16[1,1,2816]{2,1,0:T(2,128)(2,1)S(1)} %reshape.571), channel_id=2, replica_groups=mesh['seq'=4,'fsdp'=8] {'fsdp'}, dimensions={0}, use_global_device_ids=true | all-gather | bytes 50688 | tf_op jit(solution)/shard_map/all_gather | solution.py:104
  66.0 10.3 %collective-permute-done.2 = bf16[256,2048]{1,0:T(8,128)(2,1)} collective-permute-done((bf16[256,2048]{1,0:T(8,128)(2,1)S(1)}, bf16[256,2048]{1,0:T(8,128)(2,1)}, u32[]{:S(2)}, u32[]{:S(2)}) %collective-permute-start.2) | collective-permute-done | bytes 1048608 | tf_op jit(solution)/shard_map/ppermute | solution.py:56
  85.1 14.2 %collective-permute-done.6 = bf16[256,2048]{1,0:T(8,128)(2,1)} collective-permute-done((bf16[256,2048]{1,0:T(8,128)(2,1)S(1)}, bf16[256,2048]{1,0:T(8,128)(2,1)}, u32[]{:S(2)}, u32[]{:S(2)}) %collective-permute-start.6) | collective-permute-done | bytes 1048608 | tf_op jit(solution)/shard_map/ppermute | solution.py:56
  127.5 10.1 %convolution_add_fusion = f32[1024,1536]{1,0:T(8,128)S(1)} fusion(bf16[1024,2048]{1,0:T(8,128)(2,1)} %add_convert_fusion.2, bf16[2048,1536]{0,1:T(8,128)(2,1)} %all-gather.9.cloned.1.call-done, f32[1536]{0:T(1024)S(1)} %add.433), kind=kOutput, calls=%fused_computation.73 | convolution fusion | flops 6444023808 | bytes 16783360 | tf_op jit(solution)/shard_map/dot_general | solution.py:45
  152.0 32.6 %while.29 = (s32[]{:T(128)}, bf16[2,512,8,64]{1,3,2,0:T(8,128)(2,1)S(1)}, f32[2,8,512,1]{2,1,3,0:T(8,128)S(1)}, s32[1024]{0:T(1024)S(1)}, s32[2]{0:T(128)S(1)}, ...) while((s32[]{:T(128)}, ...), condition=%wide.region_7.8_spmd.clone, body=%wide.region_4.7_spmd.clone.sunk | while | flops 1125642240 | bytes 56250576 | solution.py:140
  193.3 129.2 %while.30 = (s32[]{:T(128)}, f32[1024,8,64]{0,2,1:T(8,128)}, f32[1024,8,64]{0,2,1:T(8,128)}, f32[2,512,8,64]{1,0,3,2:T(2,128)}, s32[2]{0:T(128)S(1)}, /*index=5*...) while((s32[]{:T(128)}, f32[1024,8,64]{0,2,1:T(8,128)}, ...), condition=%wide.region_10.11_spmd.clone.clone, body=%wide.region_8.10_spmd.clone.clone.sunk | while | flops 2726555648 | bytes 200642992 | solution.py:168
  200.7 11.5 %multiply_reduce_fusion.4 = (f32[8,512]{1,0:T(8,128)}, f32[8,512,1024]{2,1,0:T(8,128)}) fusion(f32[8,512,1024]{2,1,0:T(8,128)S(1)} %fusion.171, f32[8,512]{1,0:T(8,128)} %dynamic-slice_bitcast_fusion.21, bf16[1024,8,64]{0,2,1:T(8,128)(2,1)S(1)} %get-tuple-element.646, bf16[1024,8,64]{0,2,1:T(8,128)(2,1)} %get-tuple-element.643, s32[]{:T(128)S(6)} %select_n.209, ...), kind=kOutput, calls=%fused_computation.16.clone.1 | convolution fusion | flops 557838336 | bytes 35684356 | tf_op jit(solution)/shard_map/while/body/eval_jaxpr/qhd,khd->hqk/dot_general | solution.py:116
  238.3 19.6 %dynamic_update_slice.173 = f32[2,512,8,64]{1,0,3,2:T(2,128)} dynamic-update-slice(f32[2,512,8,64]{1,0,3,2:T(2,128)} %get-tuple-element.625, f32[1,512,8,64]{1,0,3,2:T(1,128)} %copy.151, s32[]{:T(128)S(6)} %copy.182, s32[]{:T(128)} %constant.350.clone.1..sunk.1, s32[]{:T(128)} %constant.350.clone.1..sunk.1, s32[]{:T(128)} %constant.350.clone.1..sunk.1) | dynamic-update-slice | bytes 2097156 | tf_op jit(solution)/shard_map/while/body/jit(dynamic_update_index_in_dim)/dynamic_update_slice | solution.py:140
  264.9 11.5 %multiply_reduce_fusion.4 = (f32[8,512]{1,0:T(8,128)}, f32[8,512,1024]{2,1,0:T(8,128)}) fusion(f32[8,512,1024]{2,1,0:T(8,128)S(1)} %fusion.171, f32[8,512]{1,0:T(8,128)} %dynamic-slice_bitcast_fusion.21, bf16[1024,8,64]{0,2,1:T(8,128)(2,1)S(1)} %get-tuple-element.646, bf16[1024,8,64]{0,2,1:T(8,128)(2,1)} %get-tuple-element.643, s32[]{:T(128)S(6)} %select_n.209, ...), kind=kOutput, calls=%fused_computation.16.clone.1 | convolution fusion | flops 557838336 | bytes 35684356 | tf_op jit(solution)/shard_map/while/body/eval_jaxpr/qhd,khd->hqk/dot_general | solution.py:116
  302.9 19.6 %dynamic_update_slice.173 = f32[2,512,8,64]{1,0,3,2:T(2,128)} dynamic-update-slice(f32[2,512,8,64]{1,0,3,2:T(2,128)} %get-tuple-element.625, f32[1,512,8,64]{1,0,3,2:T(1,128)} %copy.151, s32[]{:T(128)S(6)} %copy.182, s32[]{:T(128)} %constant.350.clone.1..sunk.1, s32[]{:T(128)} %constant.350.clone.1..sunk.1, s32[]{:T(128)} %constant.350.clone.1..sunk.1) | dynamic-update-slice | bytes 2097156 | tf_op jit(solution)/shard_map/while/body/jit(dynamic_update_index_in_dim)/dynamic_update_slice | solution.py:140
  383.9 11.7 %collective-permute-done.40 = bf16[64,2048]{1,0:T(8,128)(2,1)S(1)} collective-permute-done((bf16[64,2048]{1,0:T(8,128)(2,1)S(1)}, bf16[64,2048]{1,0:T(8,128)(2,1)S(1)}, u32[]{:S(2)}, u32[]{:S(2)}) %collective-permute-start.40) | collective-permute-done | bytes 262176 | tf_op jit(solution)/shard_map/ppermute | solution.py:56
  409.6 12.7 %fusion.114 = f32[1024,2048]{1,0:T(8,128)S(1)} fusion(bf16[1024,2048]{1,0:T(8,128)(2,1)} %add_convert_fusion.2, bf16[2048,2048]{0,1:T(8,128)(2,1)} %all-gather.11.cloned.1.call-done), kind=kOutput, calls=%fused_computation.264 | convolution fusion | flops 8589934592 | bytes 20971520 | tf_op jit(solution)/shard_map/dot_general | solution.py:45
  425.7 14.8 %convolution_convert_fusion = bf16[2048,2048]{1,0:T(8,128)(2,1)} fusion(bf16[1024,2048]{1,0:T(8,128)(2,1)} %bitcast.33, f32[1024,2048]{1,0:T(8,128)S(1)} %fusion.114, f32[2048]{0:T(1024)S(1)} %bitcast.478), kind=kOutput, calls=%fused_computation.65 | convolution fusion | flops 8615100416 | bytes 20979712 | tf_op jit(solution)/shard_map/dot_general | solution.py:45
  440.5 20.2 %convert_reduce_fusion = (f32[2048]{0:T(1024)S(1)}, bf16[1024,2048]{1,0:T(8,128)(2,1)S(1)}) fusion(bf16[1024,2048]{1,0:T(8,128)(2,1)} %bitcast.33, bf16[1,2048,2048]{2,1,0:T(8,128)(2,1)} %all-gather.15.cloned.1.call-done, f32[1024,2048]{1,0:T(8,128)} %copy-done.52, f32[2048]{0:T(1024)S(1)} %bitcast.479), kind=kOutput, calls=%fused_computation.57 | convolution fusion | flops 8646555648 | bytes 25182208 | tf_op jit(solution)/shard_map/dot_general | solution.py:45
  460.8 14.7 %fusion.115 = f32[1024,2048]{1,0:T(8,128)} fusion(bf16[1024,2048]{1,0:T(8,128)(2,1)S(1)} %get-tuple-element.428, bf16[2048,2048]{0,1:T(8,128)(2,1)} %all-gather.11.cloned.1.call-done), kind=kOutput, calls=%fused_computation.265 | convolution fusion | flops 8589934592 | bytes 20971520 | tf_op jit(solution)/shard_map/dot_general | solution.py:45
  475.5 13.7 %fusion.105 = (f32[2048]{0:T(1024)S(1)}, f32[2048]{0:T(1024)S(1)}, bf16[1024,2048]{1,0:T(8,128)(2,1)S(1)}) fusion(f32[1024]{0:T(1024)S(1)} %bitcast.474, f32[1024]{0:T(1024)S(1)} %bitcast.472, bf16[4,256,2048]{2,1,0:T(8,128)(2,1)} %bitcast_dynamic-update-slice_fusion.12, f32[1024,2048]{1,0:T(8,128)} %fusion.115, bf16[1024,1536]{0,1:T(8,128)(2,1)S(1)} %bitcast.451, ...), kind=kOutput, calls=%fused_computation.260 | convolution fusion | flops 6459224064 | bytes 26238976 | tf_op jit(solution)/shard_map/dot_general | solution.py:45
  493.1 17.2 %add_convert_fusion.1 = bf16[1024,2048]{1,0:T(8,128)(2,1)} fusion(f32[1024,2048]{1,0:T(8,128)} %fusion.69, bf16[1,2048,2048]{2,1,0:T(8,128)(2,1)S(1)} %bitcast.487, f32[1024,2048]{1,0:T(8,128)} %copy-done.52, f32[2048]{0:T(1024)S(1)} %bitcast.480), kind=kOutput, calls=%fused_computation.59 | convolution fusion | flops 8615100416 | bytes 29368320 | tf_op jit(solution)/shard_map/dot_general | solution.py:45
  510.3 13.6 %convolution_convert_fusion.1 = bf16[2048,2048]{1,0:T(8,128)(2,1)} fusion(bf16[1024,2048]{1,0:T(8,128)(2,1)S(1)} %copy-done.16, bf16[1024,2048]{1,0:T(8,128)(2,1)} %copy-done.53), kind=kOutput, calls=%fused_computation.66 | convolution fusion | flops 8594128896 | bytes 16777216 | tf_op jit(solution)/shard_map/dot_general | solution.py:45
  524.0 12.8 %collective-permute-done.11 = bf16[256,2048]{1,0:T(8,128)(2,1)} collective-permute-done((bf16[256,2048]{1,0:T(8,128)(2,1)S(1)}, bf16[256,2048]{1,0:T(8,128)(2,1)}, u32[]{:S(2)}, u32[]{:S(2)}) %collective-permute-start.11) | collective-permute-done | bytes 1048608 | tf_op jit(solution)/shard_map/ppermute | solution.py:56
  561.7 10.8 %collective-permute-done.3 = bf16[256,2048]{1,0:T(8,128)(2,1)S(1)} collective-permute-done((bf16[256,2048]{1,0:T(8,128)(2,1)S(1)}, bf16[256,2048]{1,0:T(8,128)(2,1)S(1)}, u32[]{:S(2)}, u32[]{:S(2)}) %collective-permute-start.3) | collective-permute-done | bytes 1048608 | tf_op jit(solution)/shard_map/ppermute | solution.py:56
  575.7 19.3 %collective-permute-done.5 = bf16[256,2048]{1,0:T(8,128)(2,1)S(1)} collective-permute-done((bf16[256,2048]{1,0:T(8,128)(2,1)S(1)}, bf16[256,2048]{1,0:T(8,128)(2,1)S(1)}, u32[]{:S(2)}, u32[]{:S(2)}) %collective-permute-start.5) | collective-permute-done | bytes 1048608 | tf_op jit(solution)/shard_map/ppermute | solution.py:56
  595.7 11.3 %collective-permute-done.4 = bf16[256,2048]{1,0:T(8,128)(2,1)S(1)} collective-permute-done((bf16[256,2048]{1,0:T(8,128)(2,1)S(1)}, bf16[256,2048]{1,0:T(8,128)(2,1)S(1)}, u32[]{:S(2)}, u32[]{:S(2)}) %collective-permute-start.4) | collective-permute-done | bytes 1048608 | tf_op jit(solution)/shard_map/ppermute | solution.py:56
  615.1 11.0 %collective-permute-done.18 = f32[1,2560]{1,0:T(1,128)S(1)} collective-permute-done((f32[1,2560]{1,0:T(1,128)S(1)}, f32[1,2560]{1,0:T(1,128)S(1)}, u32[]{:S(2)}, u32[]{:S(2)}) %collective-permute-start.18) | collective-permute-done | bytes 10272 | tf_op jit(solution)/shard_map/ppermute | solution.py:96
  688.6 11.4 %collective-permute-done.46 = bf16[256,2048]{1,0:T(8,128)(2,1)S(1)} collective-permute-done((bf16[256,2048]{1,0:T(8,128)(2,1)S(1)}, bf16[256,2048]{1,0:T(8,128)(2,1)S(1)}, u32[]{:S(2)}, u32[]{:S(2)}) %collective-permute-start.46) | collective-permute-done | bytes 1048608 | tf_op jit(solution)/shard_map/ppermute | solution.py:96
  706.6 15.9 %collective-permute-done.57 = bf16[256,2048]{1,0:T(8,128)(2,1)S(1)} collective-permute-done((bf16[256,2048]{1,0:T(8,128)(2,1)S(1)}, bf16[256,2048]{1,0:T(8,128)(2,1)S(1)}, u32[]{:S(2)}, u32[]{:S(2)}) %collective-permute-start.57) | collective-permute-done | bytes 1048608 | tf_op jit(solution)/shard_map/ppermute | solution.py:96
  730.8 14.1 %collective-permute-done.47 = bf16[256,2048]{1,0:T(8,128)(2,1)S(1)} collective-permute-done((bf16[256,2048]{1,0:T(8,128)(2,1)S(1)}, bf16[256,2048]{1,0:T(8,128)(2,1)S(1)}, u32[]{:S(2)}, u32[]{:S(2)}) %collective-permute-start.47) | collective-permute-done | bytes 1048608 | tf_op jit(solution)/shard_map/ppermute | solution.py:96
  755.5 11.9 %collective-permute-done.58 = bf16[256,2048]{1,0:T(8,128)(2,1)S(1)} collective-permute-done((bf16[256,2048]{1,0:T(8,128)(2,1)S(1)}, bf16[256,2048]{1,0:T(8,128)(2,1)S(1)}, u32[]{:S(2)}, u32[]{:S(2)}) %collective-permute-start.58) | collective-permute-done | bytes 1048608 | tf_op jit(solution)/shard_map/ppermute | solution.py:96
  796.5 12.0 %collective-permute-done.60 = bf16[256,2048]{1,0:T(8,128)(2,1)S(1)} collective-permute-done((bf16[256,2048]{1,0:T(8,128)(2,1)S(1)}, bf16[256,2048]{1,0:T(8,128)(2,1)S(1)}, u32[]{:S(2)}, u32[]{:S(2)}) %collective-permute-start.60) | collective-permute-done | bytes 1048608 | tf_op jit(solution)/shard_map/ppermute | solution.py:56
  818.0 21.7 %collective-permute-done.49 = bf16[256,2048]{1,0:T(8,128)(2,1)S(1)} collective-permute-done((bf16[256,2048]{1,0:T(8,128)(2,1)S(1)}, bf16[256,2048]{1,0:T(8,128)(2,1)S(1)}, u32[]{:S(2)}, u32[]{:S(2)}) %collective-permute-start.49) | collective-permute-done | bytes 1048608 | tf_op jit(solution)/shard_map/ppermute | solution.py:56
  839.8 14.6 %collective-permute-done.50 = bf16[256,2048]{1,0:T(8,128)(2,1)S(1)} collective-permute-done((bf16[256,2048]{1,0:T(8,128)(2,1)S(1)}, bf16[256,2048]{1,0:T(8,128)(2,1)S(1)}, u32[]{:S(2)}, u32[]{:S(2)}) %collective-permute-start.50) | collective-permute-done | bytes 1048608 | tf_op jit(solution)/shard_map/ppermute | solution.py:56
  864.8 12.1 %copy.147 = f32[4,256,8,256]{3,0,2,1:T(4,128)} copy(f32[4,256,8,256]{3,2,1,0:T(8,128)} %bitcast.412) | data formatting | bytes 16777216 | tf_op jit(solution)/shard_map/convert_element_type | solution.py:340
  877.0 10.8 %reshape.557 = f32[256,8192]{1,0:T(8,128)} reshape(f32[256,8,4,256]{3,2,1,0:T(4,128)} %bitcast.413) | data formatting | bytes 16777216 | tf_op jit(solution)/shard_map/convert_element_type | solution.py:340
  (461 shorter events, 457.2 us)
Async XLA Ops:
  7.2 113.9 %all-gather.13.cloned.1.call-start = ((), (), s32[]{:S(2)}) async-start(), calls=%async_computation.2 | async-start | bytes 2359296 | tf_op jit(solution)/shard_map/all_gather | solution.py:104
  9.2 118.3 %all-gather.9.cloned.1.call-start = ((), (), s32[]{:S(2)}) async-start(), calls=%async_computation | async-start | bytes 7077888 | tf_op jit(solution)/shard_map/all_gather | solution.py:104
  16.1 393.5 %all-gather.11.cloned.1.call-start = ((), (), s32[]{:S(2)}) async-start(), calls=%async_computation.1 | async-start | bytes 9437184 | tf_op jit(solution)/shard_map/all_gather | solution.py:104
  25.1 415.3 %all-gather.15.cloned.1.call-start = ((), (), s32[]{:S(2)}) async-start(), calls=%async_computation.3 | async-start | bytes 9437184 | tf_op jit(solution)/shard_map/all_gather | solution.py:104
  25.2 38.5 %collective-permute-start.1 = (bf16[256,2048]{1,0:T(8,128)(2,1)S(1)}, bf16[256,2048]{1,0:T(8,128)(2,1)}, u32[]{:S(2)}, u32[]{:S(2)}) collective-permute-start(bf16[256,2048]{1,0:T(8,128)(2,1)S(1)} %bitcast.436), channel_id=1, source_target_pairs={{0,16},{8,24},{16,0},{24,8},{1,17},{9,25},{17,1},{25,9},{2,18},{10... | collective-permute-start | bytes 3145736 | tf_op jit(solution)/shard_map/ppermute | solution.py:56
  29.6 46.7 %collective-permute-start.2 = (bf16[256,2048]{1,0:T(8,128)(2,1)S(1)}, bf16[256,2048]{1,0:T(8,128)(2,1)}, u32[]{:S(2)}, u32[]{:S(2)}) collective-permute-start(bf16[256,2048]{1,0:T(8,128)(2,1)S(1)} %bitcast.438), channel_id=1, source_target_pairs={{0,24},{8,16},{16,8},{24,0},{1,25},{9,17},{17,9},{25,1},{2,26},{10... | collective-permute-start | bytes 3145736 | tf_op jit(solution)/shard_map/ppermute | solution.py:56
  29.7 77.1 %collective-permute-start.7 = (bf16[256,2048]{1,0:T(8,128)(2,1)S(1)}, bf16[256,2048]{1,0:T(8,128)(2,1)S(1)}, u32[]{:S(2)}, u32[]{:S(2)}) collective-permute-start(bf16[256,2048]{1,0:T(8,128)(2,1)S(1)} %bitcast.445), channel_id=1, source_target_pairs={{0,16},{8,24},{16,0},{24,8},{1,17},{9,25},{17,1},{25,9},{2,18},{10... | collective-permute-start | bytes 3145736 | tf_op jit(solution)/shard_map/ppermute | solution.py:56
  31.6 67.7 %collective-permute-start.6 = (bf16[256,2048]{1,0:T(8,128)(2,1)S(1)}, bf16[256,2048]{1,0:T(8,128)(2,1)}, u32[]{:S(2)}, u32[]{:S(2)}) collective-permute-start(bf16[256,2048]{1,0:T(8,128)(2,1)S(1)} %bitcast.446), channel_id=1, source_target_pairs={{0,8},{8,0},{16,24},{24,16},{1,9},{9,1},{17,25},{25,17},{2,10},{10... | collective-permute-start | bytes 3145736 | tf_op jit(solution)/shard_map/ppermute | solution.py:56
  60.7 59.3 %collective-permute-start.8 = (bf16[256,2048]{1,0:T(8,128)(2,1)S(1)}, bf16[256,2048]{1,0:T(8,128)(2,1)S(1)}, u32[]{:S(2)}, u32[]{:S(2)}) collective-permute-start(bf16[256,2048]{1,0:T(8,128)(2,1)S(1)} %bitcast.447), channel_id=1, source_target_pairs={{0,24},{8,16},{16,8},{24,0},{1,25},{9,17},{17,9},{25,1},{2,26},{10... | collective-permute-start | bytes 3145736 | tf_op jit(solution)/shard_map/ppermute | solution.py:56
  193.3 138.9 %collective-permute-start.32 = (bf16[4,64,2048]{2,1,0:T(8,128)(2,1)}, bf16[4,64,2048]{2,1,0:T(8,128)(2,1)}, u32[]{:S(2)}, u32[]{:S(2)}) collective-permute-start(bf16[4,64,2048]{2,1,0:T(8,128)(2,1)} %dynamic-slice_bitcast_fusion.7), channel_id=1, source_target_pairs={{0,1},{1,0},{2,3},{3,2},{4,5},{5,4},{6,7},{7,6},{8,9},{9,8},{10,11... | collective-permute-start | bytes 3145736 | tf_op jit(solution)/shard_map/ppermute | solution.py:84
  359.9 37.4 %collective-permute-start.22 = (bf16[4,256,1536]{1,2,0:T(8,128)(2,1)}, bf16[4,256,1536]{1,2,0:T(8,128)(2,1)}, u32[]{:S(2)}, u32[]{:S(2)}) collective-permute-start(bf16[4,256,1536]{1,2,0:T(8,128)(2,1)} %bitcast.448), channel_id=1, source_target_pairs={{0,1},{1,0},{2,3},{3,2},{4,5},{5,4},{6,7},{7,6},{8,9},{9,8},{10,11... | collective-permute-start | bytes 9437192 | tf_op jit(solution)/shard_map/ppermute | solution.py:84
  403.0 149.7 %collective-permute-start.23 = (bf16[256,1536]{0,1:T(8,128)(2,1)}, bf16[256,1536]{0,1:T(8,128)(2,1)}, u32[]{:S(2)}, u32[]{:S(2)}) collective-permute-start(bf16[256,1536]{0,1:T(8,128)(2,1)} %get-tuple-element.385), channel_id=1, source_target_pairs={{6,4},{7,5},{14,12},{15,13},{22,20},{23,21},{30,28},{31,29}} | collective-permute-start | bytes 2359304 | tf_op jit(solution)/shard_map/ppermute | solution.py:95
  404.6 154.4 %collective-permute-start.26 = (bf16[256,1536]{0,1:T(8,128)(2,1)}, bf16[256,1536]{0,1:T(8,128)(2,1)}, u32[]{:S(2)}, u32[]{:S(2)}) collective-permute-start(bf16[256,1536]{0,1:T(8,128)(2,1)} %get-tuple-element.386), channel_id=1, source_target_pairs={{0,2},{1,3},{8,10},{9,11},{16,18},{17,19},{24,26},{25,27}} | collective-permute-start | bytes 2359304 | tf_op jit(solution)/shard_map/ppermute | solution.py:96
  490.1 46.7 %collective-permute-start.11 = (bf16[256,2048]{1,0:T(8,128)(2,1)S(1)}, bf16[256,2048]{1,0:T(8,128)(2,1)}, u32[]{:S(2)}, u32[]{:S(2)}) collective-permute-start(bf16[256,2048]{1,0:T(8,128)(2,1)S(1)} %get-tuple-element.376), channel_id=1, source_target_pairs={{0,24},{8,16},{16,8},{24,0},{1,25},{9,17},{17,9},{25,1},{2,26},{10... | collective-permute-start | bytes 3145736 | tf_op jit(solution)/shard_map/ppermute | solution.py:56
  492.6 45.6 %collective-permute-start.10 = (bf16[256,2048]{1,0:T(8,128)(2,1)S(1)}, bf16[256,2048]{1,0:T(8,128)(2,1)}, u32[]{:S(2)}, u32[]{:S(2)}) collective-permute-start(bf16[256,2048]{1,0:T(8,128)(2,1)S(1)} %get-tuple-element.377), channel_id=1, source_target_pairs={{0,16},{8,24},{16,0},{24,8},{1,17},{9,25},{17,1},{25,9},{2,18},{10... | collective-permute-start | bytes 3145736 | tf_op jit(solution)/shard_map/ppermute | solution.py:56
  552.0 89.9 %collective-permute-start.52 = (bf16[4,256,2048]{2,1,0:T(8,128)(2,1)}, bf16[4,256,2048]{2,1,0:T(8,128)(2,1)}, u32[]{:S(2)}, u32[]{:S(2)}) collective-permute-start(bf16[4,256,2048]{2,1,0:T(8,128)(2,1)} %dynamic-slice_bitcast_fusion.1), channel_id=1, source_target_pairs={{0,1},{1,0},{2,3},{3,2},{4,5},{5,4},{6,7},{7,6},{8,9},{9,8},{10,11... | collective-permute-start | bytes 12582920 | tf_op jit(solution)/shard_map/ppermute | solution.py:84
  559.0 35.9 %collective-permute-start.5 = (bf16[256,2048]{1,0:T(8,128)(2,1)S(1)}, bf16[256,2048]{1,0:T(8,128)(2,1)S(1)}, u32[]{:S(2)}, u32[]{:S(2)}) collective-permute-start(bf16[256,2048]{1,0:T(8,128)(2,1)S(1)} %get-tuple-element.379), channel_id=1, source_target_pairs={{0,24},{8,16},{16,8},{24,0},{1,25},{9,17},{17,9},{25,1},{2,26},{10... | collective-permute-start | bytes 3145736 | tf_op jit(solution)/shard_map/ppermute | solution.py:56
  560.5 46.5 %collective-permute-start.4 = (bf16[256,2048]{1,0:T(8,128)(2,1)S(1)}, bf16[256,2048]{1,0:T(8,128)(2,1)S(1)}, u32[]{:S(2)}, u32[]{:S(2)}) collective-permute-start(bf16[256,2048]{1,0:T(8,128)(2,1)S(1)} %get-tuple-element.380), channel_id=1, source_target_pairs={{0,16},{8,24},{16,0},{24,8},{1,17},{9,25},{17,1},{25,9},{2,18},{10... | collective-permute-start | bytes 3145736 | tf_op jit(solution)/shard_map/ppermute | solution.py:56
  561.7 98.7 %collective-permute-start.42 = (bf16[4,256,2048]{2,1,0:T(8,128)(2,1)}, bf16[4,256,2048]{2,1,0:T(8,128)(2,1)}, u32[]{:S(2)}, u32[]{:S(2)}) collective-permute-start(bf16[4,256,2048]{2,1,0:T(8,128)(2,1)} %dynamic-slice_bitcast_fusion.2), channel_id=1, source_target_pairs={{0,1},{1,0},{2,3},{3,2},{4,5},{5,4},{6,7},{7,6},{8,9},{9,8},{10,11... | collective-permute-start | bytes 12582920 | tf_op jit(solution)/shard_map/ppermute | solution.py:84
  572.6 38.7 %collective-permute-start.15 = (f32[1,2560]{1,0:T(1,128)S(1)}, f32[1,2560]{1,0:T(1,128)S(1)}, u32[]{:S(2)}, u32[]{:S(2)}) collective-permute-start(f32[1,2560]{1,0:T(1,128)S(1)} %get-tuple-element.410), channel_id=1, source_target_pairs={{2,0},{3,1},{4,2},{5,3},{6,4},{7,5},{10,8},{11,9},{12,10},{13,11},... | collective-permute-start | bytes 30728 | tf_op jit(solution)/shard_map/ppermute | solution.py:95
  658.2 66.4 %collective-permute-start.30 = (bf16[256,1536]{0,1:T(8,128)(2,1)}, bf16[256,1536]{0,1:T(8,128)(2,1)}, u32[]{:S(2)}, u32[]{:S(2)}) collective-permute-start(bf16[256,1536]{0,1:T(8,128)(2,1)} %get-tuple-element.348), channel_id=1, source_target_pairs={{0,16},{8,24},{16,0},{24,8},{1,17},{9,25},{17,1},{25,9},{2,18},{10... | collective-permute-start | bytes 2359304 | tf_op jit(solution)/shard_map/ppermute | solution.py:56
  680.6 41.9 %collective-permute-start.57 = (bf16[256,2048]{1,0:T(8,128)(2,1)S(1)}, bf16[256,2048]{1,0:T(8,128)(2,1)S(1)}, u32[]{:S(2)}, u32[]{:S(2)}) collective-permute-start(bf16[256,2048]{1,0:T(8,128)(2,1)S(1)} %get-tuple-element.366), channel_id=1, source_target_pairs={{0,2},{1,3},{2,4},{3,5},{8,10},{9,11},{10,12},{11,13},{16,18},{17,... | collective-permute-start | bytes 3145736 | tf_op jit(solution)/shard_map/ppermute | solution.py:96
  686.9 82.7 %collective-permute-start.31 = (bf16[256,1536]{0,1:T(8,128)(2,1)}, bf16[256,1536]{0,1:T(8,128)(2,1)S(1)}, u32[]{:S(2)}, u32[]{:S(2)}) collective-permute-start(bf16[256,1536]{0,1:T(8,128)(2,1)} %get-tuple-element.348), channel_id=1, source_target_pairs={{0,24},{8,16},{16,8},{24,0},{1,25},{9,17},{17,9},{25,1},{2,26},{10... | collective-permute-start | bytes 2359304 | tf_op jit(solution)/shard_map/ppermute | solution.py:56
  701.6 43.4 %collective-permute-start.47 = (bf16[256,2048]{1,0:T(8,128)(2,1)S(1)}, bf16[256,2048]{1,0:T(8,128)(2,1)S(1)}, u32[]{:S(2)}, u32[]{:S(2)}) collective-permute-start(bf16[256,2048]{1,0:T(8,128)(2,1)S(1)} %get-tuple-element.372), channel_id=1, source_target_pairs={{0,2},{1,3},{2,4},{3,5},{8,10},{9,11},{10,12},{11,13},{16,18},{17,... | collective-permute-start | bytes 3145736 | tf_op jit(solution)/shard_map/ppermute | solution.py:96
  724.5 42.9 %collective-permute-start.58 = (bf16[256,2048]{1,0:T(8,128)(2,1)S(1)}, bf16[256,2048]{1,0:T(8,128)(2,1)S(1)}, u32[]{:S(2)}, u32[]{:S(2)}) collective-permute-start(bf16[256,2048]{1,0:T(8,128)(2,1)S(1)} %get-tuple-element.364), channel_id=1, source_target_pairs={{0,2},{1,3},{2,4},{3,5},{4,6},{5,7},{8,10},{9,11},{10,12},{11,13},... | collective-permute-start | bytes 3145736 | tf_op jit(solution)/shard_map/ppermute | solution.py:96
  747.1 36.3 %collective-permute-start.45 = (bf16[256,2048]{1,0:T(8,128)(2,1)}, bf16[256,2048]{1,0:T(8,128)(2,1)}, u32[]{:S(2)}, u32[]{:S(2)}) collective-permute-start(bf16[256,2048]{1,0:T(8,128)(2,1)} %get-tuple-element.369), channel_id=1, source_target_pairs={{2,0},{3,1},{4,2},{5,3},{6,4},{7,5},{10,8},{11,9},{12,10},{13,11},... | collective-permute-start | bytes 3145736 | tf_op jit(solution)/shard_map/ppermute | solution.py:95
  748.3 37.8 %collective-permute-start.48 = (bf16[256,2048]{1,0:T(8,128)(2,1)}, bf16[256,2048]{1,0:T(8,128)(2,1)}, u32[]{:S(2)}, u32[]{:S(2)}) collective-permute-start(bf16[256,2048]{1,0:T(8,128)(2,1)} %get-tuple-element.370), channel_id=1, source_target_pairs={{0,2},{1,3},{2,4},{3,5},{4,6},{5,7},{8,10},{9,11},{10,12},{11,13},... | collective-permute-start | bytes 3145736 | tf_op jit(solution)/shard_map/ppermute | solution.py:96
  769.7 38.8 %collective-permute-start.60 = (bf16[256,2048]{1,0:T(8,128)(2,1)S(1)}, bf16[256,2048]{1,0:T(8,128)(2,1)S(1)}, u32[]{:S(2)}, u32[]{:S(2)}) collective-permute-start(bf16[256,2048]{1,0:T(8,128)(2,1)S(1)} %get-tuple-element.342), channel_id=1, source_target_pairs={{0,16},{8,24},{16,0},{24,8},{1,17},{9,25},{17,1},{25,9},{2,18},{10... | collective-permute-start | bytes 3145736 | tf_op jit(solution)/shard_map/ppermute | solution.py:56
  782.1 35.8 %collective-permute-start.61 = (bf16[256,2048]{1,0:T(8,128)(2,1)S(1)}, bf16[256,2048]{1,0:T(8,128)(2,1)S(1)}, u32[]{:S(2)}, u32[]{:S(2)}) collective-permute-start(bf16[256,2048]{1,0:T(8,128)(2,1)S(1)} %get-tuple-element.342), channel_id=1, source_target_pairs={{0,24},{8,16},{16,8},{24,0},{1,25},{9,17},{17,9},{25,1},{2,26},{10... | collective-permute-start | bytes 3145736 | tf_op jit(solution)/shard_map/ppermute | solution.py:56
  789.1 65.2 %collective-permute-start.50 = (bf16[256,2048]{1,0:T(8,128)(2,1)S(1)}, bf16[256,2048]{1,0:T(8,128)(2,1)S(1)}, u32[]{:S(2)}, u32[]{:S(2)}) collective-permute-start(bf16[256,2048]{1,0:T(8,128)(2,1)S(1)} %get-tuple-element.344), channel_id=1, source_target_pairs={{0,16},{8,24},{16,0},{24,8},{1,17},{9,25},{17,1},{25,9},{2,18},{10... | collective-permute-start | bytes 3145736 | tf_op jit(solution)/shard_map/ppermute | solution.py:56
  790.4 49.3 %collective-permute-start.49 = (bf16[256,2048]{1,0:T(8,128)(2,1)S(1)}, bf16[256,2048]{1,0:T(8,128)(2,1)S(1)}, u32[]{:S(2)}, u32[]{:S(2)}) collective-permute-start(bf16[256,2048]{1,0:T(8,128)(2,1)S(1)} %get-tuple-element.344), channel_id=1, source_target_pairs={{0,8},{8,0},{16,24},{24,16},{1,9},{9,1},{17,25},{25,17},{2,10},{10... | collective-permute-start | bytes 3145736 | tf_op jit(solution)/shard_map/ppermute | solution.py:56
  794.7 64.5 %collective-permute-start.51 = (bf16[256,2048]{1,0:T(8,128)(2,1)S(1)}, bf16[256,2048]{1,0:T(8,128)(2,1)S(1)}, u32[]{:S(2)}, u32[]{:S(2)}) collective-permute-start(bf16[256,2048]{1,0:T(8,128)(2,1)S(1)} %get-tuple-element.344), channel_id=1, source_target_pairs={{0,24},{8,16},{16,8},{24,0},{1,25},{9,17},{17,9},{25,1},{2,26},{10... | collective-permute-start | bytes 3145736 | tf_op jit(solution)/shard_map/ppermute | solution.py:56
  (102 other events, 1950.2 us)
Sparse Core Ops, SparseCore 0:
  10.2 31.7 all-gather.12
  44.2 66.5 all-gather.8
  112.3 79.0 all-gather.10
  192.9 80.2 all-gather.14

commit v2 on v1

v2 whole, which is shorter than its diff:
```python
import functools

import jax
import jax.numpy as jnp
from jax import lax
from jax.experimental import pallas as pl
from jax.experimental.pallas import tpu as pltpu
from jax.sharding import PartitionSpec as P

HEADS = 32
HEAD_DIM = 64
ROT = 32
EPS = 1e-05
BF = jnp.bfloat16
F32 = jnp.float32
VMEM_BYTES = 56 * 1024 * 1024


def mm(left, right, left_dim=1, right_dim=0):
    return lax.dot_general(
        left, right, (((left_dim,), (right_dim,)), ((), ())), preferred_element_type=F32
    )


def pick(array, index, axis=0):
    return lax.dynamic_index_in_dim(array, index, axis, keepdims=False)


def put(array, piece, index, axis=0):
    return lax.dynamic_update_index_in_dim(array, piece, index, axis)


def behind(array, other):
    first = lax.slice(other, (0,) * other.ndim, (1,) * other.ndim).reshape(())
    return jnp.where(jnp.isnan(first), jnp.zeros((), array.dtype), array)


def unread(arrays):
    return [pl.BlockSpec(memory_space=pl.ANY) for unused in arrays]


def params():
    return pltpu.CompilerParams(vmem_limit_bytes=VMEM_BYTES)


def cost(flops, size, transcendentals=0):
    return pl.CostEstimate(flops=flops, bytes_accessed=size, transcendentals=transcendentals)


def seq_exchange(blocks):
    return lax.all_to_all(blocks, "seq", split_axis=0, concat_axis=0)


def seq_gather(block):
    count = lax.axis_size("seq")
    return seq_exchange(jnp.broadcast_to(block[None], (count,) + block.shape))


def seq_gather_two(first, second):
    me, count = lax.axis_index("seq"), lax.axis_size("seq")
    bits = list(range(count.bit_length() - 1))
    orders = (bits, bits[::-1])
    wholes = [first[None], second[None]]
    for step in bits:
        got = []
        for whole, order in zip(wholes, orders):
            pairs = [(i, i ^ (1 << order[step])) for i in range(count)]
            got.append(lax.ppermute(whole, "seq", pairs))
        for i, order in enumerate(orders):
            low = (me >> order[step]) % 2 == 0
            whole, new = wholes[i], behind(got[i], got[1 - i])
            whole = jnp.where(low, jnp.stack([whole, new]), jnp.stack([new, whole]))
            wholes[i] = whole.reshape((-1,) + first.shape)
    sizes = (2,) * len(bits) + second.shape
    order = bits[::-1] + [len(bits) + i for i in range(second.ndim)]
    return wholes[0], wholes[1].reshape(sizes).transpose(order).reshape(wholes[1].shape)


def seq_all(block):
    return lax.all_gather(block, "seq", axis=0)


def seq_sum(blocks):
    return jnp.sum(seq_exchange(blocks).astype(F32), axis=0)


def fsdp_place():
    me = lax.axis_index("fsdp")
    return lax.axis_size("fsdp") // 2, me // 2, me % 2


def to_chips(array, moves):
    pairs = [(2 * a + core, 2 * b + core) for a, b in moves for core in (0, 1)]
    return lax.ppermute(array, "fsdp", pairs)


def to_other_core(array):
    count = lax.axis_size("fsdp")
    return lax.ppermute(array, "fsdp", [(i, i ^ 1) for i in range(count)])


def fsdp_gather(block):
    return lax.all_gather(block, "fsdp", axis=0, tiled=True)


class LineSum:
    def __init__(self, other, own_of):
        chips, chip, core = fsdp_place()
        own = own_of(to_other_core(other))
        first = jnp.where(chip == 0, own[chips - 1], own[1])
        got = to_chips(first, [(chips - 1, chips - 2), (0, 1)])
        self.first = first
        self.steps = [own, got]
        total = own[0].astype(F32) + got.astype(F32)
        down, up = got, got
        for step in range(2, chips):
            down = (down.astype(F32) + own[step].astype(F32)).astype(own.dtype)
            up = (up.astype(F32) + own[chips - step].astype(F32)).astype(own.dtype)
            down = to_chips(down, [(a, a - 1) for a in range(chips - step, chips)])
            up = to_chips(up, [(a, a + 1) for a in range(0, step)])
            self.steps += [down, up]
        if chips > 2:
            total = own[0].astype(F32) + down.astype(F32) + up.astype(F32)
        self.total = total


def attention_kernel(rows, half, qkv_ref, grad_ref, cos_ref, sin_ref, open_ref, *refs):
    mixed_ref, out_ref, key_ref, value_ref = refs[-4:]
    length = qkv_ref.shape[0]
    wide = 2 * half
    lane = lax.broadcasted_iota(jnp.int32, (length, wide), 1)
    turned = ROT // 2
    leading = (lane % half) < turned
    cosine, sine = cos_ref[...], sin_ref[...]
    scale = half ** (-0.5)

    def turn(x, s):
        other = jnp.where(leading, pltpu.roll(x, wide - turned, 1), pltpu.roll(x, turned, 1))
        return x * cosine + other * s

    query = turn(qkv_ref[:, :wide], sine).astype(BF)
    key = turn(qkv_ref[:, wide : 2 * wide], sine).astype(BF)
    value = qkv_ref[:, 2 * wide :].astype(BF)
    query = (query.astype(F32) * scale).astype(BF)
    grad = grad_ref[...]
    key_t = key.astype(F32).T.astype(BF)
    value_t = value.astype(F32).T.astype(BF)
    key_ref[...] = jnp.zeros_like(key_ref)
    value_ref[...] = jnp.zeros_like(value_ref)
    zero = jnp.zeros((), BF)
    for begin in range(0, length, rows):
        end = begin + rows
        cut = slice(begin, end)
        k_pos = lax.broadcasted_iota(jnp.int32, (end, rows), 0)
        q_pos = lax.broadcasted_iota(jnp.int32, (end, rows), 1) + begin
        allowed = (k_pos <= q_pos) & (k_pos >= open_ref[:, cut])
        side = lane[:rows] < half
        mixed_t, query_t = [], []
        for head in range(2):
            here = side if head == 0 else ~side
            q_rows = jnp.where(here, query[cut], zero)
            g_rows = jnp.where(here, grad[cut], zero)
            scores = jnp.where(allowed, mm(key[:end], q_rows, 1, 1), -1000000000.0)
            expo = jnp.exp(scores - jnp.max(scores, axis=0, keepdims=True))
            probs = expo * (1.0 / jnp.sum(expo, axis=0, keepdims=True))
            low = probs.astype(BF)
            own = slice(head * half, (head + 1) * half)
            mixed_t.append(mm(value_t[own, :end], low))
            grad_probs = mm(value[:end], g_rows, 1, 1)
            dots = jnp.sum(probs * grad_probs, axis=0, keepdims=True)
            grad_scores = (probs * (grad_probs - dots)).astype(BF)
            query_t.append(mm(key_t[own, :end], grad_scores))
            key_ref[:end] += mm(grad_scores, q_rows)
            value_ref[:end] += mm(low, g_rows)
        mixed_ref[cut] = jnp.concatenate(mixed_t, axis=0).T.astype(BF)
        q_grad = jnp.concatenate(query_t, axis=0).T * scale
        lead = leading[:rows]
        other = jnp.where(
            lead, pltpu.roll(q_grad, wide - turned, 1), pltpu.roll(q_grad, turned, 1)
        )
        out_ref[cut, :wide] = (q_grad * cosine[cut] - other * sine[cut]).astype(BF)
    out_ref[:, wide : 2 * wide] = turn(key_ref[...], -sine).astype(BF)
    out_ref[:, 2 * wide :] = value_ref[...].astype(BF)


def attention(qkv, grad, cosine, sine, opening, begin, steps, before=(), after=()):
    length = qkv.shape[0]
    wide = 2 * HEAD_DIM
    pairs = grad.shape[1] // wide

    def whole(array):
        return pl.BlockSpec(array.shape, lambda p: (0, 0))

    narrow = pl.BlockSpec((length, wide), lambda p: (0, begin + p))
    three = pl.BlockSpec((length, 3 * wide), lambda p: (0, begin + p))
    return pl.pallas_call(
        functools.partial(attention_kernel, min(256, length), HEAD_DIM),
        grid=(steps,),
        in_specs=[three, narrow, whole(cosine), whole(sine), whole(opening)]
        + unread(before)
        + unread(after),
        out_specs=[narrow, three],
        out_shape=[
            jax.ShapeDtypeStruct((length, pairs * wide), BF),
            jax.ShapeDtypeStruct((length, pairs * 3 * wide), BF),
        ],
        input_output_aliases={5 + i: i for i in range(len(before))},
        scratch_shapes=[pltpu.VMEM((length, wide), F32), pltpu.VMEM((length, wide), F32)],
        compiler_params=params(),
        cost_estimate=cost(
            24 * length * length * wide * steps,
            24 * length * wide * steps,
            length * length * steps,
        ),
    )(qkv, grad, cosine, sine, opening, *before, *after)


def norm_kernel(in_ref, gain_ref, shift_ref, out_ref, mean_ref, std_ref):
    value = in_ref[...].astype(F32)
    mean = jnp.mean(value, axis=-1, keepdims=True)
    centred = value - mean
    std = lax.rsqrt(jnp.mean(centred * centred, axis=-1, keepdims=True) + EPS)
    out_ref[...] = (centred * std * gain_ref[...] + shift_ref[...]).astype(BF)
    mean_ref[...] = mean
    std_ref[...] = std


def layer_norm(rows_in, gain, shift):
    rows, columns = rows_in.shape
    cut = min(256, rows)
    block = pl.BlockSpec((cut, columns), lambda i: (i, 0))
    vector = pl.BlockSpec((1, columns), lambda i: (0, 0))
    narrow = pl.BlockSpec((cut, 1), lambda i: (i, 0))
    return pl.pallas_call(
        norm_kernel,
        grid=(rows // cut,),
        in_specs=[block, vector, vector],
        out_specs=[block, narrow, narrow],
        out_shape=[
            jax.ShapeDtypeStruct((rows, columns), BF),
            jax.ShapeDtypeStruct((rows, 1), F32),
            jax.ShapeDtypeStruct((rows, 1), F32),
        ],
        compiler_params=params(),
        cost_estimate=cost(10 * rows * columns, 4 * rows * columns),
    )(rows_in, gain[None], shift[None])


def mixed_kernel(cut, high, left_ref, both_ref, *refs):
    weight_ref, out_ref = refs[-2:]
    wide = both_ref.shape[1]
    for i in range(both_ref.shape[0] // high):
        rows = slice(i // cut * high, (i // cut + 1) * high)
        columns = slice(i % cut * wide, (i % cut + 1) * wide)
        weight_ref[rows, columns] = both_ref[i * high : (i + 1) * high, :]
    out_ref[...] = mm(left_ref[...], weight_ref[...], 1, 1).astype(BF)


def mixed_gradient(left, both, begin, cut, high, after=()):
    rows, depth = left.shape
    wide = depth // cut
    weight = (both.shape[0] // cut, depth)

    def whole(shape):
        return pl.BlockSpec(shape, lambda i: (0, 0))

    return pl.pallas_call(
        functools.partial(mixed_kernel, cut, high),
        grid=(1,),
        in_specs=[
            whole(left.shape),
            pl.BlockSpec((both.shape[0], wide), lambda i: (0, begin // wide)),
        ]
        + unread(after),
        out_specs=[whole(weight), whole((rows, weight[0]))],
        out_shape=[
            jax.ShapeDtypeStruct(weight, BF),
            jax.ShapeDtypeStruct((rows, weight[0]), BF),
        ],
        compiler_params=params(),
        cost_estimate=cost(2 * rows * depth * weight[0], 4 * rows * depth),
    )(left, both, *after)


def hidden_kernel(left_ref, right_ref, bias_ref, active_ref, slope_ref):
    value = mm(left_ref[...], right_ref[...]) + bias_ref[...]
    square = value * value
    scaled = 0.7978845608028654 * value
    bend = 0.044715 * square
    tanh = jnp.tanh(scaled * (1.0 + bend))
    half = 0.5 * (1.0 + tanh)
    active_ref[...] = (value * half).astype(BF)
    slope = half + 0.5 * (1.0 - tanh * tanh) * scaled * (1.0 + 3.0 * bend)
    slope_ref[...] = slope.astype(BF)


def hidden_layer(left, right, bias):
    rows, depth = left.shape
    columns = right.shape[1]
    cut = min(512, columns)
    block = pl.BlockSpec((rows, cut), lambda j: (0, j))
    return pl.pallas_call(
        hidden_kernel,
        grid=(columns // cut,),
        in_specs=[
            pl.BlockSpec((rows, depth), lambda j: (0, 0)),
            pl.BlockSpec((depth, cut), lambda j: (0, j)),
            pl.BlockSpec((1, cut), lambda j: (0, j)),
        ],
        out_specs=[block, block],
        out_shape=[jax.ShapeDtypeStruct((rows, columns), BF)] * 2,
        compiler_params=params(),
        cost_estimate=cost(2 * rows * depth * columns, 4 * rows * (depth + columns), rows * columns),
    )(left, right, bias[None])


def term_kernel(adds, index_ref, left_ref, right_ref, *refs):
    value = mm(left_ref[...], right_ref[...], 0, 0)
    if adds:
        value = value + refs[0][0].astype(F32)
    refs[-1][0] = value.astype(BF)


def block_terms(left, right, width, index, add=None, after=()):
    rows, columns = right.shape
    count = len(index)
    if width % 128:
        blocks = [lax.dynamic_slice_in_dim(left, i * width, width, 1) for i in index]
        value = jnp.stack([mm(block, right, 0, 0) for block in blocks])
        return (value if add is None else value + add.astype(F32)).astype(BF)
    index = jnp.stack([jnp.asarray(i, jnp.int32) for i in index])
    adds = [] if add is None else [add]
    out = pl.BlockSpec((1, width, columns), lambda r, index: (r, 0, 0))
    return pl.pallas_call(
        functools.partial(term_kernel, len(adds)),
        grid_spec=pltpu.PrefetchScalarGridSpec(
            num_scalar_prefetch=1,
            grid=(count,),
            in_specs=[
                pl.BlockSpec((rows, width), lambda r, index: (0, index[r])),
                pl.BlockSpec((rows, columns), lambda r, index: (0, 0)),
            ]
            + [out] * len(adds)
            + unread(after),
            out_specs=out,
        ),
        out_shape=jax.ShapeDtypeStruct((count, width, columns), BF),
        compiler_params=params(),
        cost_estimate=cost(2 * rows * width * count * columns, 4 * rows * columns),
    )(index, left, right, *adds, *after)


def two_terms_kernel(cut, adds, index_ref, left_ref, right_ref, beside_ref, *refs):
    out_ref = refs[-1]
    columns = right_ref.shape[1]
    value = mm(left_ref[...], right_ref[...], 0, 0)
    if adds:
        value = value + refs[0][0, :, :columns].astype(F32)
    out_ref[0, :, :columns] = value.astype(BF)
    high = beside_ref.shape[1]
    wide = beside_ref.shape[2] // cut
    for i in range(cut):
        part = slice(i * high, (i + 1) * high)
        value = beside_ref[0, :, i * wide : (i + 1) * wide]
        if adds:
            value = (value.astype(F32) + refs[0][0, part, columns:].astype(F32)).astype(BF)
        out_ref[0, part, columns:] = value


def two_terms(left, right, width, beside, cut, index, add=None, after=()):
    rows, columns = right.shape
    count = len(index)
    extra = beside.shape[2] // cut
    index = jnp.stack([jnp.asarray(i, jnp.int32) for i in index])
    adds = [] if add is None else [add]
    out = pl.BlockSpec((1, width, columns + extra), lambda r, index: (r, 0, 0))
    return pl.pallas_call(
        functools.partial(two_terms_kernel, cut, len(adds)),
        grid_spec=pltpu.PrefetchScalarGridSpec(
            num_scalar_prefetch=1,
            grid=(count,),
            in_specs=[
                pl.BlockSpec((rows, width), lambda r, index: (0, index[r])),
                pl.BlockSpec((rows, columns), lambda r, index: (0, 0)),
                pl.BlockSpec((1,) + beside.shape[1:], lambda r, index: (index[r], 0, 0)),
            ]
            + [out] * len(adds)
            + unread(after),
            out_specs=out,
        ),
        out_shape=jax.ShapeDtypeStruct((count, width, columns + extra), BF),
        compiler_params=params(),
        cost_estimate=cost(2 * rows * width * count * columns, 4 * rows * columns),
    )(index, left, right, beside, *adds, *after)


def product_kernel(left_ref, right_ref, bias_ref, *refs):
    refs[-1][...] = mm(left_ref[...], right_ref[...]) + bias_ref[...]


def product(left, right, bias, after=()):
    rows, depth = left.shape
    columns = bias.shape[0]
    cut = 512 if columns % 512 == 0 else 256
    return pl.pallas_call(
        product_kernel,
        grid=(columns // cut,),
        in_specs=[
            pl.BlockSpec((rows, depth), lambda j: (0, 0)),
            pl.BlockSpec((depth, cut), lambda j: (0, j)),
            pl.BlockSpec((1, cut), lambda j: (0, j)),
        ]
        + unread(after),
        out_specs=pl.BlockSpec((rows, cut), lambda j: (0, j)),
        out_shape=jax.ShapeDtypeStruct((rows, columns), F32),
        compiler_params=params(),
        cost_estimate=cost(2 * rows * depth * columns, 4 * rows * (depth + columns)),
    )(left, right, bias[None], *after)


def slope_kernel(left_ref, right_ref, slope_ref, *refs):
    value = mm(left_ref[...], right_ref[...], 1, 1) * slope_ref[...].astype(F32)
    refs[-1][...] = value.astype(BF)


def times_slope(left, right, slope, after=()):
    rows, depth = left.shape
    columns = right.shape[0]
    cut = min(512, columns)
    block = pl.BlockSpec((rows, cut), lambda j: (0, j))
    return pl.pallas_call(
        slope_kernel,
        grid=(columns // cut,),
        in_specs=[
            pl.BlockSpec((rows, depth), lambda j: (0, 0)),
            pl.BlockSpec((cut, depth), lambda j: (j, 0)),
            block,
        ]
        + unread(after),
        out_specs=block,
        out_shape=jax.ShapeDtypeStruct(slope.shape, BF),
        compiler_params=params(),
        cost_estimate=cost(2 * rows * depth * columns, 6 * rows * depth),
    )(left, right, slope, *after)


def output_kernel(left_ref, right_ref, second_ref, weight_ref, *refs):
    value = mm(left_ref[...], right_ref[...]) + mm(second_ref[...], weight_ref[...])
    refs[-1][...] = value.astype(BF)


def output_terms(left, right, second, weight, after=()):
    rows, depth = left.shape
    columns = right.shape[1]
    cut = min(512, columns)
    return pl.pallas_call(
        output_kernel,
        grid=(columns // cut,),
        in_specs=[
            pl.BlockSpec((rows, depth), lambda j: (0, 0)),
            pl.BlockSpec((depth, cut), lambda j: (0, j)),
            pl.BlockSpec(second.shape, lambda j: (0, 0)),
            pl.BlockSpec((second.shape[1], cut), lambda j: (0, j)),
        ]
        + unread(after),
        out_specs=pl.BlockSpec((rows, cut), lambda j: (0, j)),
        out_shape=jax.ShapeDtypeStruct((rows, columns), BF),
        compiler_params=params(),
        cost_estimate=cost(2 * rows * (depth + second.shape[1]) * columns, 6 * rows * depth),
    )(left, right, second, weight, *after)


def normed_kernel(one_ref, first_ref, two_ref, second_ref, in_ref, mean_ref, std_ref, *refs):
    out_ref, gain_ref, shift_ref = refs[-3:]
    value = mm(one_ref[...], first_ref[...], 1, 1) + mm(two_ref[...], second_ref[...], 1, 1)
    out_ref[...] = value.astype(BF)
    normal_hat = (in_ref[...].astype(F32) - mean_ref[...]) * std_ref[...]
    gain_ref[...] = jnp.sum(value * normal_hat, axis=0, keepdims=True)
    shift_ref[...] = jnp.sum(value, axis=0, keepdims=True)


def normed_terms(one, first, two, second, rows_in, mean, std, after=()):
    rows = one.shape[0]
    columns = first.shape[0]
    cut = min(512, columns)
    vector = pl.BlockSpec((1, cut), lambda j: (0, j))

    def whole(array):
        return pl.BlockSpec(array.shape, lambda j: (0, 0))

    return pl.pallas_call(
        normed_kernel,
        grid=(columns // cut,),
        in_specs=[
            whole(one),
            pl.BlockSpec((cut, one.shape[1]), lambda j: (j, 0)),
            whole(two),
            pl.BlockSpec((cut, second.shape[1]), lambda j: (j, 0)),
            pl.BlockSpec((rows, cut), lambda j: (0, j)),
            whole(mean),
            whole(std),
        ]
        + unread(after),
        out_specs=[pl.BlockSpec((rows, cut), lambda j: (0, j)), vector, vector],
        out_shape=[
            jax.ShapeDtypeStruct((rows, columns), BF),
            jax.ShapeDtypeStruct((1, columns), F32),
            jax.ShapeDtypeStruct((1, columns), F32),
        ],
        compiler_params=params(),
        cost_estimate=cost(2 * rows * columns * (one.shape[1] + two.shape[1]), 8 * rows * columns),
    )(one, first, two, second, rows_in, mean, std, *after)


def spread_kernel(width, in_ref, out_ref):
    for s in range(in_ref.shape[0]):
        out_ref[:, s * width : (s + 1) * width] = in_ref[s].astype(F32)


def spread_columns(pieces, width):
    count, rows, columns = pieces.shape
    return pl.pallas_call(
        functools.partial(spread_kernel, width),
        grid=(columns // width,),
        in_specs=[pl.BlockSpec((count, rows, width), lambda i: (0, 0, i))],
        out_specs=pl.BlockSpec((rows, width * count), lambda i: (0, i)),
        out_shape=jax.ShapeDtypeStruct((rows, columns * count), F32),
        compiler_params=params(),
        cost_estimate=cost(0, 6 * rows * columns * count),
    )(pieces)


def heads_kernel(half, in_ref, out_ref):
    parts = []
    for head in range(2):
        for s in range(in_ref.shape[0]):
            for part in range(3):
                start = (2 * part + head) * half
                parts.append(in_ref[s, :, start : start + half].astype(F32))
    for i in range(0, len(parts), 2):
        out_ref[:, i * half : (i + 2) * half] = jnp.concatenate(parts[i : i + 2], axis=1)


def spread_heads(pieces, pairs):
    count, rows, unused = pieces.shape
    width = 6 * HEAD_DIM
    return pl.pallas_call(
        functools.partial(heads_kernel, HEAD_DIM),
        grid=(pairs,),
        in_specs=[pl.BlockSpec((count, rows, width), lambda i: (0, 0, i))],
        out_specs=pl.BlockSpec((rows, width * count), lambda i: (0, i)),
        out_shape=jax.ShapeDtypeStruct((rows, pairs * width * count), F32),
        compiler_params=params(),
        cost_estimate=cost(0, 6 * rows * pairs * width * count),
    )(pieces)


def by_pairs(array, heads):
    lead = array.shape[:-1]
    array = array.reshape(lead + (heads // 2, 2, 3, HEAD_DIM))
    return jnp.swapaxes(array, -3, -2).reshape(lead + (heads * 3 * HEAD_DIM,))


def by_heads(array, heads):
    lead = array.shape[:-1]
    array = array.reshape(lead + (heads // 2, 3, 2, HEAD_DIM))
    return jnp.swapaxes(array, -3, -2).reshape(lead + (heads * 3 * HEAD_DIM,))


def per_device(
    inputs,
    doc_starts,
    ln_gain,
    ln_bias,
    w_qkv,
    b_qkv,
    w_out,
    b_out,
    w_fc1,
    b_fc1,
    w_fc2,
    b_fc2,
    cotangent,
):
    seqs, shards = lax.axis_size("seq"), lax.axis_size("fsdp")
    me = lax.axis_index("seq")
    chips, chip, core = fsdp_place()
    tok, width = inputs.shape[1:]
    length = tok * seqs
    rows_here = w_qkv.shape[0]
    heads = HEADS // seqs
    head_cols = heads * HEAD_DIM
    shard_heads = w_out.shape[0] // HEAD_DIM
    strided = shard_heads % seqs == 0
    each = shard_heads // seqs
    unit = w_fc2.shape[0] // seqs
    hidden_cols = unit * shards
    order = [2 * ((chip + r) % chips) + (core ^ h) for h in (0, 1) for r in range(chips)]

    fc1_here = jnp.concatenate(
        [
            lax.dynamic_slice_in_dim(w_fc1, (i * seqs + me) * unit, unit, 1)
            for i in range(shards)
        ],
        axis=1,
    )
    fc2_here = pick(w_fc2.reshape(seqs, unit, width), me)
    if strided:
        qkv_here = pick(w_qkv.reshape(rows_here, shards, seqs, each * 3 * HEAD_DIM), me, 2)
    else:
        qkv_here = pick(w_qkv.reshape(rows_here, seqs, heads * 3 * HEAD_DIM), me, 1)
    qkv_here = by_pairs(qkv_here.reshape(rows_here, 3 * head_cols), heads)
    out_cut = rows_here // (each * HEAD_DIM) if strided else 1
    if strided:
        out_here = pick(w_out.reshape(seqs, each * HEAD_DIM, width), me)
        out_here = out_here.reshape(each * HEAD_DIM, out_cut, width // out_cut)
        out_here = jnp.swapaxes(out_here, 0, 1).reshape(rows_here, width // out_cut)
        qkv_here = jnp.concatenate([qkv_here, out_here], axis=1)

    sizes = [v.shape[0] for v in (ln_gain, ln_bias, b_out, b_fc2, b_qkv, b_fc1)]
    small = jnp.concatenate([ln_gain, ln_bias, b_out, b_fc2, b_qkv, b_fc1])[None]
    small = lax.all_gather(small, "fsdp", axis=0, tiled=True).astype(F32)
    cuts = [sum(sizes[:i]) for i in range(len(sizes) + 1)]
    gain, shift, bias_out, bias_fc2, bias_qkv, bias_fc1 = [
        small[:, a:b].reshape(-1) for a, b in zip(cuts[:-1], cuts[1:])
    ]
    bias_fc1 = pick(bias_fc1.reshape(shards, seqs, unit), me, 1).reshape(hidden_cols)
    if strided:
        bias_qkv = pick(bias_qkv.reshape(shards, seqs, each * 3 * HEAD_DIM), me, 1)
    else:
        bias_qkv = pick(bias_qkv.reshape(seqs, heads * 3 * HEAD_DIM), me)
    bias_qkv = by_pairs(bias_qkv.reshape(3 * head_cols), heads)

    fc1 = fsdp_gather(fc1_here)
    rows_all, grad_rows = seq_gather_two(inputs[0], cotangent[0])
    rows_all, grad_rows = rows_all.reshape(length, width), grad_rows.reshape(length, width)

    starts_row = doc_starts[0]
    pos = jnp.arange(length, dtype=jnp.int32)
    before = starts_row[None, :] <= pos[:, None]
    opening = jnp.max(jnp.where(before, starts_row[None, :], 0), axis=1)
    rates = 10000.0 ** (-2.0 * jnp.arange(ROT // 2, dtype=F32) / ROT)
    angle = (pos - opening).astype(F32)[:, None] * rates[None, :]
    cosine, sine = jnp.cos(angle), jnp.sin(angle)
    rest = jnp.ones((length, HEAD_DIM - ROT), F32)
    cosine = jnp.concatenate([cosine, cosine, rest] * 2, axis=1)
    sine = jnp.concatenate([-sine, sine, 0.0 * rest] * 2, axis=1)

    normed, mean, inv_std = layer_norm(rows_all, behind(gain, grad_rows), shift)
    both = fsdp_gather(behind(qkv_here, normed))
    mine, others = order[:chips], order[chips:]

    active, slope = hidden_layer(normed, fc1, bias_fc1)
    other_fc2 = block_terms(active, grad_rows, unit, others)
    sum_fc2 = LineSum(other_fc2, lambda got: block_terms(active, grad_rows, unit, mine, got))
    fc2 = fsdp_gather(behind(fc2_here, sum_fc2.first))

    ahead = sum_fc2.steps[1:2]
    if strided:
        high = each * HEAD_DIM
        out_w, grad_mixed = mixed_gradient(grad_rows, both, 3 * head_cols, out_cut, high, ahead)
    else:
        out_w = pick(fsdp_gather(w_out).reshape(seqs, head_cols, width), me)
        grad_mixed = mm(grad_rows, out_w, 1, 1).astype(BF)
    qkv = product(normed, both, bias_qkv, [grad_mixed])
    tables = (cosine, sine, opening[None])
    pairs = heads // 2
    early = attention(qkv, grad_mixed, *tables, 0, pairs // 2)
    mixed, grad_qkv = attention(
        qkv, grad_mixed, *tables, pairs // 2, pairs - pairs // 2, early, sum_fc2.steps[2:4]
    )
    out_grad = mm(mixed, grad_rows, 0, 0).astype(BF)
    ahead = sum_fc2.steps[4:6]
    if strided:
        out_grad = out_grad.reshape(shards, each * HEAD_DIM, width)

        def qkv_terms(index, add=None, after=()):
            return two_terms(normed, grad_qkv, rows_here, out_grad, out_cut, index, add, after)

    else:
        spread = put(jnp.zeros((seqs, head_cols, width), BF), out_grad, me)
        spread = spread.reshape(shards, shard_heads * HEAD_DIM, width)
        part_out = LineSum(
            jnp.stack([pick(spread, i) for i in others]),
            lambda got: jnp.stack([pick(spread, i) for i in mine]) + got,
        ).total

        def qkv_terms(index, add=None, after=()):
            return block_terms(normed, grad_qkv, rows_here, index, add, after)

    other_qkv = qkv_terms(others, None, ahead)
    grad_hidden = times_slope(grad_rows, fc2, slope, [other_qkv])
    sum_qkv = LineSum(other_qkv, lambda got: qkv_terms(mine, got, [grad_hidden]))
    other_fc1 = block_terms(normed, grad_hidden, rows_here, others, None, sum_qkv.steps[:1])
    partial = output_terms(active, fc2, mixed, out_w, [other_fc1])
    grad_partial, sum_gain, sum_shift = normed_terms(
        grad_qkv,
        both,
        grad_hidden,
        fc1,
        rows_all,
        mean,
        inv_std,
        [partial] + sum_qkv.steps[1:2],
    )
    sum_fc1 = LineSum(
        other_fc1,
        lambda got: block_terms(
            normed, grad_hidden, rows_here, mine, got, sum_qkv.steps[2:4] + [grad_partial]
        ),
    )
    result = seq_sum(partial.reshape(seqs, tok, width))
    grad_normed = seq_sum(grad_partial.reshape(seqs, tok, width))
    whole_fc2 = seq_all(sum_fc2.total.astype(BF))
    total = behind(sum_qkv.total.astype(BF), sum_fc1.steps[1])
    whole_qkv = seq_all(behind(total, result))
    whole_fc1 = seq_all(behind(sum_fc1.total.astype(BF), grad_normed))
    output = (inputs[0].astype(F32) + result + (bias_out + bias_fc2)).astype(BF)[None]
    sum_gain, sum_shift = sum_gain[0], sum_shift[0]
    own_std = pick(inv_std.reshape(seqs, tok, 1), me)
    own_hat = (inputs[0].astype(F32) - pick(mean.reshape(seqs, tok, 1), me)) * own_std
    scaled = grad_normed * gain
    grad_in = own_std * (
        scaled
        - jnp.mean(scaled, axis=-1, keepdims=True)
        - own_hat * jnp.mean(scaled * own_hat, axis=-1, keepdims=True)
    )
    grad_in = cotangent[0].astype(F32) + grad_in

    sum_bfc1 = jnp.sum(grad_hidden.astype(F32), axis=0).reshape(shards, unit)
    sum_bfc1 = put(jnp.zeros((shards, seqs, unit), F32), sum_bfc1, me, 1)
    sum_bqkv = by_heads(jnp.sum(grad_qkv.astype(F32), axis=0), heads)
    if strided:
        sum_bqkv = sum_bqkv.reshape(shards, each * 3 * HEAD_DIM)
        sum_bqkv = put(jnp.zeros((shards, seqs, each * 3 * HEAD_DIM), F32), sum_bqkv, me, 1)
    else:
        sum_bqkv = put(jnp.zeros((seqs, heads * 3 * HEAD_DIM), F32), sum_bqkv, me)
    sum_out = jnp.sum(cotangent[0].astype(F32), axis=0)
    vectors = jnp.concatenate(
        [v.reshape(shards, -1) for v in (sum_gain, sum_shift, sum_out, sum_bqkv, sum_bfc1)], axis=1
    )
    vectors = vectors[:, None]
    vectors = LineSum(
        jnp.stack([pick(vectors, i) for i in others]),
        lambda got: jnp.stack([pick(vectors, i) for i in mine]) + got,
    ).total
    vectors = jnp.sum(seq_gather(vectors), axis=(0, 1))
    ends = [sizes[0], sizes[1], sizes[2], sizes[4], sizes[5]]
    ends = [sum(ends[:i]) for i in range(len(ends) + 1)]
    total_gain, total_shift, total_bout, total_bqkv, total_bfc1 = [
        vectors[a:b] for a, b in zip(ends[:-1], ends[1:])
    ]

    total_wfc2 = whole_fc2.astype(F32).reshape(seqs * unit, width)
    if unit % 128 == 0:
        total_wfc1 = spread_columns(whole_fc1, unit)
    else:
        total_wfc1 = whole_fc1.astype(F32).reshape(seqs, rows_here, shards, unit)
        total_wfc1 = total_wfc1.transpose(1, 2, 0, 3).reshape(rows_here, -1)
    if strided and each == 1:
        total_wqkv = spread_heads(whole_qkv, heads // 2)
    else:
        total_wqkv = by_heads(whole_qkv[:, :, : 3 * head_cols].astype(F32), heads)
        if strided:
            total_wqkv = total_wqkv.reshape(seqs, rows_here, shards, each * 3 * HEAD_DIM)
            total_wqkv = total_wqkv.transpose(1, 2, 0, 3).reshape(rows_here, -1)
        else:
            total_wqkv = total_wqkv.transpose(1, 0, 2).reshape(rows_here, -1)
    if strided:
        total_wout = whole_qkv[:, :, 3 * head_cols :].astype(F32)
        total_wout = total_wout.reshape(seqs, out_cut, each * HEAD_DIM, width // out_cut)
        total_wout = jnp.swapaxes(total_wout, 1, 2).reshape(-1, width)
    else:
        total_wout = jnp.sum(seq_all(part_out.astype(BF)).astype(F32), axis=0)
    return (
        output,
        grad_in[None],
        total_gain,
        total_shift,
        total_wqkv,
        total_bqkv,
        total_wout,
        total_bout,
        total_wfc1,
        total_bfc1,
        total_wfc2,
        total_bout,
    )


def solution(mesh):
    rows, vector, matrix = P("fsdp", "seq", None), P("fsdp"), P("fsdp", None)
    weights = (vector, vector) + (matrix, vector) * 4
    return jax.shard_map(
        per_device,
        mesh=mesh,
        in_specs=(rows, matrix) + weights + (rows,),
        out_specs=(rows, rows) + weights,
        check_vma=False,
    )
```

time: 906 us -> 686 us (0.76)
  matrix products: 223 us -> 4.92 us
  Pallas kernels: 0 us -> 213 us
  local copies, waits for them, and re-layouts: 183 us -> 52 us
  waiting for transfers between devices: 235 us -> 176 us
  other arithmetic: 106 us -> 78.1 us
  between operations: 15.7 us -> 28.6 us
    pallas_call x0 -> x17, Pallas kernels: none -> 213 us  [the longest x2 47.1 us: attention(): pl.pallas_call(functools.partial(attention_kernel, min(256, length), HEAD...]
    dot_general x12 -> x1, matrix products: 143 us -> 4.92 us  [mm(): lax.dot_general(left, right, (((left_dim,), (right_dim,)), ((), ())), pre...]
    ppermute x62 -> x28, waiting for transfers between devices: 235 us -> 136 us  [the longest x20 93.2 us: to_chips(): return lax.ppermute(array, 'fsdp', pairs)]
    dot_general x14 -> x0, matrix products: 80.1 us -> none  [the longest x4 31.2 us: block_scores(): jnp.einsum('qhd,khd->hqk', lax.dynamic_slice_in_dim(query, begin, rows, 0...]
    dynamic_update_slice x30 -> x2, local copies, waits for them, and re-layouts: 60.7 us -> 0.12 us  [put(): return lax.dynamic_update_index_in_dim(array, piece, index, axis)]
    convert_element_type x20 -> x8, other arithmetic: 63.6 us -> 18.7 us  [the longest x5 12.6 us: __init__(): down = (down.astype(F32) + own[step].astype(F32)).astype(own.dtype)]
    all_to_all x0 -> x3, waiting for transfers between devices: none -> 39.7 us  [seq_exchange(): return lax.all_to_all(blocks, 'seq', split_axis=0, concat_axis=0)]
    convert_element_type x4 -> x0, local copies, waits for them, and re-layouts: 27.5 us -> none  [the longest x2 22.9 us: per_device(): total_wfc1.transpose(1, 2, 0, 3).reshape(rows_here, -1).astype(F32)]
  transfers between devices with their start and end apart: 66 -> 37, of which waited for: 24 -> 19; matrix products, arithmetic and copies ran while one was open for 53% -> 17% of each run, Pallas kernels for 0% -> 28%
where the time goes in v2:
time: 686 us; the launch traced here: 677 us
  Pallas kernels  213 us (31%)
  waiting for transfers between devices  176 us (26%)
  starting transfers between devices  108 us (16%)
  other arithmetic  78.1 us (11%)
  local copies, waits for them, and re-layouts  52 us (8%)
  between operations  28.6 us (4%)
  blocking collectives  15.9 us (2%)
    ppermute x20, waiting for transfers between devices, to_chips(): return lax.ppermute(array, 'fsdp', pairs)  93.2 us
    ppermute x20, starting transfers between devices, to_chips(): return lax.ppermute(array, 'fsdp', pairs)  85.7 us
    pallas_call x2, Pallas kernels, attention(): pl.pallas_call(functools.partial(attention_kernel, min(256, length), HEAD...  47.1 us
    all_to_all x3, waiting for transfers between devices, seq_exchange(): return lax.all_to_all(blocks, 'seq', split_axis=0, concat_axis=0)  39.7 us
    pallas_call x4, Pallas kernels, block_terms(): pl.pallas_call(functools.partial(term_kernel, len(adds)), grid_spec=pltpu...  39.4 us
    ppermute x4, waiting for transfers between devices, seq_gather_two(): got.append(lax.ppermute(whole, 'seq', pairs))  34.4 us
    unnamed x98, local copies, waits for them, and re-layouts  25.2 us
    pallas_call x1, Pallas kernels, normed_terms(): pl.pallas_call(normed_kernel, grid=(columns // cut,), in_specs=[whole(one...  23 us
  transfers between devices with their start and end apart: 37, of which 19 were waited for; matrix products, arithmetic and copies ran while one was open for 17% of the time, Pallas kernels for 28%

profile of v2, /device:TPU:0, one launch (start us, length us, event | category | flops | bytes accessed | tf_op | source)
XLA Modules:
  0.0 676.5 jit_solution(2800295030432153783)
XLA Ops:
  24.6 21.8 %collective-permute-done = bf16[1,256,2048]{2,1,0:T(8,128)(2,1)} collective-permute-done((bf16[1,256,2048]{2,1,0:T(8,128)(2,1)S(1)}, bf16[1,256,2048]{2,1,0:T(8,128)(2,1)}, u32[]{:S(2)}, u32[]{:S(2)}) %collective-permute-start) | collective-permute-done | bytes 1048608 | tf_op jit(solution)/shard_map/ppermute | solution.py:68
  61.9 15.9 %all-gather.5 = bf16[8,1,2816]{2,1,0:T(2,128)(2,1)S(1)} all-gather(bf16[1,1,2816]{2,1,0:T(2,128)(2,1)S(1)} %reshape.531), channel_id=2, replica_groups=mesh['seq'=4,'fsdp'=8] {'fsdp'}, dimensions={0}, use_global_device_ids=true | all-gather | bytes 50688 | tf_op jit(solution)/shard_map/all_gather | solution.py:622
  90.5 10.9 %collective-permute-done.2 = bf16[2,256,2048]{2,1,0:T(8,128)(2,1)} collective-permute-done((bf16[2,256,2048]{2,1,0:T(8,128)(2,1)}, bf16[2,256,2048]{2,1,0:T(8,128)(2,1)}, u32[]{:S(2)}, u32[]{:S(2)}) %collective-permute-start.2) | collective-permute-done | bytes 2097184 | tf_op jit(solution)/shard_map/ppermute | solution.py:68
  118.4 6.3 shard_map.220
  130.1 17.9 %shard_map.221 = (bf16[1024,2048]{1,0:T(8,128)(2,1)}, bf16[1024,2048]{1,0:T(8,128)(2,1)}) custom-call(bf16[1024,2048]{1,0:T(8,128)(2,1)} %get-tuple-element.26.left_ref, bf16[2048,2048]{1,0:T(8,128)(2,1)} %all-gather.13.cloned.1.call-done.right_ref.second_ref, f32[1,2048]{1,0:T(1,128)} %bitcast.246), custom_call_target="tpu_custom_call" | custom-call | flops 8589934592 | bytes 16777216 | tf_op jit(solution)/shard_map/pallas_call | solution.py:302
  148.0 9.5 %shard_map.222 = bf16[4,256,2048]{2,1,0:T(8,128)(2,1)} custom-call(s32[4]{0:T(128)} %pad_add_fusion.1.index_ref, bf16[1024,2048]{1,0:T(8,128)(2,1)} %get-tuple-element.27.left_ref, bf16[1024,2048]{1,0:T(8,128)(2,1)} %bitcast.201), custom_call_target="tpu_custom_call" | custom-call | flops 4294967296 | bytes 8388608 | tf_op jit(solution)/shard_map/pallas_call | solution.py:334
  158.1 6.9 %collective-permute-done.4.refs_0_ = bf16[4,256,2048]{2,1,0:T(8,128)(2,1)} collective-permute-done((bf16[4,256,2048]{2,1,0:T(8,128)(2,1)}, bf16[4,256,2048]{2,1,0:T(8,128)(2,1)}, u32[]{:S(2)}, u32[]{:S(2)}) %collective-permute-start.4) | collective-permute-done | bytes 4194336 | tf_op jit(solution)/shard_map/ppermute | solution.py:99
  165.0 10.3 %shard_map.223 = bf16[4,256,2048]{2,1,0:T(8,128)(2,1)} custom-call(s32[4]{0:T(128)} %pad_add_fusion.index_ref, bf16[1024,2048]{1,0:T(8,128)(2,1)} %get-tuple-element.27.left_ref, bf16[1024,2048]{1,0:T(8,128)(2,1)} %bitcast.202, bf16[4,256,2048]{2,1,0:T(8,128)(2,1)} %collective-permute-done.4.refs_0_), custom_call_target="tpu_custom_call" | custom-call | flops 4294967296 | bytes 8388608 | tf_op jit(solution)/shard_map/pallas_call | solution.py:334
  192.8 35.3 %collective-permute-done.5.refs_0_ = bf16[256,2048]{1,0:T(8,128)(2,1)S(1)} collective-permute-done((bf16[256,2048]{1,0:T(8,128)(2,1)}, bf16[256,2048]{1,0:T(8,128)(2,1)S(1)}, u32[]{:S(2)}, u32[]{:S(2)}) %collective-permute-start.5) | collective-permute-done | bytes 1048608 | tf_op jit(solution)/shard_map/ppermute | solution.py:94
  230.8 6.3 collective-permute-start.7
  237.2 7.0 %shard_map.224 = (bf16[512,2048]{1,0:T(8,128)(2,1)}, bf16[1024,512]{1,0:T(8,128)(2,1)}) custom-call(bf16[1024,2048]{1,0:T(8,128)(2,1)} %bitcast.203, bf16[2048,2048]{1,0:T(8,128)(2,1)} %all-gather.15.cloned.1.call-done.both_ref.right_ref.first_ref, bf16[256,2048]{1,0:T(8,128)(2,1)} %copy-done.18), custom_call_target="tpu_custom_call" | custom-call | flops 2147483648 | bytes 8388608 | tf_op jit(solution)/shard_map/pallas_call | solution.py:267
  244.2 11.2 %shard_map.225.qkv_ref = f32[1024,1536]{1,0:T(8,128)} custom-call(bf16[1024,2048]{1,0:T(8,128)(2,1)} %get-tuple-element.26.left_ref, bf16[2048,2048]{1,0:T(8,128)(2,1)} %all-gather.15.cloned.1.call-done.both_ref.right_ref.first_ref, f32[1,1536]{1,0:T(1,128)} %broadcast_in_dim_reshape.12.bias_ref, bf16[1024,512]{1,0:T(8,128)(2,1)} %get-tuple-element.28.refs_0_.grad_ref), custom_call_target="tpu_custom_call" | custom-call | flops 6442450944 | bytes 14680064 | tf_op jit(solution)/shard_map/pallas_call | solution.py:405
  255.4 23.5 %shard_map.226 = (bf16[1024,512]{1,0:T(8,128)(2,1)}, bf16[1024,1536]{1,0:T(8,128)(2,1)}) custom-call(f32[1024,1536]{1,0:T(8,128)} %shard_map.225.qkv_ref, bf16[1024,512]{1,0:T(8,128)(2,1)} %get-tuple-element.28.refs_0_.grad_ref, f32[1024,128]{1,0:T(8,128)} %concatenate.61.cos_ref, f32[1024,128]{1,0:T(8,128)} %concatenate.62.sin_ref, s32[1,1024]{1,0:T(1,128)} %bitcast.240), custom_call_target="tpu_custom_call" | custom-call | flops 6442450944 | bytes 6291456 | tf_op jit(solution)/shard_map/pallas_call | solution.py:196
  283.5 27.2 %collective-permute-start.9 = (bf16[256,2048]{1,0:T(8,128)(2,1)S(1)}, bf16[256,2048]{1,0:T(8,128)(2,1)S(1)}, u32[]{:S(2)}, u32[]{:S(2)}) collective-permute-start(bf16[256,2048]{1,0:T(8,128)(2,1)S(1)} %get-tuple-element.46), channel_id=1, source_target_pairs={{0,2},{1,3},{2,4},{3,5},{4,6},{5,7},{8,10},{9,11},{10,12},{11,13},... | collective-permute-start | bytes 3145736 | tf_op jit(solution)/shard_map/ppermute | solution.py:94
  310.7 23.6 %shard_map.227 = (bf16[1024,512]{1,0:T(8,128)(2,1)}, bf16[1024,1536]{1,0:T(8,128)(2,1)}) custom-call(f32[1024,1536]{1,0:T(8,128)} %shard_map.225.qkv_ref, bf16[1024,512]{1,0:T(8,128)(2,1)} %get-tuple-element.28.refs_0_.grad_ref, f32[1024,128]{1,0:T(8,128)} %concatenate.61.cos_ref, ...), custom_call_target="tpu_custom_call", output_to_operand_aliasing={{0}: (5, {}), {1}: (6, {})} | custom-call | flops 6442450944 | bytes 6291456 | tf_op jit(solution)/shard_map/pallas_call | solution.py:196
  341.1 7.1 %collective-permute-done.9.refs_1_ = bf16[256,2048]{1,0:T(8,128)(2,1)S(1)} collective-permute-done((bf16[256,2048]{1,0:T(8,128)(2,1)S(1)}, bf16[256,2048]{1,0:T(8,128)(2,1)S(1)}, u32[]{:S(2)}, u32[]{:S(2)}) %collective-permute-start.9) | collective-permute-done | bytes 1048608 | tf_op jit(solution)/shard_map/ppermute | solution.py:94
  349.2 8.5 %shard_map.228.refs_0_ = bf16[4,256,2048]{2,1,0:T(8,128)(2,1)} custom-call(s32[4]{0:T(128)} %pad_add_fusion.1.index_ref, bf16[1024,2048]{1,0:T(8,128)(2,1)} %get-tuple-element.26.left_ref, bf16[1024,1536]{1,0:T(8,128)(2,1)} %get-tuple-element.34.right_ref.one_ref, bf16[8,64,2048]{2,1,0:T(8,128)(2,1)} %bitcast.211, bf16[256,2048]{1,0:T(8,128)(2,1)} %copy-done.12, ...), custom_call_target="tpu_custom_call" | custom-call | flops 3221225472 | bytes 6291456 | tf_op jit(solution)/shard_map/pallas_call | solution.py:377
  357.6 14.6 %shard_map.229.refs_1_.right_ref.two_ref = bf16[1024,2048]{1,0:T(8,128)(2,1)} custom-call(bf16[1024,2048]{1,0:T(8,128)(2,1)} %bitcast.204, bf16[2048,2048]{1,0:T(8,128)(2,1)} %bitcast.248, bf16[1024,2048]{1,0:T(8,128)(2,1)} %get-tuple-element.33.slope_ref, bf16[4,256,2048]{2,1,0:T(8,128)(2,1)} %shard_map.228.refs_0_), custom_call_target="tpu_custom_call" | custom-call | flops 8589934592 | bytes 12582912 | tf_op jit(solution)/shard_map/pallas_call | solution.py:431
  372.2 9.4 %shard_map.230.refs_0_ = bf16[4,256,2048]{2,1,0:T(8,128)(2,1)} custom-call(s32[4]{0:T(128)} %pad_add_fusion.index_ref, bf16[1024,2048]{1,0:T(8,128)(2,1)} %get-tuple-element.26.left_ref, bf16[1024,1536]{1,0:T(8,128)(2,1)} %get-tuple-element.34.right_ref.one_ref, bf16[8,64,2048]{2,1,0:T(8,128)(2,1)} %bitcast.212, ...), custom_call_target="tpu_custom_call" | custom-call | flops 3221225472 | bytes 6291456 | tf_op jit(solution)/shard_map/pallas_call | solution.py:377
  381.6 9.5 %shard_map.231.refs_0_ = bf16[4,256,2048]{2,1,0:T(8,128)(2,1)} custom-call(s32[4]{0:T(128)} %pad_add_fusion.1.index_ref, bf16[1024,2048]{1,0:T(8,128)(2,1)} %get-tuple-element.26.left_ref, bf16[1024,2048]{1,0:T(8,128)(2,1)} %shard_map.229.refs_1_.right_ref.two_ref, bf16[4,256,2048]{2,1,0:T(8,128)(2,1)} %shard_map.230.refs_0_), custom_call_target="tpu_custom_call" | custom-call | flops 4294967296 | bytes 8388608 | tf_op jit(solution)/shard_map/pallas_call | solution.py:334
  401.1 16.3 %shard_map.232.refs_0_ = bf16[1024,2048]{1,0:T(8,128)(2,1)} custom-call(bf16[1024,2048]{1,0:T(8,128)(2,1)} %get-tuple-element.27.left_ref, bf16[2048,2048]{1,0:T(8,128)(2,1)} %bitcast.249, bf16[1024,512]{1,0:T(8,128)(2,1)} %get-tuple-element.31.second_ref, bf16[512,2048]{1,0:T(8,128)(2,1)} %get-tuple-element.32.weight_ref, ...), custom_call_target="tpu_custom_call" | custom-call | flops 10737418240 | bytes 12582912 | tf_op jit(solution)/shard_map/pallas_call | solution.py:456
  427.4 5.1 collective-permute-start.20
  432.5 23.0 %shard_map.233 = (bf16[1024,2048]{1,0:T(8,128)(2,1)}, f32[1,2048]{1,0:T(1,128)}, f32[1,2048]{1,0:T(1,128)}) custom-call(bf16[1024,1536]{1,0:T(8,128)(2,1)} %get-tuple-element.34.right_ref.one_ref, bf16[2048,2048]{1,0:T(8,128)(2,1)} %all-gather.15.cloned.1.call-done.both_ref.right_ref.first_ref, bf16[1024,2048]{1,0:T(8,128)(2,1)} %shard_map.229.refs_1_.right_ref.two_ref, ...), custom_call_target="tpu_custom_call" | custom-call | flops 15032385536 | bytes 16777216 | tf_op jit(solution)/shard_map/pallas_call | solution.py:491
  457.9 10.1 %shard_map.234 = bf16[4,256,2048]{2,1,0:T(8,128)(2,1)} custom-call(s32[4]{0:T(128)} %pad_add_fusion.index_ref, bf16[1024,2048]{1,0:T(8,128)(2,1)} %get-tuple-element.26.left_ref, bf16[1024,2048]{1,0:T(8,128)(2,1)} %shard_map.229.refs_1_.right_ref.two_ref, bf16[4,256,2048]{2,1,0:T(8,128)(2,1)} %collective-permute-done.18.refs_0_, ...), custom_call_target="tpu_custom_call" | custom-call | flops 4294967296 | bytes 8388608 | tf_op jit(solution)/shard_map/pallas_call | solution.py:334
  478.5 13.5 %all-to-all-done = bf16[4,256,2048]{2,1,0:T(8,128)(2,1)} async-done(((bf16[4,256,2048]{2,1,0:T(8,128)(2,1)}), bf16[4,256,2048]{2,1,0:T(8,128)(2,1)}, u32[]{:S(2)}, u32[]{:S(2)}) %all-to-all-start) | async-done | bytes 4194336 | tf_op jit(solution)/shard_map/all_to_all | solution.py:51
  501.1 18.8 %collective-permute-done.23 = bf16[256,2048]{1,0:T(8,128)(2,1)S(1)} collective-permute-done((bf16[256,2048]{1,0:T(8,128)(2,1)}, bf16[256,2048]{1,0:T(8,128)(2,1)S(1)}, u32[]{:S(2)}, u32[]{:S(2)}) %collective-permute-start.23) | collective-permute-done | bytes 1048608 | tf_op jit(solution)/shard_map/ppermute | solution.py:94
  535.1 20.7 %collective-permute-done.26 = bf16[256,2048]{1,0:T(8,128)(2,1)S(1)} collective-permute-done((bf16[256,2048]{1,0:T(8,128)(2,1)S(1)}, bf16[256,2048]{1,0:T(8,128)(2,1)S(1)}, u32[]{:S(2)}, u32[]{:S(2)}) %collective-permute-start.26) | collective-permute-done | bytes 1048608 | tf_op jit(solution)/shard_map/ppermute | solution.py:94
  565.8 26.1 %all-to-all-done.1 = bf16[4,256,2048]{2,1,0:T(8,128)(2,1)} async-done(((bf16[4,256,2048]{2,1,0:T(8,128)(2,1)}), bf16[4,256,2048]{2,1,0:T(8,128)(2,1)}, u32[]{:S(2)}, u32[]{:S(2)}) %all-to-all-start.1) | async-done | bytes 4194336 | tf_op jit(solution)/shard_map/all_to_all | solution.py:51
  614.2 5.2 collective-permute-start.13
  642.3 6.7 reshape.528
  650.7 5.5 shard_map.235
  661.5 7.4 %shard_map.236 = f32[256,8192]{1,0:T(8,128)} custom-call(bf16[4,256,2048]{2,1,0:T(8,128)(2,1)} %bitcast.217), custom_call_target="tpu_custom_call" | custom-call | bytes 12582912 | tf_op jit(solution)/shard_map/pallas_call | solution.py:522
  (273 shorter events, 206.8 us)
Async XLA Ops:
  7.2 122.9 %all-gather.13.cloned.1.call-start = ((), (), s32[]{:S(2)}) async-start(), calls=%async_computation.3 | async-start | bytes 9437184 | tf_op jit(solution)/shard_map/all_gather | solution.py:103
  20.1 217.1 %all-gather.15.cloned.1.call-start = ((), (), s32[]{:S(2)}) async-start(), calls=%async_computation.4 | async-start | bytes 9437184 | tf_op jit(solution)/shard_map/all_gather | solution.py:103
  20.1 26.3 %collective-permute-start = (bf16[1,256,2048]{2,1,0:T(8,128)(2,1)S(1)}, bf16[1,256,2048]{2,1,0:T(8,128)(2,1)}, u32[]{:S(2)}, u32[]{:S(2)}) collective-permute-start(bf16[1,256,2048]{2,1,0:T(8,128)(2,1)S(1)} %copy-done.8), channel_id=1, source_target_pairs={{0,16},{8,24},{16,0},{24,8},{1,17},{9,25},{17,1},{25,9},{2,18},{10... | collective-permute-start | bytes 3145736 | tf_op jit(solution)/shard_map/ppermute | solution.py:68
  23.2 25.7 %collective-permute-start.1 = (bf16[1,256,2048]{2,1,0:T(8,128)(2,1)S(1)}, bf16[1,256,2048]{2,1,0:T(8,128)(2,1)}, u32[]{:S(2)}, u32[]{:S(2)}) collective-permute-start(bf16[1,256,2048]{2,1,0:T(8,128)(2,1)S(1)} %copy-done.6), channel_id=1, source_target_pairs={{0,8},{8,0},{16,24},{24,16},{1,9},{9,1},{17,25},{25,17},{2,10},{10... | collective-permute-start | bytes 3145736 | tf_op jit(solution)/shard_map/ppermute | solution.py:68
  54.3 47.1 %collective-permute-start.2 = (bf16[2,256,2048]{2,1,0:T(8,128)(2,1)}, bf16[2,256,2048]{2,1,0:T(8,128)(2,1)}, u32[]{:S(2)}, u32[]{:S(2)}) collective-permute-start(bf16[2,256,2048]{2,1,0:T(8,128)(2,1)} %maximum_select_fusion.3), channel_id=1, source_target_pairs={{0,8},{8,0},{16,24},{24,16},{1,9},{9,1},{17,25},{25,17},{2,10},{10... | collective-permute-start | bytes 6291464 | tf_op jit(solution)/shard_map/ppermute | solution.py:68
  59.1 46.5 %collective-permute-start.3 = (bf16[2,256,2048]{2,1,0:T(8,128)(2,1)}, bf16[2,256,2048]{2,1,0:T(8,128)(2,1)}, u32[]{:S(2)}, u32[]{:S(2)}) collective-permute-start(bf16[2,256,2048]{2,1,0:T(8,128)(2,1)} %maximum_select_fusion.4), channel_id=1, source_target_pairs={{0,16},{8,24},{16,0},{24,8},{1,17},{9,25},{17,1},{25,9},{2,18},{10... | collective-permute-start | bytes 6291464 | tf_op jit(solution)/shard_map/ppermute | solution.py:68
  128.4 229.2 %all-gather.17.cloned.1.call-start = ((), (), s32[]{:S(2)}) async-start(), calls=%async_computation.5 | async-start | bytes 9437184 | tf_op jit(solution)/shard_map/all_gather | solution.py:103
  157.5 7.5 %collective-permute-start.4 = (bf16[4,256,2048]{2,1,0:T(8,128)(2,1)}, bf16[4,256,2048]{2,1,0:T(8,128)(2,1)}, u32[]{:S(2)}, u32[]{:S(2)}) collective-permute-start(bf16[4,256,2048]{2,1,0:T(8,128)(2,1)} %shard_map.222), channel_id=1, source_target_pairs={{0,1},{1,0},{2,3},{3,2},{4,5},{5,4},{6,7},{7,6},{8,9},{9,8},{10,11... | collective-permute-start | bytes 12582920 | tf_op jit(solution)/shard_map/ppermute | solution.py:99
  182.7 459.6 %all-gather.23.cloned.1.call-start = ((), (), s32[]{:S(2)}) async-start(), calls=%async_computation.8 | async-start | bytes 5242880 | tf_op jit(solution)/shard_map/all_gather | solution.py:80
  182.7 45.4 %collective-permute-start.5 = (bf16[256,2048]{1,0:T(8,128)(2,1)}, bf16[256,2048]{1,0:T(8,128)(2,1)S(1)}, u32[]{:S(2)}, u32[]{:S(2)}) collective-permute-start(bf16[256,2048]{1,0:T(8,128)(2,1)} %select_bitcast_fusion.4), channel_id=1, source_target_pairs={{6,4},{7,5},{0,2},{1,3},{14,12},{15,13},{8,10},{9,11},{22,20},{23,... | collective-permute-start | bytes 3145736 | tf_op jit(solution)/shard_map/ppermute | solution.py:94
  230.1 48.8 %collective-permute-start.6 = (bf16[256,2048]{1,0:T(8,128)(2,1)S(1)}, bf16[256,2048]{1,0:T(8,128)(2,1)S(1)}, u32[]{:S(2)}, u32[]{:S(2)}) collective-permute-start(bf16[256,2048]{1,0:T(8,128)(2,1)S(1)} %fusion.25), channel_id=1, source_target_pairs={{4,2},{5,3},{6,4},{7,5},{12,10},{13,11},{14,12},{15,13},{20,18},{2... | collective-permute-start | bytes 3145736 | tf_op jit(solution)/shard_map/ppermute | solution.py:94
  230.8 48.1 %collective-permute-start.7 = (bf16[256,2048]{1,0:T(8,128)(2,1)S(1)}, bf16[256,2048]{1,0:T(8,128)(2,1)}, u32[]{:S(2)}, u32[]{:S(2)}) collective-permute-start(bf16[256,2048]{1,0:T(8,128)(2,1)S(1)} %fusion.25), channel_id=1, source_target_pairs={{0,2},{1,3},{2,4},{3,5},{8,10},{9,11},{10,12},{11,13},{16,18},{17,... | collective-permute-start | bytes 3145736 | tf_op jit(solution)/shard_map/ppermute | solution.py:94
  282.2 58.9 %collective-permute-start.8 = (bf16[256,2048]{1,0:T(8,128)(2,1)}, bf16[256,2048]{1,0:T(8,128)(2,1)S(1)}, u32[]{:S(2)}, u32[]{:S(2)}) collective-permute-start(bf16[256,2048]{1,0:T(8,128)(2,1)} %get-tuple-element.47), channel_id=1, source_target_pairs={{2,0},{3,1},{4,2},{5,3},{6,4},{7,5},{10,8},{11,9},{12,10},{13,11},... | collective-permute-start | bytes 3145736 | tf_op jit(solution)/shard_map/ppermute | solution.py:94
  283.5 64.7 %collective-permute-start.9 = (bf16[256,2048]{1,0:T(8,128)(2,1)S(1)}, bf16[256,2048]{1,0:T(8,128)(2,1)S(1)}, u32[]{:S(2)}, u32[]{:S(2)}) collective-permute-start(bf16[256,2048]{1,0:T(8,128)(2,1)S(1)} %get-tuple-element.46), channel_id=1, source_target_pairs={{0,2},{1,3},{2,4},{3,5},{4,6},{5,7},{8,10},{9,11},{10,12},{11,13},... | collective-permute-start | bytes 3145736 | tf_op jit(solution)/shard_map/ppermute | solution.py:94
  357.6 14.6 %collective-permute-start.10 = (bf16[4,256,2048]{2,1,0:T(8,128)(2,1)}, bf16[4,256,2048]{2,1,0:T(8,128)(2,1)}, u32[]{:S(2)}, u32[]{:S(2)}) collective-permute-start(bf16[4,256,2048]{2,1,0:T(8,128)(2,1)} %shard_map.228.refs_0_), channel_id=1, source_target_pairs={{0,1},{1,0},{2,3},{3,2},{4,5},{5,4},{6,7},{7,6},{8,9},{9,8},{10,11... | collective-permute-start | bytes 12582920 | tf_op jit(solution)/shard_map/ppermute | solution.py:99
  391.1 66.8 %collective-permute-start.18 = (bf16[4,256,2048]{2,1,0:T(8,128)(2,1)}, bf16[4,256,2048]{2,1,0:T(8,128)(2,1)}, u32[]{:S(2)}, u32[]{:S(2)}) collective-permute-start(bf16[4,256,2048]{2,1,0:T(8,128)(2,1)} %shard_map.231.refs_0_), channel_id=1, source_target_pairs={{0,1},{1,0},{2,3},{3,2},{4,5},{5,4},{6,7},{7,6},{8,9},{9,8},{10,11... | collective-permute-start | bytes 12582920 | tf_op jit(solution)/shard_map/ppermute | solution.py:99
  396.0 27.5 %collective-permute-start.11 = (bf16[256,2048]{1,0:T(8,128)(2,1)S(1)}, bf16[256,2048]{1,0:T(8,128)(2,1)S(1)}, u32[]{:S(2)}, u32[]{:S(2)}) collective-permute-start(bf16[256,2048]{1,0:T(8,128)(2,1)S(1)} %select_bitcast_fusion.3), channel_id=1, source_target_pairs={{6,4},{7,5},{0,2},{1,3},{14,12},{15,13},{8,10},{9,11},{22,20},{23,... | collective-permute-start | bytes 3145736 | tf_op jit(solution)/shard_map/ppermute | solution.py:94
  417.4 74.7 %all-to-all-start = ((bf16[4,256,2048]{2,1,0:T(8,128)(2,1)}), bf16[4,256,2048]{2,1,0:T(8,128)(2,1)}, u32[]{:S(2)}, u32[]{:S(2)}) async-start(bf16[4,256,2048]{2,1,0:T(8,128)(2,1)} %bitcast.219), calls=%async_computation | async-start | bytes 8388608 | tf_op jit(solution)/shard_map/all_to_all | solution.py:51
  422.2 228.5 %all-gather.19.cloned.1.call-start = ((), (), s32[]{:S(2)}) async-start(), calls=%async_computation.6 | async-start | bytes 5242880 | tf_op jit(solution)/shard_map/all_gather | solution.py:80
  426.7 28.9 %collective-permute-start.19 = (bf16[256,2048]{1,0:T(8,128)(2,1)}, bf16[256,2048]{1,0:T(8,128)(2,1)S(1)}, u32[]{:S(2)}, u32[]{:S(2)}) collective-permute-start(bf16[256,2048]{1,0:T(8,128)(2,1)} %fusion.22), channel_id=1, source_target_pairs={{4,2},{5,3},{6,4},{7,5},{12,10},{13,11},{14,12},{15,13},{20,18},{2... | collective-permute-start | bytes 3145736 | tf_op jit(solution)/shard_map/ppermute | solution.py:94
  427.4 28.2 %collective-permute-start.20 = (bf16[256,2048]{1,0:T(8,128)(2,1)}, bf16[256,2048]{1,0:T(8,128)(2,1)S(1)}, u32[]{:S(2)}, u32[]{:S(2)}) collective-permute-start(bf16[256,2048]{1,0:T(8,128)(2,1)} %fusion.22), channel_id=1, source_target_pairs={{0,2},{1,3},{2,4},{3,5},{8,10},{9,11},{10,12},{11,13},{16,18},{17,... | collective-permute-start | bytes 3145736 | tf_op jit(solution)/shard_map/ppermute | solution.py:94
  470.6 28.7 %collective-permute-start.21 = (bf16[256,2048]{1,0:T(8,128)(2,1)}, bf16[256,2048]{1,0:T(8,128)(2,1)S(1)}, u32[]{:S(2)}, u32[]{:S(2)}) collective-permute-start(bf16[256,2048]{1,0:T(8,128)(2,1)} %select_bitcast_fusion.2), channel_id=1, source_target_pairs={{6,4},{7,5},{0,2},{1,3},{14,12},{15,13},{8,10},{9,11},{22,20},{23,... | collective-permute-start | bytes 3145736 | tf_op jit(solution)/shard_map/ppermute | solution.py:94
  475.5 44.5 %collective-permute-start.23 = (bf16[256,2048]{1,0:T(8,128)(2,1)}, bf16[256,2048]{1,0:T(8,128)(2,1)S(1)}, u32[]{:S(2)}, u32[]{:S(2)}) collective-permute-start(bf16[256,2048]{1,0:T(8,128)(2,1)} %get-tuple-element.45), channel_id=1, source_target_pairs={{0,2},{1,3},{2,4},{3,5},{4,6},{5,7},{8,10},{9,11},{10,12},{11,13},... | collective-permute-start | bytes 3145736 | tf_op jit(solution)/shard_map/ppermute | solution.py:94
  476.8 43.1 %collective-permute-start.22 = (bf16[256,2048]{1,0:T(8,128)(2,1)}, bf16[256,2048]{1,0:T(8,128)(2,1)S(1)}, u32[]{:S(2)}, u32[]{:S(2)}) collective-permute-start(bf16[256,2048]{1,0:T(8,128)(2,1)} %get-tuple-element.44), channel_id=1, source_target_pairs={{2,0},{3,1},{4,2},{5,3},{6,4},{7,5},{10,8},{11,9},{12,10},{13,11},... | collective-permute-start | bytes 3145736 | tf_op jit(solution)/shard_map/ppermute | solution.py:94
  522.7 69.3 %all-to-all-start.1 = ((bf16[4,256,2048]{2,1,0:T(8,128)(2,1)}), bf16[4,256,2048]{2,1,0:T(8,128)(2,1)}, u32[]{:S(2)}, u32[]{:S(2)}) async-start(bf16[4,256,2048]{2,1,0:T(8,128)(2,1)} %bitcast.207), calls=%async_computation.1 | async-start | bytes 8388608 | tf_op jit(solution)/shard_map/all_to_all | solution.py:51
  527.6 133.9 %all-gather.21.cloned.1.call-start = ((), (), s32[]{:S(2)}) async-start(), calls=%async_computation.7 | async-start | bytes 5242880 | tf_op jit(solution)/shard_map/all_gather | solution.py:80
  530.2 25.7 %collective-permute-start.26 = (bf16[256,2048]{1,0:T(8,128)(2,1)S(1)}, bf16[256,2048]{1,0:T(8,128)(2,1)S(1)}, u32[]{:S(2)}, u32[]{:S(2)}) collective-permute-start(bf16[256,2048]{1,0:T(8,128)(2,1)S(1)} %fusion.15), channel_id=1, source_target_pairs={{0,2},{1,3},{2,4},{3,5},{8,10},{9,11},{10,12},{11,13},{16,18},{17,... | collective-permute-start | bytes 3145736 | tf_op jit(solution)/shard_map/ppermute | solution.py:94
  559.5 37.5 %collective-permute-start.27 = (bf16[256,2048]{1,0:T(8,128)(2,1)}, bf16[256,2048]{1,0:T(8,128)(2,1)S(1)}, u32[]{:S(2)}, u32[]{:S(2)}) collective-permute-start(bf16[256,2048]{1,0:T(8,128)(2,1)} %get-tuple-element.43), channel_id=1, source_target_pairs={{0,2},{1,3},{2,4},{3,5},{4,6},{5,7},{8,10},{9,11},{10,12},{11,13},... | collective-permute-start | bytes 3145736 | tf_op jit(solution)/shard_map/ppermute | solution.py:94
  564.0 33.0 %collective-permute-start.25 = (bf16[256,2048]{1,0:T(8,128)(2,1)}, bf16[256,2048]{1,0:T(8,128)(2,1)}, u32[]{:S(2)}, u32[]{:S(2)}) collective-permute-start(bf16[256,2048]{1,0:T(8,128)(2,1)} %get-tuple-element.42), channel_id=1, source_target_pairs={{2,0},{3,1},{4,2},{5,3},{6,4},{7,5},{10,8},{11,9},{12,10},{13,11},... | collective-permute-start | bytes 3145736 | tf_op jit(solution)/shard_map/ppermute | solution.py:94
  614.2 6.5 collective-permute-start.13
  621.5 6.2 collective-permute-start.16
  638.8 10.1 %all-to-all-start.2 = ((f32[4,1,2560]{2,1,0:T(1,128)}), f32[4,1,2560]{2,1,0:T(1,128)S(1)}, u32[]{:S(2)}, u32[]{:S(2)}) async-start(f32[4,1,2560]{2,1,0:T(1,128)} %broadcast_in_dim.86), calls=%async_computation.2 | async-start | bytes 81920 | tf_op jit(solution)/shard_map/all_to_all | solution.py:51
  (40 other events, 412.8 us)
Sparse Core Ops, SparseCore 0:
  20.2 85.4 all-gather.12
  128.5 95.7 all-gather.14
  225.9 118.8 all-gather.16
  394.5 97.7 all-gather.22
  522.8 84.7 all-gather.18
  609.3 52.1 all-gather.20

commit v3 on v2

--- a/solution.py
+++ b/solution.py
@@ -101,6 +101,10 @@
 
 def fsdp_gather(block):
     return lax.all_gather(block, "fsdp", axis=0, tiled=True)
+
+
+def fsdp_sum(parts):
+    return lax.psum_scatter(parts, "fsdp", scatter_dimension=0, tiled=True)
 
 
 class LineSum:
@@ -296,7 +300,7 @@
 
 def hidden_layer(left, right, bias):
     rows, depth = left.shape
-    columns = right.shape[1]
+    columns = bias.shape[0]
     cut = min(512, columns)
     block = pl.BlockSpec((rows, cut), lambda j: (0, j))
     return pl.pallas_call(
@@ -348,6 +352,29 @@
         compiler_params=params(),
         cost_estimate=cost(2 * rows * width * count * columns, 4 * rows * columns),
     )(index, left, right, *adds, *after)
+
+
+def rows_kernel(left_ref, right_ref, *refs):
+    refs[-1][...] = mm(left_ref[...], right_ref[...], 0, 0).astype(BF)
+
+
+def row_terms(left, right, width, total, place, before=()):
+    rows, columns = right.shape
+    count = left.shape[1] // width
+    return pl.pallas_call(
+        rows_kernel,
+        grid=(count,),
+        in_specs=[
+            pl.BlockSpec((rows, width), lambda r: (0, r)),
+            pl.BlockSpec((rows, columns), lambda r: (0, 0)),
+        ]
+        + unread(before),
+        out_specs=pl.BlockSpec((width, columns), lambda r: (r, place)),
+        out_shape=jax.ShapeDtypeStruct((left.shape[1], total), BF),
+        input_output_aliases={2 + i: i for i in range(len(before))},
+        compiler_params=params(),
+        cost_estimate=cost(2 * rows * width * count * columns, 4 * rows * columns),
+    )(left, right, *before)
 
 
 def two_terms_kernel(cut, adds, index_ref, left_ref, right_ref, beside_ref, *refs):
@@ -423,7 +450,7 @@
     refs[-1][...] = value.astype(BF)
 
 
-def times_slope(left, right, slope, after=()):
+def times_slope(left, right, begin, slope, after=()):
     rows, depth = left.shape
     columns = right.shape[0]
     cut = min(512, columns)
@@ -433,7 +460,7 @@
         grid=(columns // cut,),
         in_specs=[
             pl.BlockSpec((rows, depth), lambda j: (0, 0)),
-            pl.BlockSpec((cut, depth), lambda j: (j, 0)),
+            pl.BlockSpec((cut, depth), lambda j: (j, begin // depth)),
             block,
         ]
         + unread(after),
@@ -449,16 +476,16 @@
     refs[-1][...] = value.astype(BF)
 
 
-def output_terms(left, right, second, weight, after=()):
+def output_terms(left, right, begin, second, weight, after=()):
     rows, depth = left.shape
-    columns = right.shape[1]
+    columns = weight.shape[1]
     cut = min(512, columns)
     return pl.pallas_call(
         output_kernel,
         grid=(columns // cut,),
         in_specs=[
             pl.BlockSpec((rows, depth), lambda j: (0, 0)),
-            pl.BlockSpec((depth, cut), lambda j: (0, j)),
+            pl.BlockSpec((depth, cut), lambda j: (0, begin // cut + j)),
             pl.BlockSpec(second.shape, lambda j: (0, 0)),
             pl.BlockSpec((second.shape[1], cut), lambda j: (0, j)),
         ]
@@ -495,7 +522,7 @@
             whole(one),
             pl.BlockSpec((cut, one.shape[1]), lambda j: (j, 0)),
             whole(two),
-            pl.BlockSpec((cut, second.shape[1]), lambda j: (j, 0)),
+            pl.BlockSpec((cut, two.shape[1]), lambda j: (j, 0)),
             pl.BlockSpec((rows, cut), lambda j: (0, j)),
             whole(mean),
             whole(std),
@@ -631,7 +658,12 @@
         bias_qkv = pick(bias_qkv.reshape(seqs, heads * 3 * HEAD_DIM), me)
     bias_qkv = by_pairs(bias_qkv.reshape(3 * head_cols), heads)
 
-    fc1 = fsdp_gather(fc1_here)
+    joined = rows_here == unit and hidden_cols == width and unit % 128 == 0
+    if joined:
+        fc1 = fc2 = fsdp_gather(jnp.concatenate([fc1_here, fc2_here], axis=1))
+        begin = hidden_cols
+    else:
+        fc1, fc2, begin = fsdp_gather(fc1_here), fsdp_gather(fc2_here), 0
     rows_all, grad_rows = seq_gather_two(inputs[0], cotangent[0])
     rows_all, grad_rows = rows_all.reshape(length, width), grad_rows.reshape(length, width)
 
@@ -651,70 +683,49 @@
     mine, others = order[:chips], order[chips:]
 
     active, slope = hidden_layer(normed, fc1, bias_fc1)
-    other_fc2 = block_terms(active, grad_rows, unit, others)
-    sum_fc2 = LineSum(other_fc2, lambda got: block_terms(active, grad_rows, unit, mine, got))
-    fc2 = fsdp_gather(behind(fc2_here, sum_fc2.first))
-
-    ahead = sum_fc2.steps[1:2]
+    if joined:
+        terms = row_terms(active, grad_rows, unit, 2 * width, 0)
+        grad_hidden = times_slope(grad_rows, fc2, begin, slope, [terms])
+        terms = row_terms(normed, grad_hidden, rows_here, 2 * width, 1, [terms])
+        sums = fsdp_sum(terms)
+        part_fc2, part_fc1 = sums[:, :width], sums[:, width:]
+    else:
+        part_fc2 = fsdp_sum(mm(active, grad_rows, 0, 0).astype(BF))
+        grad_hidden = times_slope(grad_rows, fc2, begin, slope)
+        terms = mm(normed, grad_hidden, 0, 0).astype(BF)
+        part_fc1 = fsdp_sum(terms)
+
     if strided:
         high = each * HEAD_DIM
-        out_w, grad_mixed = mixed_gradient(grad_rows, both, 3 * head_cols, out_cut, high, ahead)
+        out_w, grad_mixed = mixed_gradient(grad_rows, both, 3 * head_cols, out_cut, high, [terms])
     else:
         out_w = pick(fsdp_gather(w_out).reshape(seqs, head_cols, width), me)
         grad_mixed = mm(grad_rows, out_w, 1, 1).astype(BF)
     qkv = product(normed, both, bias_qkv, [grad_mixed])
     tables = (cosine, sine, opening[None])
-    pairs = heads // 2
-    early = attention(qkv, grad_mixed, *tables, 0, pairs // 2)
-    mixed, grad_qkv = attention(
-        qkv, grad_mixed, *tables, pairs // 2, pairs - pairs // 2, early, sum_fc2.steps[2:4]
-    )
+    mixed, grad_qkv = attention(qkv, grad_mixed, *tables, 0, heads // 2)
     out_grad = mm(mixed, grad_rows, 0, 0).astype(BF)
-    ahead = sum_fc2.steps[4:6]
     if strided:
         out_grad = out_grad.reshape(shards, each * HEAD_DIM, width)
-
-        def qkv_terms(index, add=None, after=()):
-            return two_terms(normed, grad_qkv, rows_here, out_grad, out_cut, index, add, after)
-
+        all_qkv = two_terms(normed, grad_qkv, rows_here, out_grad, out_cut, list(range(shards)))
+        all_qkv = all_qkv.reshape(width, -1)
     else:
         spread = put(jnp.zeros((seqs, head_cols, width), BF), out_grad, me)
-        spread = spread.reshape(shards, shard_heads * HEAD_DIM, width)
-        part_out = LineSum(
-            jnp.stack([pick(spread, i) for i in others]),
-            lambda got: jnp.stack([pick(spread, i) for i in mine]) + got,
-        ).total
-
-        def qkv_terms(index, add=None, after=()):
-            return block_terms(normed, grad_qkv, rows_here, index, add, after)
-
-    other_qkv = qkv_terms(others, None, ahead)
-    grad_hidden = times_slope(grad_rows, fc2, slope, [other_qkv])
-    sum_qkv = LineSum(other_qkv, lambda got: qkv_terms(mine, got, [grad_hidden]))
-    other_fc1 = block_terms(normed, grad_hidden, rows_here, others, None, sum_qkv.steps[:1])
-    partial = output_terms(active, fc2, mixed, out_w, [other_fc1])
+        part_out = fsdp_sum(spread.reshape(seqs * head_cols, width))
+        all_qkv = mm(normed, grad_qkv, 0, 0).astype(BF)
+    part_qkv = fsdp_sum(all_qkv)
+    partial = output_terms(active, fc2, begin, mixed, out_w, [all_qkv])
+    result = seq_sum(partial.reshape(seqs, tok, width))
     grad_partial, sum_gain, sum_shift = normed_terms(
-        grad_qkv,
-        both,
-        grad_hidden,
-        fc1,
-        rows_all,
-        mean,
-        inv_std,
-        [partial] + sum_qkv.steps[1:2],
+        grad_qkv, both, grad_hidden, fc1, rows_all, mean, inv_std, [partial]
     )
-    sum_fc1 = LineSum(
-        other_fc1,
-        lambda got: block_terms(
-            normed, grad_hidden, rows_here, mine, got, sum_qkv.steps[2:4] + [grad_partial]
-        ),
-    )
-    result = seq_sum(partial.reshape(seqs, tok, width))
     grad_normed = seq_sum(grad_partial.reshape(seqs, tok, width))
-    whole_fc2 = seq_all(sum_fc2.total.astype(BF))
-    total = behind(sum_qkv.total.astype(BF), sum_fc1.steps[1])
-    whole_qkv = seq_all(behind(total, result))
-    whole_fc1 = seq_all(behind(sum_fc1.total.astype(BF), grad_normed))
+    part_fc2 = behind(part_fc2, result)
+    if joined:
+        whole_fc2, whole_fc1 = seq_gather_two(part_fc2, part_fc1)
+    else:
+        whole_fc2, whole_fc1 = seq_all(part_fc2), seq_all(part_fc1)
+    whole_qkv = seq_all(behind(behind(part_qkv, grad_normed), whole_fc1))
     output = (inputs[0].astype(F32) + result + (bias_out + bias_fc2)).astype(BF)[None]
     sum_gain, sum_shift = sum_gain[0], sum_shift[0]
     own_std = pick(inv_std.reshape(seqs, tok, 1), me)

time: 686 us -> 625 us (0.911)
  starting transfers between devices: 108 us -> 36.7 us
  waiting for transfers between devices: 176 us -> 207 us
  other arithmetic: 78.1 us -> 58.3 us
  Pallas kernels: 213 us -> 195 us
  blocking collectives: 15.9 us -> 25 us
    ppermute x20 -> x5, waiting for transfers between devices: 93.2 us -> 4.09 us  [to_chips(): return lax.ppermute(array, 'fsdp', pairs)]
    ppermute x20 -> x5, starting transfers between devices: 85.7 us -> 13.2 us  [to_chips(): return lax.ppermute(array, 'fsdp', pairs)]
    all_gather x3 -> x2, waiting for transfers between devices: 0.02 us -> 59.9 us  [fsdp_gather(): return lax.all_gather(block, 'fsdp', axis=0, tiled=True)]
    ppermute x4 -> x8, waiting for transfers between devices: 34.4 us -> 86.9 us  [seq_gather_two(): got.append(lax.ppermute(whole, 'seq', pairs))]
    convert_element_type x7 -> x1, other arithmetic: 18.7 us -> 4.75 us  [per_device(): total_wfc2 = whole_fc2.astype(F32).reshape(seqs * unit, width)]
    pallas_call x4 -> x2, Pallas kernels: 39.4 us -> 28.4 us  [row_terms(): pl.pallas_call(rows_kernel, grid=(count,), in_specs=[pl.BlockSpec((rows,...]
    all_to_all x3 -> x2, waiting for transfers between devices: 39.7 us -> 49.8 us  [seq_exchange(): return lax.all_to_all(blocks, 'seq', split_axis=0, concat_axis=0)]
    all_to_all x0 -> x1, blocking collectives: none -> 8.16 us  [seq_exchange(): return lax.all_to_all(blocks, 'seq', split_axis=0, concat_axis=0)]
  transfers between devices with their start and end apart: 37 -> 21, of which waited for: 19 -> 16; matrix products, arithmetic and copies ran while one was open for 17% -> 15% of each run, Pallas kernels for 28% -> 31%
where the time goes in v3:
time: 625 us; the launch traced here: 616 us
  waiting for transfers between devices  207 us (33%)
  Pallas kernels  195 us (31%)
  other arithmetic  58.3 us (9%)
  local copies, waits for them, and re-layouts  56.8 us (9%)
  starting transfers between devices  36.7 us (6%)
  between operations  32.3 us (5%)
  blocking collectives  25 us (4%)
    ppermute x8, waiting for transfers between devices, seq_gather_two(): got.append(lax.ppermute(whole, 'seq', pairs))  86.9 us
    all_gather x2, waiting for transfers between devices, fsdp_gather(): return lax.all_gather(block, 'fsdp', axis=0, tiled=True)  59.9 us
    all_to_all x2, waiting for transfers between devices, seq_exchange(): return lax.all_to_all(blocks, 'seq', split_axis=0, concat_axis=0)  49.8 us
    pallas_call x1, Pallas kernels, attention(): pl.pallas_call(functools.partial(attention_kernel, min(256, length), HEAD...  44.3 us
    pallas_call x2, Pallas kernels, row_terms(): pl.pallas_call(rows_kernel, grid=(count,), in_specs=[pl.BlockSpec((rows,...  28.4 us
    unnamed x95, local copies, waits for them, and re-layouts  25.3 us
    pallas_call x1, Pallas kernels, normed_terms(): pl.pallas_call(normed_kernel, grid=(columns // cut,), in_specs=[whole(one...  22.9 us
    pallas_call x1, Pallas kernels, hidden_layer(): pl.pallas_call(hidden_kernel, grid=(columns // cut,), in_specs=[pl.BlockS...  17.9 us
  transfers between devices with their start and end apart: 21, of which 16 were waited for; matrix products, arithmetic and copies ran while one was open for 15% of the time, Pallas kernels for 31%

profile of v3, /device:TPU:0, one launch (start us, length us, event | category | flops | bytes accessed | tf_op | source)
XLA Modules:
  0.0 615.9 jit_solution(424007337995158192)
XLA Ops:
  23.2 21.7 %collective-permute-done.1 = bf16[1,256,2048]{2,1,0:T(8,128)(2,1)} collective-permute-done((bf16[1,256,2048]{2,1,0:T(8,128)(2,1)S(1)}, bf16[1,256,2048]{2,1,0:T(8,128)(2,1)}, u32[]{:S(2)}, u32[]{:S(2)}) %collective-permute-start.1) | collective-permute-done | bytes 1048608 | tf_op jit(solution)/shard_map/ppermute | solution.py:68
  60.4 16.9 %all-gather.2 = bf16[8,1,2816]{2,1,0:T(2,128)(2,1)S(1)} all-gather(bf16[1,1,2816]{2,1,0:T(2,128)(2,1)S(1)} %reshape.657), channel_id=2, replica_groups=mesh['seq'=4,'fsdp'=8] {'fsdp'}, dimensions={0}, use_global_device_ids=true | all-gather | bytes 50688 | tf_op jit(solution)/shard_map/all_gather | solution.py:649
  77.3 4.6 copy.79
  90.1 9.9 %collective-permute-done.3 = bf16[2,256,2048]{2,1,0:T(8,128)(2,1)} collective-permute-done((bf16[2,256,2048]{2,1,0:T(8,128)(2,1)}, bf16[2,256,2048]{2,1,0:T(8,128)(2,1)}, u32[]{:S(2)}, u32[]{:S(2)}) %collective-permute-start.3) | collective-permute-done | bytes 2097184 | tf_op jit(solution)/shard_map/ppermute | solution.py:68
  117.1 6.4 %shard_map.220 = (bf16[1024,2048]{1,0:T(8,128)(2,1)}, f32[1024,1]{1,0:T(8,128)}, f32[1024,1]{1,0:T(8,128)}) custom-call(bf16[1024,2048]{1,0:T(8,128)(2,1)} %bitcast.172, f32[1,2048]{1,0:T(1,128)} %bitcast.201, f32[1,2048]{1,0:T(1,128)} %bitcast.202), custom_call_target="tpu_custom_call" | custom-call | flops 20971520 | bytes 8388608 | tf_op jit(solution)/shard_map/pallas_call | solution.py:238
  128.3 44.9 %all-gather.7.cloned.1.call-done.right_ref.second_ref = bf16[2048,4096]{1,0:T(8,128)(2,1)} async-done(((bf16[256,4096]{1,0:T(8,128)(2,1)}), bf16[2048,4096]{1,0:T(8,128)(2,1)}) %all-gather.7.cloned.1.call-update) | async-done | bytes 16777232 | tf_op jit(solution)/shard_map/all_gather | solution.py:103
  173.3 17.9 %shard_map.221 = (bf16[1024,2048]{1,0:T(8,128)(2,1)}, bf16[1024,2048]{1,0:T(8,128)(2,1)}) custom-call(bf16[1024,2048]{1,0:T(8,128)(2,1)} %get-tuple-element.24.left_ref, bf16[2048,4096]{1,0:T(8,128)(2,1)} %all-gather.7.cloned.1.call-done.right_ref.second_ref, f32[1,2048]{1,0:T(1,128)} %bitcast.209), custom_call_target="tpu_custom_call" | custom-call | flops 8589934592 | bytes 16777216 | tf_op jit(solution)/shard_map/pallas_call | solution.py:306
  191.1 14.1 %shard_map.222.refs_0_ = bf16[2048,4096]{1,0:T(8,128)(2,1)} custom-call(bf16[1024,2048]{1,0:T(8,128)(2,1)} %get-tuple-element.25.left_ref, bf16[1024,2048]{1,0:T(8,128)(2,1)} %bitcast.165), custom_call_target="tpu_custom_call" | custom-call | flops 8589934592 | bytes 8388608 | tf_op jit(solution)/shard_map/pallas_call | solution.py:364
  205.3 14.4 %shard_map.223.right_ref.two_ref = bf16[1024,2048]{1,0:T(8,128)(2,1)} custom-call(bf16[1024,2048]{1,0:T(8,128)(2,1)} %bitcast.166, bf16[2048,4096]{1,0:T(8,128)(2,1)} %all-gather.7.cloned.1.call-done.right_ref.second_ref, bf16[1024,2048]{1,0:T(8,128)(2,1)} %get-tuple-element.26.slope_ref, bf16[2048,4096]{1,0:T(8,128)(2,1)} %shard_map.222.refs_0_), custom_call_target="tpu_custom_call" | custom-call | flops 8589934592 | bytes 12582912 | tf_op jit(solution)/shard_map/pallas_call | solution.py:458
  219.7 14.2 %shard_map.224.refs_0_ = bf16[2048,4096]{1,0:T(8,128)(2,1)} custom-call(bf16[1024,2048]{1,0:T(8,128)(2,1)} %get-tuple-element.24.left_ref, bf16[1024,2048]{1,0:T(8,128)(2,1)} %shard_map.223.right_ref.two_ref, bf16[2048,4096]{1,0:T(8,128)(2,1)} %shard_map.222.refs_0_), custom_call_target="tpu_custom_call", output_to_operand_aliasing={{}: (2, {})} | custom-call | flops 8589934592 | bytes 8388608 | tf_op jit(solution)/shard_map/pallas_call | solution.py:364
  240.7 15.0 %all-gather.9.cloned.1.call-done.both_ref.right_ref.first_ref = bf16[2048,2048]{1,0:T(8,128)(2,1)} async-done(((bf16[256,2048]{1,0:T(8,128)(2,1)}), bf16[2048,2048]{1,0:T(8,128)(2,1)}) %all-gather.9.cloned.1.call-update) | async-done | bytes 8388624 | tf_op jit(solution)/shard_map/all_gather | solution.py:103
  255.8 6.4 %shard_map.225 = (bf16[512,2048]{1,0:T(8,128)(2,1)}, bf16[1024,512]{1,0:T(8,128)(2,1)}) custom-call(bf16[1024,2048]{1,0:T(8,128)(2,1)} %bitcast.167, bf16[2048,2048]{1,0:T(8,128)(2,1)} %all-gather.9.cloned.1.call-done.both_ref.right_ref.first_ref, bf16[2048,4096]{1,0:T(8,128)(2,1)} %shard_map.224.refs_0_), custom_call_target="tpu_custom_call" | custom-call | flops 2147483648 | bytes 8388608 | tf_op jit(solution)/shard_map/pallas_call | solution.py:271
  262.1 11.6 %shard_map.226.qkv_ref = f32[1024,1536]{1,0:T(8,128)} custom-call(bf16[1024,2048]{1,0:T(8,128)(2,1)} %get-tuple-element.24.left_ref, bf16[2048,2048]{1,0:T(8,128)(2,1)} %all-gather.9.cloned.1.call-done.both_ref.right_ref.first_ref, f32[1,1536]{1,0:T(1,128)} %broadcast_in_dim_reshape.12.bias_ref, bf16[1024,512]{1,0:T(8,128)(2,1)} %get-tuple-element.27.refs_0_.grad_ref), custom_call_target="tpu_custom_call" | custom-call | flops 6442450944 | bytes 14680064 | tf_op jit(solution)/shard_map/pallas_call | solution.py:432
  273.7 44.3 %shard_map.227 = (bf16[1024,512]{1,0:T(8,128)(2,1)}, bf16[1024,1536]{1,0:T(8,128)(2,1)}) custom-call(f32[1024,1536]{1,0:T(8,128)} %shard_map.226.qkv_ref, bf16[1024,512]{1,0:T(8,128)(2,1)} %get-tuple-element.27.refs_0_.grad_ref, f32[1024,128]{1,0:T(8,128)} %concatenate.101.cos_ref, f32[1024,128]{1,0:T(8,128)} %concatenate.102.sin_ref, s32[1,1024]{1,0:T(1,128)} %bitcast.204), custom_call_target="tpu_custom_call" | custom-call | flops 12884901888 | bytes 12582912 | tf_op jit(solution)/shard_map/pallas_call | solution.py:200
  318.0 4.9 convolution_convert_fusion
  323.5 13.6 %shard_map.228 = bf16[8,256,2048]{2,1,0:T(8,128)(2,1)} custom-call(s32[8]{0:T(128)} %iota.18.index_ref, bf16[1024,2048]{1,0:T(8,128)(2,1)} %get-tuple-element.24.left_ref, bf16[1024,1536]{1,0:T(8,128)(2,1)} %get-tuple-element.30.right_ref.one_ref, bf16[8,64,2048]{2,1,0:T(8,128)(2,1)} %bitcast.211), custom_call_target="tpu_custom_call" | custom-call | flops 6442450944 | bytes 6291456 | tf_op jit(solution)/shard_map/pallas_call | solution.py:404
  337.1 16.0 %shard_map.229.refs_0_ = bf16[1024,2048]{1,0:T(8,128)(2,1)} custom-call(bf16[1024,2048]{1,0:T(8,128)(2,1)} %get-tuple-element.25.left_ref, bf16[2048,4096]{1,0:T(8,128)(2,1)} %all-gather.7.cloned.1.call-done.right_ref.second_ref, bf16[1024,512]{1,0:T(8,128)(2,1)} %get-tuple-element.28.second_ref, bf16[512,2048]{1,0:T(8,128)(2,1)} %get-tuple-element.29.weight_ref, ...), custom_call_target="tpu_custom_call" | custom-call | flops 10737418240 | bytes 12582912 | tf_op jit(solution)/shard_map/pallas_call | solution.py:483
  353.1 4.9 all-to-all-start
  358.0 22.9 %shard_map.230 = (bf16[1024,2048]{1,0:T(8,128)(2,1)}, f32[1,2048]{1,0:T(1,128)}, f32[1,2048]{1,0:T(1,128)}) custom-call(bf16[1024,1536]{1,0:T(8,128)(2,1)} %get-tuple-element.30.right_ref.one_ref, bf16[2048,2048]{1,0:T(8,128)(2,1)} %all-gather.9.cloned.1.call-done.both_ref.right_ref.first_ref, bf16[1024,2048]{1,0:T(8,128)(2,1)} %shard_map.223.right_ref.two_ref, ...), custom_call_target="tpu_custom_call" | custom-call | flops 15032385536 | bytes 16777216 | tf_op jit(solution)/shard_map/pallas_call | solution.py:518
  380.9 25.3 %all-to-all-done = bf16[4,256,2048]{2,1,0:T(8,128)(2,1)} async-done(((bf16[4,256,2048]{2,1,0:T(8,128)(2,1)}), bf16[4,256,2048]{2,1,0:T(8,128)(2,1)}, u32[]{:S(2)}, u32[]{:S(2)}) %all-to-all-start) | async-done | bytes 4194336 | tf_op jit(solution)/shard_map/all_to_all | solution.py:51
  406.2 5.0 all-to-all-start.1
  420.2 4.7 reduce-scatter.3.cloned.1.call-done
  435.5 24.5 %all-to-all-done.1 = bf16[4,256,2048]{2,1,0:T(8,128)(2,1)} async-done(((bf16[4,256,2048]{2,1,0:T(8,128)(2,1)}), bf16[4,256,2048]{2,1,0:T(8,128)(2,1)}, u32[]{:S(2)}, u32[]{:S(2)}) %all-to-all-start.1) | async-done | bytes 4194336 | tf_op jit(solution)/shard_map/all_to_all | solution.py:51
  465.1 16.0 %collective-permute-done.11 = bf16[1,256,2048]{2,1,0:T(8,128)(2,1)} collective-permute-done((bf16[1,256,2048]{2,1,0:T(8,128)(2,1)S(1)}, bf16[1,256,2048]{2,1,0:T(8,128)(2,1)}, u32[]{:S(2)}, u32[]{:S(2)}) %collective-permute-start.11) | collective-permute-done | bytes 1048608 | tf_op jit(solution)/shard_map/ppermute | solution.py:68
  498.4 35.0 %collective-permute-done.12 = bf16[2,256,2048]{2,1,0:T(8,128)(2,1)S(1)} collective-permute-done((bf16[2,256,2048]{2,1,0:T(8,128)(2,1)S(1)}, bf16[2,256,2048]{2,1,0:T(8,128)(2,1)S(1)}, u32[]{:S(2)}, u32[]{:S(2)}) %collective-permute-start.12) | collective-permute-done | bytes 2097184 | tf_op jit(solution)/shard_map/ppermute | solution.py:68
  546.7 4.9 convert_reduce_fusion.4
  556.4 4.8 collective-permute-start.8
  563.9 5.2 collective-permute-start.9
  570.6 8.2 %all_to_all.15 = f32[4,1,2560]{2,1,0:T(1,128)S(1)} all-to-all(f32[4,1,2560]{2,1,0:T(1,128)S(1)} %broadcast_in_dim.95), channel_id=1, replica_groups=mesh['seq'=4,'fsdp'=8] {'seq'}, dimensions={0} | all-to-all | bytes 81920 | tf_op jit(solution)/shard_map/all_to_all | solution.py:51
  580.5 7.4 %shard_map.232 = f32[256,8192]{1,0:T(8,128)} custom-call(bf16[4,256,2048]{2,1,0:T(8,128)(2,1)} %bitcast.171), custom_call_target="tpu_custom_call" | custom-call | bytes 12582912 | tf_op jit(solution)/shard_map/pallas_call | solution.py:549
  592.7 4.7 bitcast_convert_fusion
  599.0 5.5 shard_map.231
  (237 shorter events, 127.6 us)
Async XLA Ops:
  7.2 79.3 %copy-start = (bf16[256,2048]{1,0:T(8,128)(2,1)S(1)}, bf16[256,2048]{1,0:T(8,128)(2,1)}, u32[]{:S(2)}) copy-start(bf16[256,2048]{1,0:T(8,128)(2,1)} %param.19) | copy-start | bytes 3145732
  7.2 166.1 %all-gather.7.cloned.1.call-start = ((), (), s32[]{:S(2)}) async-start(), calls=%async_computation.5 | async-start | bytes 18874368 | tf_op jit(solution)/shard_map/all_gather | solution.py:103
  16.1 5.6 copy-start.7
  18.6 237.1 %all-gather.9.cloned.1.call-start = ((), (), s32[]{:S(2)}) async-start(), calls=%async_computation.6 | async-start | bytes 9437184 | tf_op jit(solution)/shard_map/all_gather | solution.py:103
  18.7 26.3 %collective-permute-start.1 = (bf16[1,256,2048]{2,1,0:T(8,128)(2,1)S(1)}, bf16[1,256,2048]{2,1,0:T(8,128)(2,1)}, u32[]{:S(2)}, u32[]{:S(2)}) collective-permute-start(bf16[1,256,2048]{2,1,0:T(8,128)(2,1)S(1)} %copy-done.4), channel_id=1, source_target_pairs={{0,8},{8,0},{16,24},{24,16},{1,9},{9,1},{17,25},{25,17},{2,10},{10... | collective-permute-start | bytes 3145736 | tf_op jit(solution)/shard_map/ppermute | solution.py:68
  21.7 25.7 %collective-permute-start = (bf16[1,256,2048]{2,1,0:T(8,128)(2,1)S(1)}, bf16[1,256,2048]{2,1,0:T(8,128)(2,1)}, u32[]{:S(2)}, u32[]{:S(2)}) collective-permute-start(bf16[1,256,2048]{2,1,0:T(8,128)(2,1)S(1)} %copy-done.7), channel_id=1, source_target_pairs={{0,16},{8,24},{16,0},{24,8},{1,17},{9,25},{17,1},{25,9},{2,18},{10... | collective-permute-start | bytes 3145736 | tf_op jit(solution)/shard_map/ppermute | solution.py:68
  52.9 47.1 %collective-permute-start.3 = (bf16[2,256,2048]{2,1,0:T(8,128)(2,1)}, bf16[2,256,2048]{2,1,0:T(8,128)(2,1)}, u32[]{:S(2)}, u32[]{:S(2)}) collective-permute-start(bf16[2,256,2048]{2,1,0:T(8,128)(2,1)} %maximum_select_fusion.6), channel_id=1, source_target_pairs={{0,16},{8,24},{16,0},{24,8},{1,17},{9,25},{17,1},{25,9},{2,18},{10... | collective-permute-start | bytes 6291464 | tf_op jit(solution)/shard_map/ppermute | solution.py:68
  57.6 46.6 %collective-permute-start.2 = (bf16[2,256,2048]{2,1,0:T(8,128)(2,1)}, bf16[2,256,2048]{2,1,0:T(8,128)(2,1)}, u32[]{:S(2)}, u32[]{:S(2)}) collective-permute-start(bf16[2,256,2048]{2,1,0:T(8,128)(2,1)} %maximum_select_fusion.5), channel_id=1, source_target_pairs={{0,8},{8,0},{16,24},{24,16},{1,9},{9,1},{17,25},{25,17},{2,10},{10... | collective-permute-start | bytes 6291464 | tf_op jit(solution)/shard_map/ppermute | solution.py:68
  107.3 7.4 %copy-start.2 = (bf16[2,2,256,2048]{3,2,1,0:T(8,128)(2,1)}, bf16[2,2,256,2048]{3,2,1,0:T(8,128)(2,1)S(1)}, u32[]{:S(2)}) copy-start(bf16[2,2,256,2048]{3,2,1,0:T(8,128)(2,1)S(1)} %copy.78) | copy-start | bytes 12582916
  117.1 8.9 %copy-start.15 = (bf16[256,1536]{1,0:T(8,128)(2,1)S(1)}, bf16[256,1536]{1,0:T(8,128)(2,1)}, u32[]{:S(2)}) copy-start(bf16[256,1536]{1,0:T(8,128)(2,1)} %copy.82) | copy-start | bytes 2359300
  127.2 297.7 %reduce-scatter.3.cloned.1.call-start = ((), (), s32[]{:S(2)}) async-start(), calls=%async_computation.7 | async-start | bytes 18874368 | tf_op jit(solution)/shard_map/reduce_scatter | solution.py:107
  234.0 310.4 %reduce-scatter.5.cloned.1.call-start = ((), (), s32[]{:S(2)}) async-start(), calls=%async_computation.8 | async-start | bytes 9437184 | tf_op jit(solution)/shard_map/reduce_scatter | solution.py:107
  273.7 44.3 %copy-start.3 = (bf16[2,2,256,2048]{3,2,1,0:T(8,128)(2,1)S(1)}, bf16[2,2,256,2048]{3,2,1,0:T(8,128)(2,1)}, u32[]{:S(2)}) copy-start(bf16[2,2,256,2048]{3,2,1,0:T(8,128)(2,1)} %copy-done.2) | copy-start | bytes 12582916
  353.1 53.1 %all-to-all-start = ((bf16[4,256,2048]{2,1,0:T(8,128)(2,1)}), bf16[4,256,2048]{2,1,0:T(8,128)(2,1)}, u32[]{:S(2)}, u32[]{:S(2)}) async-start(bf16[4,256,2048]{2,1,0:T(8,128)(2,1)} %bitcast.183), calls=%async_computation | async-start | bytes 8388608 | tf_op jit(solution)/shard_map/all_to_all | solution.py:51
  406.2 6.2 %copy-start.24 = (f32[1,2048]{1,0:T(1,128)S(1)}, f32[1,2048]{1,0:T(1,128)}, u32[]{:S(2)}) copy-start(f32[1,2048]{1,0:T(1,128)} %get-tuple-element.34) | copy-start | bytes 24580
  406.2 6.9 %copy-start.23 = (f32[1,2048]{1,0:T(1,128)S(1)}, f32[1,2048]{1,0:T(1,128)}, u32[]{:S(2)}) copy-start(f32[1,2048]{1,0:T(1,128)} %get-tuple-element.35) | copy-start | bytes 24580
  406.2 53.8 %all-to-all-start.1 = ((bf16[4,256,2048]{2,1,0:T(8,128)(2,1)}), bf16[4,256,2048]{2,1,0:T(8,128)(2,1)}, u32[]{:S(2)}, u32[]{:S(2)}) async-start(bf16[4,256,2048]{2,1,0:T(8,128)(2,1)} %bitcast.182), calls=%async_computation.1 | async-start | bytes 8388608 | tf_op jit(solution)/shard_map/all_to_all | solution.py:51
  411.2 186.5 %all-gather.11.cloned.1.call-start = ((), (), s32[]{:S(2)}) async-start(), calls=%async_computation.9 | async-start | bytes 5242880 | tf_op jit(solution)/shard_map/all_gather | solution.py:80
  424.9 6.4 %copy-start.14 = (bf16[1024,1536]{1,0:T(8,128)(2,1)S(1)}, bf16[1024,1536]{1,0:T(8,128)(2,1)}, u32[]{:S(2)}) copy-start(bf16[1024,1536]{1,0:T(8,128)(2,1)} %get-tuple-element.30.right_ref.one_ref) | copy-start | bytes 9437188
  428.4 6.7 %copy-start.12 = (bf16[1,256,2048]{2,1,0:T(8,128)(2,1)}, bf16[1,256,2048]{2,1,0:T(8,128)(2,1)S(1)}, u32[]{:S(2)}) copy-start(bf16[1,256,2048]{2,1,0:T(8,128)(2,1)S(1)} %get-tuple-element.39) | copy-start | bytes 3145732
  428.4 52.6 %collective-permute-start.11 = (bf16[1,256,2048]{2,1,0:T(8,128)(2,1)S(1)}, bf16[1,256,2048]{2,1,0:T(8,128)(2,1)}, u32[]{:S(2)}, u32[]{:S(2)}) collective-permute-start(bf16[1,256,2048]{2,1,0:T(8,128)(2,1)S(1)} %get-tuple-element.39), channel_id=1, source_target_pairs={{0,16},{8,24},{16,0},{24,8},{1,17},{9,25},{17,1},{25,9},{2,18},{10... | collective-permute-start | bytes 3145736 | tf_op jit(solution)/shard_map/ppermute | solution.py:68
  429.9 53.7 %collective-permute-start.10 = (bf16[1,256,2048]{2,1,0:T(8,128)(2,1)}, bf16[1,256,2048]{2,1,0:T(8,128)(2,1)}, u32[]{:S(2)}, u32[]{:S(2)}) collective-permute-start(bf16[1,256,2048]{2,1,0:T(8,128)(2,1)} %get-tuple-element.40), channel_id=1, source_target_pairs={{0,8},{8,0},{16,24},{24,16},{1,9},{9,1},{17,25},{25,17},{2,10},{10... | collective-permute-start | bytes 3145736 | tf_op jit(solution)/shard_map/ppermute | solution.py:68
  486.8 46.7 %collective-permute-start.12 = (bf16[2,256,2048]{2,1,0:T(8,128)(2,1)S(1)}, bf16[2,256,2048]{2,1,0:T(8,128)(2,1)S(1)}, u32[]{:S(2)}, u32[]{:S(2)}) collective-permute-start(bf16[2,256,2048]{2,1,0:T(8,128)(2,1)S(1)} %maximum_select_fusion.9), channel_id=1, source_target_pairs={{0,16},{8,24},{16,0},{24,8},{1,17},{9,25},{17,1},{25,9},{2,18},{10... | collective-permute-start | bytes 6291464 | tf_op jit(solution)/shard_map/ppermute | solution.py:68
  491.4 46.5 %collective-permute-start.13 = (bf16[2,256,2048]{2,1,0:T(8,128)(2,1)S(1)}, bf16[2,256,2048]{2,1,0:T(8,128)(2,1)S(1)}, u32[]{:S(2)}, u32[]{:S(2)}) collective-permute-start(bf16[2,256,2048]{2,1,0:T(8,128)(2,1)S(1)} %maximum_select_fusion.10), channel_id=1, source_target_pairs={{0,8},{8,0},{16,24},{24,16},{1,9},{9,1},{17,25},{25,17},{2,10},{10... | collective-permute-start | bytes 6291464 | tf_op jit(solution)/shard_map/ppermute | solution.py:68
  551.7 1.3 collective-permute-start.4
  553.1 2.7 collective-permute-start.5
  555.7 5.5 collective-permute-start.6
  556.4 6.2 %collective-permute-start.8 = (f32[1,2560]{1,0:T(1,128)S(1)}, f32[1,2560]{1,0:T(1,128)S(1)}, u32[]{:S(2)}, u32[]{:S(2)}) collective-permute-start(f32[1,2560]{1,0:T(1,128)S(1)} %fusion.16), channel_id=1, source_target_pairs={{0,2},{1,3},{2,4},{3,5},{8,10},{9,11},{10,12},{11,13},{16,18},{17,... | collective-permute-start | bytes 30728 | tf_op jit(solution)/shard_map/ppermute | solution.py:94
  562.6 6.5 %collective-permute-start.7 = (f32[1,2560]{1,0:T(1,128)S(1)}, f32[1,2560]{1,0:T(1,128)S(1)}, u32[]{:S(2)}, u32[]{:S(2)}) collective-permute-start(f32[1,2560]{1,0:T(1,128)S(1)} %get-tuple-element.57), channel_id=1, source_target_pairs={{2,0},{3,1},{4,2},{5,3},{6,4},{7,5},{10,8},{11,9},{12,10},{13,11},... | collective-permute-start | bytes 30728 | tf_op jit(solution)/shard_map/ppermute | solution.py:94
  563.9 6.6 %collective-permute-start.9 = (f32[1,2560]{1,0:T(1,128)S(1)}, f32[1,2560]{1,0:T(1,128)S(1)}, u32[]{:S(2)}, u32[]{:S(2)}) collective-permute-start(f32[1,2560]{1,0:T(1,128)S(1)} %get-tuple-element.58), channel_id=1, source_target_pairs={{0,2},{1,3},{2,4},{3,5},{4,6},{5,7},{8,10},{9,11},{10,12},{11,13},... | collective-permute-start | bytes 30728 | tf_op jit(solution)/shard_map/ppermute | solution.py:94
  580.5 27.9 %copy-start.25 = (f32[256]{0:T(256)}, f32[256]{0:T(256)S(1)}, u32[]{:S(2)}) copy-start(f32[256]{0:T(256)S(1)} %get-tuple-element.92) | copy-start | bytes 3076
  580.5 9.9 %copy-start.18 = (bf16[2,256,2048]{2,1,0:T(8,128)(2,1)S(1)}, bf16[2,256,2048]{2,1,0:T(8,128)(2,1)}, u32[]{:S(2)}) copy-start(bf16[2,256,2048]{2,1,0:T(8,128)(2,1)} %copy-done.17) | copy-start | bytes 6291460
  (22 other events, 67.2 us)
Sparse Core Ops, SparseCore 0:
  18.7 154.4 all-gather.6
  175.4 80.2 all-gather.8
  258.1 166.7 reduce-scatter.2
  427.7 87.9 reduce-scatter.4
  546.8 50.9 all-gather.10

commit v4 on v3

--- a/solution.py
+++ b/solution.py
@@ -78,6 +78,28 @@
 
 def seq_all(block):
     return lax.all_gather(block, "seq", axis=0)
+
+
+def seq_sum_halves(blocks):
+    me, count = lax.axis_index("seq"), lax.axis_size("seq")
+    bits = list(range(count.bit_length() - 1))
+    half = blocks.shape[-1] // 2
+    orders = (bits, bits[::-1])
+    shape = (2,) * len(bits) + blocks.shape[1:-1] + (half,)
+    parts = [blocks[..., :half].reshape(shape), blocks[..., half:].reshape(shape)]
+    left = [list(bits[::-1]), list(bits[::-1])]
+    for step in bits:
+        got = []
+        for i, order in enumerate(orders):
+            mine, axis = (me >> order[step]) % 2, left[i].index(order[step])
+            pairs = [(j, j ^ (1 << order[step])) for j in range(count)]
+            got.append(lax.ppermute(pick(parts[i], 1 - mine, axis), "seq", pairs))
+        for i, order in enumerate(orders):
+            mine, axis = (me >> order[step]) % 2, left[i].index(order[step])
+            left[i].remove(order[step])
+            total = pick(parts[i], mine, axis).astype(F32) + behind(got[i], got[1 - i]).astype(F32)
+            parts[i] = total.astype(blocks.dtype) if left[i] else total
+    return jnp.concatenate(parts, axis=-1)
 
 
 def seq_sum(blocks):
@@ -219,6 +241,51 @@
     )(qkv, grad, cosine, sine, opening, *before, *after)
 
 
+def pick_kernel(me_ref, *refs):
+    *pieces, second_ref, out_ref = refs
+    step = pl.program_id(0)
+    unit = pieces[0].shape[1]
+
+    @pl.when(step < 2)
+    def _():
+        for i, piece in enumerate(pieces):
+            out_ref[:, i * unit : (i + 1) * unit] = piece[...]
+
+    @pl.when(step >= 2)
+    def _():
+        out_ref[...] = second_ref[...]
+
+
+def pick_two(first, second, unit):
+    seqs = lax.axis_size("seq")
+    rows, columns = first.shape[0], first.shape[1] // seqs
+    count = columns // unit // 2
+    me = lax.axis_index("seq").astype(jnp.int32).reshape(1)
+
+    def piece(i):
+        return pl.BlockSpec(
+            (rows, unit), lambda j, me: (0, (jnp.minimum(j, 1) * count + i) * seqs + me[0])
+        )
+
+    return pl.pallas_call(
+        pick_kernel,
+        grid_spec=pltpu.PrefetchScalarGridSpec(
+            num_scalar_prefetch=1,
+            grid=(4,),
+            in_specs=[piece(i) for i in range(count)]
+            + [
+                pl.BlockSpec(
+                    (unit, columns // 2), lambda j, me: (me[0], jnp.maximum(j - 2, 0))
+                )
+            ],
+            out_specs=pl.BlockSpec((rows, columns // 2), lambda j, me: (0, j)),
+        ),
+        out_shape=jax.ShapeDtypeStruct((rows, 2 * columns), BF),
+        compiler_params=params(),
+        cost_estimate=cost(0, 8 * rows * columns),
+    )(me, *([first] * count), second)
+
+
 def norm_kernel(in_ref, gain_ref, shift_ref, out_ref, mean_ref, std_ref):
     value = in_ref[...].astype(F32)
     mean = jnp.mean(value, axis=-1, keepdims=True)
@@ -658,9 +725,9 @@
         bias_qkv = pick(bias_qkv.reshape(seqs, heads * 3 * HEAD_DIM), me)
     bias_qkv = by_pairs(bias_qkv.reshape(3 * head_cols), heads)
 
-    joined = rows_here == unit and hidden_cols == width and unit % 128 == 0
+    joined = rows_here == unit and hidden_cols == width and unit % 128 == 0 and shards % 2 == 0
     if joined:
-        fc1 = fc2 = fsdp_gather(jnp.concatenate([fc1_here, fc2_here], axis=1))
+        fc1 = fc2 = fsdp_gather(pick_two(w_fc1, w_fc2, unit))
         begin = hidden_cols
     else:
         fc1, fc2, begin = fsdp_gather(fc1_here), fsdp_gather(fc2_here), 0
@@ -704,22 +771,25 @@
     qkv = product(normed, both, bias_qkv, [grad_mixed])
     tables = (cosine, sine, opening[None])
     mixed, grad_qkv = attention(qkv, grad_mixed, *tables, 0, heads // 2)
+    partial = output_terms(active, fc2, begin, mixed, out_w, [grad_qkv])
+    result = seq_sum_halves(partial.reshape(seqs, tok, width))
+    grad_partial, sum_gain, sum_shift = normed_terms(
+        grad_qkv, both, grad_hidden, fc1, rows_all, mean, inv_std, [partial]
+    )
+    grad_normed = seq_sum_halves(grad_partial.reshape(seqs, tok, width))
     out_grad = mm(mixed, grad_rows, 0, 0).astype(BF)
     if strided:
         out_grad = out_grad.reshape(shards, each * HEAD_DIM, width)
-        all_qkv = two_terms(normed, grad_qkv, rows_here, out_grad, out_cut, list(range(shards)))
+        every = list(range(shards))
+        all_qkv = two_terms(
+            normed, grad_qkv, rows_here, out_grad, out_cut, every, None, [grad_partial]
+        )
         all_qkv = all_qkv.reshape(width, -1)
     else:
         spread = put(jnp.zeros((seqs, head_cols, width), BF), out_grad, me)
         part_out = fsdp_sum(spread.reshape(seqs * head_cols, width))
         all_qkv = mm(normed, grad_qkv, 0, 0).astype(BF)
     part_qkv = fsdp_sum(all_qkv)
-    partial = output_terms(active, fc2, begin, mixed, out_w, [all_qkv])
-    result = seq_sum(partial.reshape(seqs, tok, width))
-    grad_partial, sum_gain, sum_shift = normed_terms(
-        grad_qkv, both, grad_hidden, fc1, rows_all, mean, inv_std, [partial]
-    )
-    grad_normed = seq_sum(grad_partial.reshape(seqs, tok, width))
     part_fc2 = behind(part_fc2, result)
     if joined:
         whole_fc2, whole_fc1 = seq_gather_two(part_fc2, part_fc1)

time: 625 us -> 612 us (0.979)
  waiting for transfers between devices: 207 us -> 177 us
  between operations: 32.3 us -> 42.6 us
    all_to_all x2 -> x0, waiting for transfers between devices: 49.8 us -> none  [seq_exchange(): return lax.all_to_all(blocks, 'seq', split_axis=0, concat_axis=0)]
    ppermute x0 -> x8, waiting for transfers between devices: none -> 39 us  [seq_sum_halves(): got.append(lax.ppermute(pick(parts[i], 1 - mine, axis), 'seq', pairs))]
    ppermute x8, waiting for transfers between devices: 86.9 us -> 72.2 us  [seq_gather_two(): got.append(lax.ppermute(whole, 'seq', pairs))]
    ppermute x0 -> x8, starting transfers between devices: none -> 12 us  [seq_sum_halves(): got.append(lax.ppermute(pick(parts[i], 1 - mine, axis), 'seq', pairs))]
    all_to_all x2 -> x0, starting transfers between devices: 9.85 us -> none  [seq_exchange(): return lax.all_to_all(blocks, 'seq', split_axis=0, concat_axis=0)]
    unnamed x95 -> x99, local copies, waits for them, and re-layouts: 25.3 us -> 18.1 us
    reduce_sum x2 -> x0, other arithmetic: 6.44 us -> none  [seq_sum(): return jnp.sum(seq_exchange(blocks).astype(F32), axis=0)]
    slice x13 -> x21, local copies, waits for them, and re-layouts: 12.1 us -> 18.3 us  [behind(): first = lax.slice(other, (0,) * other.ndim, (1,) * other.ndim).reshape(())]
  transfers between devices with their start and end apart: 21 -> 27, of which waited for: 16 -> 18; matrix products, arithmetic and copies ran while one was open for 15% -> 17% of each run, Pallas kernels for 31% -> 31%
where the time goes in v4:
time: 612 us; the launch traced here: 604 us
  Pallas kernels  200 us (33%)
  waiting for transfers between devices  177 us (29%)
  local copies, waits for them, and re-layouts  56.9 us (9%)
  other arithmetic  56 us (9%)
  between operations  42.6 us (7%)
  starting transfers between devices  39.2 us (6%)
  blocking collectives  27.7 us (5%)
    ppermute x8, waiting for transfers between devices, seq_gather_two(): got.append(lax.ppermute(whole, 'seq', pairs))  72.2 us
    all_gather x2, waiting for transfers between devices, fsdp_gather(): return lax.all_gather(block, 'fsdp', axis=0, tiled=True)  59.1 us
    pallas_call x1, Pallas kernels, attention(): pl.pallas_call(functools.partial(attention_kernel, min(256, length), HEAD...  44.6 us
    ppermute x8, waiting for transfers between devices, seq_sum_halves(): got.append(lax.ppermute(pick(parts[i], 1 - mine, axis), 'seq', pairs))  39 us
    pallas_call x2, Pallas kernels, row_terms(): pl.pallas_call(rows_kernel, grid=(count,), in_specs=[pl.BlockSpec((rows,...  28.4 us
    pallas_call x1, Pallas kernels, normed_terms(): pl.pallas_call(normed_kernel, grid=(columns // cut,), in_specs=[whole(one...  23.4 us
    all_gather x1, blocking collectives, per_device(): small = lax.all_gather(small, 'fsdp', axis=0, tiled=True).astype(F32)  20.4 us
    slice x21, local copies, waits for them, and re-layouts, behind(): first = lax.slice(other, (0,) * other.ndim, (1,) * other.ndim).reshape(())  18.3 us
  transfers between devices with their start and end apart: 27, of which 18 were waited for; matrix products, arithmetic and copies ran while one was open for 17% of the time, Pallas kernels for 31%

profile of v4, /device:TPU:0, one launch (start us, length us, event | category | flops | bytes accessed | tf_op | source)
XLA Modules:
  0.0 603.8 jit_solution(10721856285285343161)
XLA Ops:
  7.2 4.4 shard_map.221
  17.3 21.7 %collective-permute-done.1 = bf16[1,256,2048]{2,1,0:T(8,128)(2,1)} collective-permute-done((bf16[1,256,2048]{2,1,0:T(8,128)(2,1)S(1)}, bf16[1,256,2048]{2,1,0:T(8,128)(2,1)}, u32[]{:S(2)}, u32[]{:S(2)}) %collective-permute-start.1) | collective-permute-done | bytes 1048608 | tf_op jit(solution)/shard_map/ppermute | solution.py:68
  54.6 20.4 %all-gather.2 = bf16[8,1,2816]{2,1,0:T(2,128)(2,1)S(1)} all-gather(bf16[1,1,2816]{2,1,0:T(2,128)(2,1)S(1)} %reshape.736), channel_id=2, replica_groups=mesh['seq'=4,'fsdp'=8] {'fsdp'}, dimensions={0}, use_global_device_ids=true | all-gather | bytes 50688 | tf_op jit(solution)/shard_map/all_gather | solution.py:716
  75.0 4.7 copy.84
  87.9 6.2 %collective-permute-done.3 = bf16[2,256,2048]{2,1,0:T(8,128)(2,1)} collective-permute-done((bf16[2,256,2048]{2,1,0:T(8,128)(2,1)}, bf16[2,256,2048]{2,1,0:T(8,128)(2,1)}, u32[]{:S(2)}, u32[]{:S(2)}) %collective-permute-start.3) | collective-permute-done | bytes 2097184 | tf_op jit(solution)/shard_map/ppermute | solution.py:68
  111.1 6.3 %shard_map.220 = (bf16[1024,2048]{1,0:T(8,128)(2,1)}, f32[1024,1]{1,0:T(8,128)}, f32[1024,1]{1,0:T(8,128)}) custom-call(bf16[1024,2048]{1,0:T(8,128)(2,1)} %bitcast.221, f32[1,2048]{1,0:T(1,128)} %bitcast.260, f32[1,2048]{1,0:T(1,128)} %bitcast.261), custom_call_target="tpu_custom_call" | custom-call | flops 20971520 | bytes 8388608 | tf_op jit(solution)/shard_map/pallas_call | solution.py:305
  122.1 44.2 %all-gather.7.cloned.1.call-done.right_ref.second_ref = bf16[2048,4096]{1,0:T(8,128)(2,1)} async-done(((bf16[256,4096]{1,0:T(8,128)(2,1)}), bf16[2048,4096]{1,0:T(8,128)(2,1)}) %all-gather.7.cloned.1.call-update) | async-done | bytes 16777232 | tf_op jit(solution)/shard_map/all_gather | solution.py:125
  166.3 17.9 %shard_map.222 = (bf16[1024,2048]{1,0:T(8,128)(2,1)}, bf16[1024,2048]{1,0:T(8,128)(2,1)}) custom-call(bf16[1024,2048]{1,0:T(8,128)(2,1)} %get-tuple-element.24.left_ref, bf16[2048,4096]{1,0:T(8,128)(2,1)} %all-gather.7.cloned.1.call-done.right_ref.second_ref, f32[1,2048]{1,0:T(1,128)} %bitcast.267), custom_call_target="tpu_custom_call" | custom-call | flops 8589934592 | bytes 16777216 | tf_op jit(solution)/shard_map/pallas_call | solution.py:373
  184.2 14.2 %shard_map.223.refs_0_ = bf16[2048,4096]{1,0:T(8,128)(2,1)} custom-call(bf16[1024,2048]{1,0:T(8,128)(2,1)} %get-tuple-element.25.left_ref, bf16[1024,2048]{1,0:T(8,128)(2,1)} %bitcast.214), custom_call_target="tpu_custom_call" | custom-call | flops 8589934592 | bytes 8388608 | tf_op jit(solution)/shard_map/pallas_call | solution.py:431
  198.3 14.4 %shard_map.224.right_ref.two_ref = bf16[1024,2048]{1,0:T(8,128)(2,1)} custom-call(bf16[1024,2048]{1,0:T(8,128)(2,1)} %bitcast.215, bf16[2048,4096]{1,0:T(8,128)(2,1)} %all-gather.7.cloned.1.call-done.right_ref.second_ref, bf16[1024,2048]{1,0:T(8,128)(2,1)} %get-tuple-element.26.slope_ref, bf16[2048,4096]{1,0:T(8,128)(2,1)} %shard_map.223.refs_0_), custom_call_target="tpu_custom_call" | custom-call | flops 8589934592 | bytes 12582912 | tf_op jit(solution)/shard_map/pallas_call | solution.py:525
  212.7 14.2 %shard_map.225.refs_0_ = bf16[2048,4096]{1,0:T(8,128)(2,1)} custom-call(bf16[1024,2048]{1,0:T(8,128)(2,1)} %get-tuple-element.24.left_ref, bf16[1024,2048]{1,0:T(8,128)(2,1)} %shard_map.224.right_ref.two_ref, bf16[2048,4096]{1,0:T(8,128)(2,1)} %shard_map.223.refs_0_), custom_call_target="tpu_custom_call", output_to_operand_aliasing={{}: (2, {})} | custom-call | flops 8589934592 | bytes 8388608 | tf_op jit(solution)/shard_map/pallas_call | solution.py:431
  233.9 14.9 %all-gather.9.cloned.1.call-done.both_ref.right_ref.first_ref = bf16[2048,2048]{1,0:T(8,128)(2,1)} async-done(((bf16[256,2048]{1,0:T(8,128)(2,1)}), bf16[2048,2048]{1,0:T(8,128)(2,1)}) %all-gather.9.cloned.1.call-update) | async-done | bytes 8388624 | tf_op jit(solution)/shard_map/all_gather | solution.py:125
  248.8 6.4 %shard_map.226 = (bf16[512,2048]{1,0:T(8,128)(2,1)}, bf16[1024,512]{1,0:T(8,128)(2,1)}) custom-call(bf16[1024,2048]{1,0:T(8,128)(2,1)} %bitcast.216, bf16[2048,2048]{1,0:T(8,128)(2,1)} %all-gather.9.cloned.1.call-done.both_ref.right_ref.first_ref, bf16[2048,4096]{1,0:T(8,128)(2,1)} %shard_map.225.refs_0_), custom_call_target="tpu_custom_call" | custom-call | flops 2147483648 | bytes 8388608 | tf_op jit(solution)/shard_map/pallas_call | solution.py:338
  255.2 11.6 %shard_map.227.qkv_ref = f32[1024,1536]{1,0:T(8,128)} custom-call(bf16[1024,2048]{1,0:T(8,128)(2,1)} %get-tuple-element.24.left_ref, bf16[2048,2048]{1,0:T(8,128)(2,1)} %all-gather.9.cloned.1.call-done.both_ref.right_ref.first_ref, f32[1,1536]{1,0:T(1,128)} %broadcast_in_dim_reshape.12.bias_ref, bf16[1024,512]{1,0:T(8,128)(2,1)} %get-tuple-element.27.refs_0_.grad_ref), custom_call_target="tpu_custom_call" | custom-call | flops 6442450944 | bytes 14680064 | tf_op jit(solution)/shard_map/pallas_call | solution.py:499
  266.8 44.6 %shard_map.228 = (bf16[1024,512]{1,0:T(8,128)(2,1)}, bf16[1024,1536]{1,0:T(8,128)(2,1)}) custom-call(f32[1024,1536]{1,0:T(8,128)} %shard_map.227.qkv_ref, bf16[1024,512]{1,0:T(8,128)(2,1)} %get-tuple-element.27.refs_0_.grad_ref, f32[1024,128]{1,0:T(8,128)} %concatenate.121.cos_ref, f32[1024,128]{1,0:T(8,128)} %concatenate.122.sin_ref, s32[1,1024]{1,0:T(1,128)} %bitcast.262), custom_call_target="tpu_custom_call" | custom-call | flops 12884901888 | bytes 12582912 | tf_op jit(solution)/shard_map/pallas_call | solution.py:222
  311.4 4.9 convolution_convert_fusion
  316.3 15.8 %shard_map.229.refs_0_ = bf16[1024,2048]{1,0:T(8,128)(2,1)} custom-call(bf16[1024,2048]{1,0:T(8,128)(2,1)} %get-tuple-element.25.left_ref, bf16[2048,4096]{1,0:T(8,128)(2,1)} %all-gather.7.cloned.1.call-done.right_ref.second_ref, bf16[1024,512]{1,0:T(8,128)(2,1)} %get-tuple-element.28.second_ref, bf16[512,2048]{1,0:T(8,128)(2,1)} %get-tuple-element.29.weight_ref, ...), custom_call_target="tpu_custom_call" | custom-call | flops 10737418240 | bytes 12582912 | tf_op jit(solution)/shard_map/pallas_call | solution.py:550
  332.1 23.4 %shard_map.230 = (bf16[1024,2048]{1,0:T(8,128)(2,1)}, f32[1,2048]{1,0:T(1,128)}, f32[1,2048]{1,0:T(1,128)}) custom-call(bf16[1024,1536]{1,0:T(8,128)(2,1)} %get-tuple-element.30.refs_0_.one_ref.right_ref, bf16[2048,2048]{1,0:T(8,128)(2,1)} %all-gather.9.cloned.1.call-done.both_ref.right_ref.first_ref, bf16[1024,2048]{1,0:T(8,128)(2,1)} %shard_map.224.right_ref.two_ref, ...), custom_call_target="tpu_custom_call" | custom-call | flops 15032385536 | bytes 16777216 | tf_op jit(solution)/shard_map/pallas_call | solution.py:585
  356.0 13.6 %shard_map.231 = bf16[8,256,2048]{2,1,0:T(8,128)(2,1)} custom-call(s32[8]{0:T(128)} %iota.18.index_ref, bf16[1024,2048]{1,0:T(8,128)(2,1)} %get-tuple-element.24.left_ref, bf16[1024,1536]{1,0:T(8,128)(2,1)} %get-tuple-element.30.refs_0_.one_ref.right_ref, bf16[8,64,2048]{2,1,0:T(8,128)(2,1)} %bitcast.269, bf16[1024,2048]{1,0:T(8,128)(2,1)} %get-tuple-element.33.refs_0_), custom_call_target="tpu_custom_call" | custom-call | flops 6442450944 | bytes 6291456 | tf_op jit(solution)/shard_map/pallas_call | solution.py:471
  381.1 19.0 %collective-permute-done.4 = bf16[2,256,1024]{2,1,0:T(8,128)(2,1)S(1)} collective-permute-done((bf16[2,256,1024]{2,1,0:T(8,128)(2,1)S(1)}, bf16[2,256,1024]{2,1,0:T(8,128)(2,1)S(1)}, u32[]{:S(2)}, u32[]{:S(2)}) %collective-permute-start.4) | collective-permute-done | bytes 1048608 | tf_op jit(solution)/shard_map/ppermute | solution.py:96
  408.1 14.4 %collective-permute-done.8 = bf16[2,256,1024]{2,1,0:T(8,128)(2,1)S(1)} collective-permute-done((bf16[2,256,1024]{2,1,0:T(8,128)(2,1)S(1)}, bf16[2,256,1024]{2,1,0:T(8,128)(2,1)S(1)}, u32[]{:S(2)}, u32[]{:S(2)}) %collective-permute-start.8) | collective-permute-done | bytes 1048608 | tf_op jit(solution)/shard_map/ppermute | solution.py:96
  430.6 5.2 collective-permute-done.6
  461.9 5.2 collective-permute-done.19
  487.5 31.8 %collective-permute-done.20 = bf16[2,256,2048]{2,1,0:T(8,128)(2,1)S(1)} collective-permute-done((bf16[2,256,2048]{2,1,0:T(8,128)(2,1)S(1)}, bf16[2,256,2048]{2,1,0:T(8,128)(2,1)S(1)}, u32[]{:S(2)}, u32[]{:S(2)}) %collective-permute-start.20) | collective-permute-done | bytes 2097184 | tf_op jit(solution)/shard_map/ppermute | solution.py:68
  521.2 5.5 collective-permute-done.21
  535.6 4.0 convert_reduce_fusion.2
  544.5 5.0 collective-permute-start.16
  552.0 5.2 collective-permute-start.17
  558.6 7.3 %all_to_all.5 = f32[4,1,2560]{2,1,0:T(1,128)S(1)} all-to-all(f32[4,1,2560]{2,1,0:T(1,128)S(1)} %broadcast_in_dim.111), channel_id=1, replica_groups=mesh['seq'=4,'fsdp'=8] {'seq'}, dimensions={0} | all-to-all | bytes 81920 | tf_op jit(solution)/shard_map/all_to_all | solution.py:51
  567.7 7.4 %shard_map.233 = f32[256,8192]{1,0:T(8,128)} custom-call(bf16[4,256,2048]{2,1,0:T(8,128)(2,1)} %bitcast.220), custom_call_target="tpu_custom_call" | custom-call | bytes 12582912 | tf_op jit(solution)/shard_map/pallas_call | solution.py:616
  579.9 4.7 bitcast_convert_fusion
  587.1 5.5 shard_map.232
  (277 shorter events, 137.0 us)
Async XLA Ops:
  7.2 77.0 %copy-start = (bf16[256,2048]{1,0:T(8,128)(2,1)S(1)}, bf16[256,2048]{1,0:T(8,128)(2,1)}, u32[]{:S(2)}) copy-start(bf16[256,2048]{1,0:T(8,128)(2,1)} %param.19) | copy-start | bytes 3145732
  7.2 159.1 %all-gather.7.cloned.1.call-start = ((), (), s32[]{:S(2)}) async-start(), calls=%async_computation.3 | async-start | bytes 18874368 | tf_op jit(solution)/shard_map/all_gather | solution.py:125
  11.7 237.1 %all-gather.9.cloned.1.call-start = ((), (), s32[]{:S(2)}) async-start(), calls=%async_computation.4 | async-start | bytes 9437184 | tf_op jit(solution)/shard_map/all_gather | solution.py:125
  12.9 26.2 %collective-permute-start.1 = (bf16[1,256,2048]{2,1,0:T(8,128)(2,1)S(1)}, bf16[1,256,2048]{2,1,0:T(8,128)(2,1)}, u32[]{:S(2)}, u32[]{:S(2)}) collective-permute-start(bf16[1,256,2048]{2,1,0:T(8,128)(2,1)S(1)} %copy-done.5), channel_id=1, source_target_pairs={{0,8},{8,0},{16,24},{24,16},{1,9},{9,1},{17,25},{25,17},{2,10},{10... | collective-permute-start | bytes 3145736 | tf_op jit(solution)/shard_map/ppermute | solution.py:68
  15.8 25.7 %collective-permute-start = (bf16[1,256,2048]{2,1,0:T(8,128)(2,1)S(1)}, bf16[1,256,2048]{2,1,0:T(8,128)(2,1)}, u32[]{:S(2)}, u32[]{:S(2)}) collective-permute-start(bf16[1,256,2048]{2,1,0:T(8,128)(2,1)S(1)} %copy-done.7), channel_id=1, source_target_pairs={{0,16},{8,24},{16,0},{24,8},{1,17},{9,25},{17,1},{25,9},{2,18},{10... | collective-permute-start | bytes 3145736 | tf_op jit(solution)/shard_map/ppermute | solution.py:68
  47.0 47.1 %collective-permute-start.3 = (bf16[2,256,2048]{2,1,0:T(8,128)(2,1)}, bf16[2,256,2048]{2,1,0:T(8,128)(2,1)}, u32[]{:S(2)}, u32[]{:S(2)}) collective-permute-start(bf16[2,256,2048]{2,1,0:T(8,128)(2,1)} %maximum_select_fusion.6), channel_id=1, source_target_pairs={{0,16},{8,24},{16,0},{24,8},{1,17},{9,25},{17,1},{25,9},{2,18},{10... | collective-permute-start | bytes 6291464 | tf_op jit(solution)/shard_map/ppermute | solution.py:68
  51.9 46.4 %collective-permute-start.2 = (bf16[2,256,2048]{2,1,0:T(8,128)(2,1)}, bf16[2,256,2048]{2,1,0:T(8,128)(2,1)}, u32[]{:S(2)}, u32[]{:S(2)}) collective-permute-start(bf16[2,256,2048]{2,1,0:T(8,128)(2,1)} %maximum_select_fusion.5), channel_id=1, source_target_pairs={{0,8},{8,0},{16,24},{24,16},{1,9},{9,1},{17,25},{25,17},{2,10},{10... | collective-permute-start | bytes 6291464 | tf_op jit(solution)/shard_map/ppermute | solution.py:68
  121.2 318.6 %reduce-scatter.3.cloned.1.call-start = ((), (), s32[]{:S(2)}) async-start(), calls=%async_computation.5 | async-start | bytes 18874368 | tf_op jit(solution)/shard_map/reduce_scatter | solution.py:129
  227.0 306.2 %reduce-scatter.5.cloned.1.call-start = ((), (), s32[]{:S(2)}) async-start(), calls=%async_computation.6 | async-start | bytes 9437184 | tf_op jit(solution)/shard_map/reduce_scatter | solution.py:129
  266.8 44.6 %copy-start.4 = (bf16[2,2,256,2048]{3,2,1,0:T(8,128)(2,1)S(1)}, bf16[2,2,256,2048]{3,2,1,0:T(8,128)(2,1)}, u32[]{:S(2)}) copy-start(bf16[2,2,256,2048]{3,2,1,0:T(8,128)(2,1)} %copy-done.3) | copy-start | bytes 12582916
  369.7 216.1 %all-gather.11.cloned.1.call-start = ((), (), s32[]{:S(2)}) async-start(), calls=%async_computation.7 | async-start | bytes 5242880 | tf_op jit(solution)/shard_map/all_gather | solution.py:80
  374.0 26.0 %collective-permute-start.4 = (bf16[2,256,1024]{2,1,0:T(8,128)(2,1)S(1)}, bf16[2,256,1024]{2,1,0:T(8,128)(2,1)S(1)}, u32[]{:S(2)}, u32[]{:S(2)}) collective-permute-start(bf16[2,256,1024]{2,1,0:T(8,128)(2,1)S(1)} %dynamic-slice_bitcast_fusion.3), channel_id=1, source_target_pairs={{0,16},{8,24},{16,0},{24,8},{1,17},{9,25},{17,1},{25,9},{2,18},{10... | collective-permute-start | bytes 3145736 | tf_op jit(solution)/shard_map/ppermute | solution.py:96
  376.0 26.1 %collective-permute-start.5 = (bf16[2,256,1024]{2,1,0:T(8,128)(2,1)S(1)}, bf16[2,256,1024]{2,1,0:T(8,128)(2,1)S(1)}, u32[]{:S(2)}, u32[]{:S(2)}) collective-permute-start(bf16[2,256,1024]{2,1,0:T(8,128)(2,1)S(1)} %dynamic-slice_bitcast_fusion.2), channel_id=1, source_target_pairs={{0,8},{8,0},{16,24},{24,16},{1,9},{9,1},{17,25},{25,17},{2,10},{10... | collective-permute-start | bytes 3145736 | tf_op jit(solution)/shard_map/ppermute | solution.py:96
  378.3 46.3 %collective-permute-start.9 = (bf16[2,256,1024]{2,1,0:T(8,128)(2,1)S(1)}, bf16[2,256,1024]{2,1,0:T(8,128)(2,1)S(1)}, u32[]{:S(2)}, u32[]{:S(2)}) collective-permute-start(bf16[2,256,1024]{2,1,0:T(8,128)(2,1)S(1)} %dynamic-slice_bitcast_fusion), channel_id=1, source_target_pairs={{0,8},{8,0},{16,24},{24,16},{1,9},{9,1},{17,25},{25,17},{2,10},{10... | collective-permute-start | bytes 3145736 | tf_op jit(solution)/shard_map/ppermute | solution.py:96
  379.0 43.6 %collective-permute-start.8 = (bf16[2,256,1024]{2,1,0:T(8,128)(2,1)S(1)}, bf16[2,256,1024]{2,1,0:T(8,128)(2,1)S(1)}, u32[]{:S(2)}, u32[]{:S(2)}) collective-permute-start(bf16[2,256,1024]{2,1,0:T(8,128)(2,1)S(1)} %dynamic-slice_bitcast_fusion.1), channel_id=1, source_target_pairs={{0,16},{8,24},{16,0},{24,8},{1,17},{9,25},{17,1},{25,9},{2,18},{10... | collective-permute-start | bytes 3145736 | tf_op jit(solution)/shard_map/ppermute | solution.py:96
  402.6 35.1 %collective-permute-start.7 = (bf16[256,1024]{1,0:T(8,128)(2,1)S(1)}, bf16[256,1024]{1,0:T(8,128)(2,1)S(1)}, u32[]{:S(2)}, u32[]{:S(2)}) collective-permute-start(bf16[256,1024]{1,0:T(8,128)(2,1)S(1)} %dynamic-slice_bitcast_fusion.6), channel_id=1, source_target_pairs={{0,16},{8,24},{16,0},{24,8},{1,17},{9,25},{17,1},{25,9},{2,18},{10... | collective-permute-start | bytes 1572872 | tf_op jit(solution)/shard_map/ppermute | solution.py:96
  406.6 18.5 %copy-start.14 = (bf16[2,256,1024]{2,1,0:T(8,128)(2,1)}, bf16[2,256,1024]{2,1,0:T(8,128)(2,1)S(1)}, u32[]{:S(2)}) copy-start(bf16[2,256,1024]{2,1,0:T(8,128)(2,1)S(1)} %fusion.15) | copy-start | bytes 3145732
  406.6 29.2 %collective-permute-start.6 = (bf16[256,1024]{1,0:T(8,128)(2,1)S(1)}, bf16[256,1024]{1,0:T(8,128)(2,1)S(1)}, u32[]{:S(2)}, u32[]{:S(2)}) collective-permute-start(bf16[256,1024]{1,0:T(8,128)(2,1)S(1)} %dynamic-slice_bitcast_fusion.7), channel_id=1, source_target_pairs={{0,8},{8,0},{16,24},{24,16},{1,9},{9,1},{17,25},{25,17},{2,10},{10... | collective-permute-start | bytes 1572872 | tf_op jit(solution)/shard_map/ppermute | solution.py:96
  425.1 25.6 %collective-permute-start.11 = (bf16[256,1024]{1,0:T(8,128)(2,1)S(1)}, bf16[256,1024]{1,0:T(8,128)(2,1)}, u32[]{:S(2)}, u32[]{:S(2)}) collective-permute-start(bf16[256,1024]{1,0:T(8,128)(2,1)S(1)} %dynamic-slice_bitcast_fusion.4), channel_id=1, source_target_pairs={{0,16},{8,24},{16,0},{24,8},{1,17},{9,25},{17,1},{25,9},{2,18},{10... | collective-permute-start | bytes 1572872 | tf_op jit(solution)/shard_map/ppermute | solution.py:96
  429.1 19.1 %collective-permute-start.10 = (bf16[256,1024]{1,0:T(8,128)(2,1)S(1)}, bf16[256,1024]{1,0:T(8,128)(2,1)}, u32[]{:S(2)}, u32[]{:S(2)}) collective-permute-start(bf16[256,1024]{1,0:T(8,128)(2,1)S(1)} %dynamic-slice_bitcast_fusion.5), channel_id=1, source_target_pairs={{0,8},{8,0},{16,24},{24,16},{1,9},{9,1},{17,25},{25,17},{2,10},{10... | collective-permute-start | bytes 1572872 | tf_op jit(solution)/shard_map/ppermute | solution.py:96
  443.4 23.7 %collective-permute-start.19 = (bf16[1,256,2048]{2,1,0:T(8,128)(2,1)}, bf16[1,256,2048]{2,1,0:T(8,128)(2,1)}, u32[]{:S(2)}, u32[]{:S(2)}) collective-permute-start(bf16[1,256,2048]{2,1,0:T(8,128)(2,1)} %get-tuple-element.43), channel_id=1, source_target_pairs={{0,16},{8,24},{16,0},{24,8},{1,17},{9,25},{17,1},{25,9},{2,18},{10... | collective-permute-start | bytes 3145736 | tf_op jit(solution)/shard_map/ppermute | solution.py:68
  443.5 26.1 %collective-permute-start.18 = (bf16[1,256,2048]{2,1,0:T(8,128)(2,1)}, bf16[1,256,2048]{2,1,0:T(8,128)(2,1)}, u32[]{:S(2)}, u32[]{:S(2)}) collective-permute-start(bf16[1,256,2048]{2,1,0:T(8,128)(2,1)} %get-tuple-element.44), channel_id=1, source_target_pairs={{0,8},{8,0},{16,24},{24,16},{1,9},{9,1},{17,25},{25,17},{2,10},{10... | collective-permute-start | bytes 3145736 | tf_op jit(solution)/shard_map/ppermute | solution.py:68
  472.8 46.6 %collective-permute-start.20 = (bf16[2,256,2048]{2,1,0:T(8,128)(2,1)S(1)}, bf16[2,256,2048]{2,1,0:T(8,128)(2,1)S(1)}, u32[]{:S(2)}, u32[]{:S(2)}) collective-permute-start(bf16[2,256,2048]{2,1,0:T(8,128)(2,1)S(1)} %maximum_select_fusion.9), channel_id=1, source_target_pairs={{0,16},{8,24},{16,0},{24,8},{1,17},{9,25},{17,1},{25,9},{2,18},{10... | collective-permute-start | bytes 6291464 | tf_op jit(solution)/shard_map/ppermute | solution.py:68
  480.4 46.3 %collective-permute-start.21 = (bf16[2,256,2048]{2,1,0:T(8,128)(2,1)S(1)}, bf16[2,256,2048]{2,1,0:T(8,128)(2,1)S(1)}, u32[]{:S(2)}, u32[]{:S(2)}) collective-permute-start(bf16[2,256,2048]{2,1,0:T(8,128)(2,1)S(1)} %maximum_select_fusion.10), channel_id=1, source_target_pairs={{0,8},{8,0},{16,24},{24,16},{1,9},{9,1},{17,25},{25,17},{2,10},{10... | collective-permute-start | bytes 6291464 | tf_op jit(solution)/shard_map/ppermute | solution.py:68
  539.7 1.3 collective-permute-start.12
  541.1 2.7 collective-permute-start.13
  543.8 5.7 collective-permute-start.14
  544.5 6.2 %collective-permute-start.16 = (f32[1,2560]{1,0:T(1,128)S(1)}, f32[1,2560]{1,0:T(1,128)S(1)}, u32[]{:S(2)}, u32[]{:S(2)}) collective-permute-start(f32[1,2560]{1,0:T(1,128)S(1)} %fusion.22), channel_id=1, source_target_pairs={{0,2},{1,3},{2,4},{3,5},{8,10},{9,11},{10,12},{11,13},{16,18},{17,... | collective-permute-start | bytes 30728 | tf_op jit(solution)/shard_map/ppermute | solution.py:116
  550.7 6.5 %collective-permute-start.15 = (f32[1,2560]{1,0:T(1,128)S(1)}, f32[1,2560]{1,0:T(1,128)S(1)}, u32[]{:S(2)}, u32[]{:S(2)}) collective-permute-start(f32[1,2560]{1,0:T(1,128)S(1)} %get-tuple-element.61), channel_id=1, source_target_pairs={{2,0},{3,1},{4,2},{5,3},{6,4},{7,5},{10,8},{11,9},{12,10},{13,11},... | collective-permute-start | bytes 30728 | tf_op jit(solution)/shard_map/ppermute | solution.py:116
  552.0 6.6 %collective-permute-start.17 = (f32[1,2560]{1,0:T(1,128)S(1)}, f32[1,2560]{1,0:T(1,128)S(1)}, u32[]{:S(2)}, u32[]{:S(2)}) collective-permute-start(f32[1,2560]{1,0:T(1,128)S(1)} %get-tuple-element.62), channel_id=1, source_target_pairs={{0,2},{1,3},{2,4},{3,5},{4,6},{5,7},{8,10},{9,11},{10,12},{11,13},... | collective-permute-start | bytes 30728 | tf_op jit(solution)/shard_map/ppermute | solution.py:116
  567.7 28.8 %copy-start.31 = (f32[256]{0:T(256)}, f32[256]{0:T(256)S(1)}, u32[]{:S(2)}) copy-start(f32[256]{0:T(256)S(1)} %get-tuple-element.96) | copy-start | bytes 3076
  567.7 9.9 %copy-start.21 = (bf16[2,256,2048]{2,1,0:T(8,128)(2,1)S(1)}, bf16[2,256,2048]{2,1,0:T(8,128)(2,1)}, u32[]{:S(2)}) copy-start(bf16[2,256,2048]{2,1,0:T(8,128)(2,1)} %copy-done.20) | copy-start | bytes 6291460
  (34 other events, 118.9 us)
Sparse Core Ops, SparseCore 0:
  11.8 154.4 all-gather.6
  168.5 80.2 all-gather.8
  251.2 166.7 reduce-scatter.2
  420.7 87.9 reduce-scatter.4
  535.7 50.0 all-gather.10

commit v5 on v4

--- a/solution.py
+++ b/solution.py
@@ -61,11 +61,13 @@
     bits = list(range(count.bit_length() - 1))
     orders = (bits, bits[::-1])
     wholes = [first[None], second[None]]
+    late = None
     for step in bits:
         got = []
         for whole, order in zip(wholes, orders):
             pairs = [(i, i ^ (1 << order[step])) for i in range(count)]
             got.append(lax.ppermute(whole, "seq", pairs))
+        late = got
         for i, order in enumerate(orders):
             low = (me >> order[step]) % 2 == 0
             whole, new = wholes[i], behind(got[i], got[1 - i])
@@ -73,7 +75,8 @@
             wholes[i] = whole.reshape((-1,) + first.shape)
     sizes = (2,) * len(bits) + second.shape
     order = bits[::-1] + [len(bits) + i for i in range(second.ndim)]
-    return wholes[0], wholes[1].reshape(sizes).transpose(order).reshape(wholes[1].shape)
+    second = wholes[1].reshape(sizes).transpose(order).reshape(wholes[1].shape)
+    return wholes[0], second, late
 
 
 def seq_all(block):
@@ -731,7 +734,7 @@
         begin = hidden_cols
     else:
         fc1, fc2, begin = fsdp_gather(fc1_here), fsdp_gather(fc2_here), 0
-    rows_all, grad_rows = seq_gather_two(inputs[0], cotangent[0])
+    rows_all, grad_rows, unused = seq_gather_two(inputs[0], cotangent[0])
     rows_all, grad_rows = rows_all.reshape(length, width), grad_rows.reshape(length, width)
 
     starts_row = doc_starts[0]
@@ -792,10 +795,12 @@
     part_qkv = fsdp_sum(all_qkv)
     part_fc2 = behind(part_fc2, result)
     if joined:
-        whole_fc2, whole_fc1 = seq_gather_two(part_fc2, part_fc1)
+        whole_fc2, whole_fc1, brought = seq_gather_two(part_fc2, part_fc1)
     else:
         whole_fc2, whole_fc1 = seq_all(part_fc2), seq_all(part_fc1)
-    whole_qkv = seq_all(behind(behind(part_qkv, grad_normed), whole_fc1))
+        brought = [whole_fc1, whole_fc2]
+    part_qkv = behind(behind(part_qkv, brought[0]), brought[1])
+    whole_qkv = seq_all(behind(part_qkv, grad_normed))
     output = (inputs[0].astype(F32) + result + (bias_out + bias_fc2)).astype(BF)[None]
     sum_gain, sum_shift = sum_gain[0], sum_shift[0]
     own_std = pick(inv_std.reshape(seqs, tok, 1), me)

time: 612 us -> 616 us (level)
  waiting for transfers between devices: 177 us -> 188 us
    ppermute x8, waiting for transfers between devices: 72.2 us -> 84.1 us  [seq_gather_two(): got.append(lax.ppermute(whole, 'seq', pairs))]
    unnamed x99 -> x95, local copies, waits for them, and re-layouts: 18.1 us -> 13.5 us
    slice x21 -> x20, local copies, waits for them, and re-layouts: 18.3 us -> 17.9 us  [behind(): first = lax.slice(other, (0,) * other.ndim, (1,) * other.ndim).reshape(())]
where the time goes in v5:
time: 616 us; the launch traced here: 607 us
  Pallas kernels  200 us (32%)
  waiting for transfers between devices  188 us (31%)
  local copies, waits for them, and re-layouts  55.3 us (9%)
  other arithmetic  51.3 us (8%)
  between operations  41.3 us (7%)
  starting transfers between devices  38.5 us (6%)
  blocking collectives  27.7 us (4%)
    ppermute x8, waiting for transfers between devices, seq_gather_two(): got.append(lax.ppermute(whole, 'seq', pairs))  84.1 us
    all_gather x2, waiting for transfers between devices, fsdp_gather(): return lax.all_gather(block, 'fsdp', axis=0, tiled=True)  59.2 us
    pallas_call x1, Pallas kernels, attention(): pl.pallas_call(functools.partial(attention_kernel, min(256, length), HEAD...  44.6 us
    ppermute x8, waiting for transfers between devices, seq_sum_halves(): got.append(lax.ppermute(pick(parts[i], 1 - mine, axis), 'seq', pairs))  39.2 us
    pallas_call x2, Pallas kernels, row_terms(): pl.pallas_call(rows_kernel, grid=(count,), in_specs=[pl.BlockSpec((rows,...  28.4 us
    pallas_call x1, Pallas kernels, normed_terms(): pl.pallas_call(normed_kernel, grid=(columns // cut,), in_specs=[whole(one...  23.4 us
    all_gather x1, blocking collectives, per_device(): small = lax.all_gather(small, 'fsdp', axis=0, tiled=True).astype(F32)  20.4 us
    slice x20, local copies, waits for them, and re-layouts, behind(): first = lax.slice(other, (0,) * other.ndim, (1,) * other.ndim).reshape(())  17.9 us
  transfers between devices with their start and end apart: 27, of which 18 were waited for; matrix products, arithmetic and copies ran while one was open for 17% of the time, Pallas kernels for 31%

profile of v5, /device:TPU:0, one launch (start us, length us, event | category | flops | bytes accessed | tf_op | source)
XLA Modules:
  0.0 606.9 jit_solution(3964228991712797611)
XLA Ops:
  7.2 4.4 shard_map.221
  12.9 2.9 collective-permute-start.1
  17.4 21.7 %collective-permute-done.1 = bf16[1,256,2048]{2,1,0:T(8,128)(2,1)} collective-permute-done((bf16[1,256,2048]{2,1,0:T(8,128)(2,1)S(1)}, bf16[1,256,2048]{2,1,0:T(8,128)(2,1)}, u32[]{:S(2)}, u32[]{:S(2)}) %collective-permute-start.1) | collective-permute-done | bytes 1048608 | tf_op jit(solution)/shard_map/ppermute | solution.py:69
  54.7 20.4 %all-gather.2 = bf16[8,1,2816]{2,1,0:T(2,128)(2,1)S(1)} all-gather(bf16[1,1,2816]{2,1,0:T(2,128)(2,1)S(1)} %reshape.736), channel_id=2, replica_groups=mesh['seq'=4,'fsdp'=8] {'fsdp'}, dimensions={0}, use_global_device_ids=true | all-gather | bytes 50688 | tf_op jit(solution)/shard_map/all_gather | solution.py:719
  75.1 4.7 copy.84
  87.9 6.3 %collective-permute-done.3 = bf16[2,256,2048]{2,1,0:T(8,128)(2,1)} collective-permute-done((bf16[2,256,2048]{2,1,0:T(8,128)(2,1)}, bf16[2,256,2048]{2,1,0:T(8,128)(2,1)}, u32[]{:S(2)}, u32[]{:S(2)}) %collective-permute-start.3) | collective-permute-done | bytes 2097184 | tf_op jit(solution)/shard_map/ppermute | solution.py:69
  111.2 6.3 %shard_map.220 = (bf16[1024,2048]{1,0:T(8,128)(2,1)}, f32[1024,1]{1,0:T(8,128)}, f32[1024,1]{1,0:T(8,128)}) custom-call(bf16[1024,2048]{1,0:T(8,128)(2,1)} %bitcast.219, f32[1,2048]{1,0:T(1,128)} %bitcast.258, f32[1,2048]{1,0:T(1,128)} %bitcast.259), custom_call_target="tpu_custom_call" | custom-call | flops 20971520 | bytes 8388608 | tf_op jit(solution)/shard_map/pallas_call | solution.py:308
  122.1 44.2 %all-gather.7.cloned.1.call-done.right_ref.second_ref = bf16[2048,4096]{1,0:T(8,128)(2,1)} async-done(((bf16[256,4096]{1,0:T(8,128)(2,1)}), bf16[2048,4096]{1,0:T(8,128)(2,1)}) %all-gather.7.cloned.1.call-update) | async-done | bytes 16777232 | tf_op jit(solution)/shard_map/all_gather | solution.py:128
  166.4 17.9 %shard_map.222 = (bf16[1024,2048]{1,0:T(8,128)(2,1)}, bf16[1024,2048]{1,0:T(8,128)(2,1)}) custom-call(bf16[1024,2048]{1,0:T(8,128)(2,1)} %get-tuple-element.24.left_ref, bf16[2048,4096]{1,0:T(8,128)(2,1)} %all-gather.7.cloned.1.call-done.right_ref.second_ref, f32[1,2048]{1,0:T(1,128)} %bitcast.265), custom_call_target="tpu_custom_call" | custom-call | flops 8589934592 | bytes 16777216 | tf_op jit(solution)/shard_map/pallas_call | solution.py:376
  184.2 14.2 %shard_map.223.refs_0_ = bf16[2048,4096]{1,0:T(8,128)(2,1)} custom-call(bf16[1024,2048]{1,0:T(8,128)(2,1)} %get-tuple-element.25.left_ref, bf16[1024,2048]{1,0:T(8,128)(2,1)} %bitcast.213), custom_call_target="tpu_custom_call" | custom-call | flops 8589934592 | bytes 8388608 | tf_op jit(solution)/shard_map/pallas_call | solution.py:434
  198.4 14.4 %shard_map.224.right_ref.two_ref = bf16[1024,2048]{1,0:T(8,128)(2,1)} custom-call(bf16[1024,2048]{1,0:T(8,128)(2,1)} %bitcast.214, bf16[2048,4096]{1,0:T(8,128)(2,1)} %all-gather.7.cloned.1.call-done.right_ref.second_ref, bf16[1024,2048]{1,0:T(8,128)(2,1)} %get-tuple-element.26.slope_ref, bf16[2048,4096]{1,0:T(8,128)(2,1)} %shard_map.223.refs_0_), custom_call_target="tpu_custom_call" | custom-call | flops 8589934592 | bytes 12582912 | tf_op jit(solution)/shard_map/pallas_call | solution.py:528
  212.8 14.2 %shard_map.225.refs_0_ = bf16[2048,4096]{1,0:T(8,128)(2,1)} custom-call(bf16[1024,2048]{1,0:T(8,128)(2,1)} %get-tuple-element.24.left_ref, bf16[1024,2048]{1,0:T(8,128)(2,1)} %shard_map.224.right_ref.two_ref, bf16[2048,4096]{1,0:T(8,128)(2,1)} %shard_map.223.refs_0_), custom_call_target="tpu_custom_call", output_to_operand_aliasing={{}: (2, {})} | custom-call | flops 8589934592 | bytes 8388608 | tf_op jit(solution)/shard_map/pallas_call | solution.py:434
  233.9 14.9 %all-gather.9.cloned.1.call-done.both_ref.right_ref.first_ref = bf16[2048,2048]{1,0:T(8,128)(2,1)} async-done(((bf16[256,2048]{1,0:T(8,128)(2,1)}), bf16[2048,2048]{1,0:T(8,128)(2,1)}) %all-gather.9.cloned.1.call-update) | async-done | bytes 8388624 | tf_op jit(solution)/shard_map/all_gather | solution.py:128
  248.9 6.4 %shard_map.226 = (bf16[512,2048]{1,0:T(8,128)(2,1)}, bf16[1024,512]{1,0:T(8,128)(2,1)}) custom-call(bf16[1024,2048]{1,0:T(8,128)(2,1)} %bitcast.215, bf16[2048,2048]{1,0:T(8,128)(2,1)} %all-gather.9.cloned.1.call-done.both_ref.right_ref.first_ref, bf16[2048,4096]{1,0:T(8,128)(2,1)} %shard_map.225.refs_0_), custom_call_target="tpu_custom_call" | custom-call | flops 2147483648 | bytes 8388608 | tf_op jit(solution)/shard_map/pallas_call | solution.py:341
  255.2 11.6 %shard_map.227.qkv_ref = f32[1024,1536]{1,0:T(8,128)} custom-call(bf16[1024,2048]{1,0:T(8,128)(2,1)} %get-tuple-element.24.left_ref, bf16[2048,2048]{1,0:T(8,128)(2,1)} %all-gather.9.cloned.1.call-done.both_ref.right_ref.first_ref, f32[1,1536]{1,0:T(1,128)} %broadcast_in_dim_reshape.12.bias_ref, bf16[1024,512]{1,0:T(8,128)(2,1)} %get-tuple-element.27.refs_0_.grad_ref), custom_call_target="tpu_custom_call" | custom-call | flops 6442450944 | bytes 14680064 | tf_op jit(solution)/shard_map/pallas_call | solution.py:502
  266.8 44.6 %shard_map.228 = (bf16[1024,512]{1,0:T(8,128)(2,1)}, bf16[1024,1536]{1,0:T(8,128)(2,1)}) custom-call(f32[1024,1536]{1,0:T(8,128)} %shard_map.227.qkv_ref, bf16[1024,512]{1,0:T(8,128)(2,1)} %get-tuple-element.27.refs_0_.grad_ref, f32[1024,128]{1,0:T(8,128)} %concatenate.121.cos_ref, f32[1024,128]{1,0:T(8,128)} %concatenate.122.sin_ref, s32[1,1024]{1,0:T(1,128)} %bitcast.260), custom_call_target="tpu_custom_call" | custom-call | flops 12884901888 | bytes 12582912 | tf_op jit(solution)/shard_map/pallas_call | solution.py:225
  311.4 4.9 convolution_convert_fusion
  316.3 15.8 %shard_map.229.refs_0_ = bf16[1024,2048]{1,0:T(8,128)(2,1)} custom-call(bf16[1024,2048]{1,0:T(8,128)(2,1)} %get-tuple-element.25.left_ref, bf16[2048,4096]{1,0:T(8,128)(2,1)} %all-gather.7.cloned.1.call-done.right_ref.second_ref, bf16[1024,512]{1,0:T(8,128)(2,1)} %get-tuple-element.28.second_ref, bf16[512,2048]{1,0:T(8,128)(2,1)} %get-tuple-element.29.weight_ref, ...), custom_call_target="tpu_custom_call" | custom-call | flops 10737418240 | bytes 12582912 | tf_op jit(solution)/shard_map/pallas_call | solution.py:553
  332.2 23.4 %shard_map.230 = (bf16[1024,2048]{1,0:T(8,128)(2,1)}, f32[1,2048]{1,0:T(1,128)}, f32[1,2048]{1,0:T(1,128)}) custom-call(bf16[1024,1536]{1,0:T(8,128)(2,1)} %get-tuple-element.30.refs_0_.one_ref.right_ref, bf16[2048,2048]{1,0:T(8,128)(2,1)} %all-gather.9.cloned.1.call-done.both_ref.right_ref.first_ref, bf16[1024,2048]{1,0:T(8,128)(2,1)} %shard_map.224.right_ref.two_ref, ...), custom_call_target="tpu_custom_call" | custom-call | flops 15032385536 | bytes 16777216 | tf_op jit(solution)/shard_map/pallas_call | solution.py:588
  356.0 13.6 %shard_map.231 = bf16[8,256,2048]{2,1,0:T(8,128)(2,1)} custom-call(s32[8]{0:T(128)} %iota.18.index_ref, bf16[1024,2048]{1,0:T(8,128)(2,1)} %get-tuple-element.24.left_ref, bf16[1024,1536]{1,0:T(8,128)(2,1)} %get-tuple-element.30.refs_0_.one_ref.right_ref, bf16[8,64,2048]{2,1,0:T(8,128)(2,1)} %bitcast.267, bf16[1024,2048]{1,0:T(8,128)(2,1)} %get-tuple-element.33.refs_0_), custom_call_target="tpu_custom_call" | custom-call | flops 6442450944 | bytes 6291456 | tf_op jit(solution)/shard_map/pallas_call | solution.py:474
  381.1 19.0 %collective-permute-done.4 = bf16[2,256,1024]{2,1,0:T(8,128)(2,1)S(1)} collective-permute-done((bf16[2,256,1024]{2,1,0:T(8,128)(2,1)S(1)}, bf16[2,256,1024]{2,1,0:T(8,128)(2,1)S(1)}, u32[]{:S(2)}, u32[]{:S(2)}) %collective-permute-start.4) | collective-permute-done | bytes 1048608 | tf_op jit(solution)/shard_map/ppermute | solution.py:99
  409.0 13.5 %collective-permute-done.8 = bf16[2,256,1024]{2,1,0:T(8,128)(2,1)S(1)} collective-permute-done((bf16[2,256,1024]{2,1,0:T(8,128)(2,1)S(1)}, bf16[2,256,1024]{2,1,0:T(8,128)(2,1)S(1)}, u32[]{:S(2)}, u32[]{:S(2)}) %collective-permute-start.8) | collective-permute-done | bytes 1048608 | tf_op jit(solution)/shard_map/ppermute | solution.py:99
  441.6 4.6 collective-permute-done.10
  452.4 2.9 fusion.19
  463.1 16.4 %collective-permute-done.18 = bf16[1,256,2048]{2,1,0:T(8,128)(2,1)S(1)} collective-permute-done((bf16[1,256,2048]{2,1,0:T(8,128)(2,1)S(1)}, bf16[1,256,2048]{2,1,0:T(8,128)(2,1)S(1)}, u32[]{:S(2)}, u32[]{:S(2)}) %collective-permute-start.18) | collective-permute-done | bytes 1048608 | tf_op jit(solution)/shard_map/ppermute | solution.py:69
  493.4 35.8 %collective-permute-done.20 = bf16[2,256,2048]{2,1,0:T(8,128)(2,1)} collective-permute-done((bf16[2,256,2048]{2,1,0:T(8,128)(2,1)}, bf16[2,256,2048]{2,1,0:T(8,128)(2,1)}, u32[]{:S(2)}, u32[]{:S(2)}) %collective-permute-start.20) | collective-permute-done | bytes 2097184 | tf_op jit(solution)/shard_map/ppermute | solution.py:69
  542.3 4.8 collective-permute-start.16
  549.9 5.8 collective-permute-start.17
  557.1 7.3 %all_to_all.5 = f32[4,1,2560]{2,1,0:T(1,128)S(1)} all-to-all(f32[4,1,2560]{2,1,0:T(1,128)S(1)} %broadcast_in_dim.110), channel_id=1, replica_groups=mesh['seq'=4,'fsdp'=8] {'seq'}, dimensions={0} | all-to-all | bytes 81920 | tf_op jit(solution)/shard_map/all_to_all | solution.py:51
  572.9 7.3 %shard_map.233 = f32[256,8192]{1,0:T(8,128)} custom-call(bf16[4,256,2048]{2,1,0:T(8,128)(2,1)} %bitcast.218), custom_call_target="tpu_custom_call" | custom-call | bytes 12582912 | tf_op jit(solution)/shard_map/pallas_call | solution.py:619
  582.6 4.7 bitcast_convert_fusion
  590.2 5.5 shard_map.232
  (272 shorter events, 131.0 us)
Async XLA Ops:
  7.2 77.1 %copy-start = (bf16[256,2048]{1,0:T(8,128)(2,1)S(1)}, bf16[256,2048]{1,0:T(8,128)(2,1)}, u32[]{:S(2)}) copy-start(bf16[256,2048]{1,0:T(8,128)(2,1)} %param.19) | copy-start | bytes 3145732
  7.2 159.2 %all-gather.7.cloned.1.call-start = ((), (), s32[]{:S(2)}) async-start(), calls=%async_computation.3 | async-start | bytes 18874368 | tf_op jit(solution)/shard_map/all_gather | solution.py:128
  11.7 237.1 %all-gather.9.cloned.1.call-start = ((), (), s32[]{:S(2)}) async-start(), calls=%async_computation.4 | async-start | bytes 9437184 | tf_op jit(solution)/shard_map/all_gather | solution.py:128
  12.9 26.2 %collective-permute-start.1 = (bf16[1,256,2048]{2,1,0:T(8,128)(2,1)S(1)}, bf16[1,256,2048]{2,1,0:T(8,128)(2,1)}, u32[]{:S(2)}, u32[]{:S(2)}) collective-permute-start(bf16[1,256,2048]{2,1,0:T(8,128)(2,1)S(1)} %copy-done.5), channel_id=1, source_target_pairs={{0,8},{8,0},{16,24},{24,16},{1,9},{9,1},{17,25},{25,17},{2,10},{10... | collective-permute-start | bytes 3145736 | tf_op jit(solution)/shard_map/ppermute | solution.py:69
  15.9 25.7 %collective-permute-start = (bf16[1,256,2048]{2,1,0:T(8,128)(2,1)S(1)}, bf16[1,256,2048]{2,1,0:T(8,128)(2,1)}, u32[]{:S(2)}, u32[]{:S(2)}) collective-permute-start(bf16[1,256,2048]{2,1,0:T(8,128)(2,1)S(1)} %copy-done.6), channel_id=1, source_target_pairs={{0,16},{8,24},{16,0},{24,8},{1,17},{9,25},{17,1},{25,9},{2,18},{10... | collective-permute-start | bytes 3145736 | tf_op jit(solution)/shard_map/ppermute | solution.py:69
  47.1 47.1 %collective-permute-start.3 = (bf16[2,256,2048]{2,1,0:T(8,128)(2,1)}, bf16[2,256,2048]{2,1,0:T(8,128)(2,1)}, u32[]{:S(2)}, u32[]{:S(2)}) collective-permute-start(bf16[2,256,2048]{2,1,0:T(8,128)(2,1)} %maximum_select_fusion.6), channel_id=1, source_target_pairs={{0,16},{8,24},{16,0},{24,8},{1,17},{9,25},{17,1},{25,9},{2,18},{10... | collective-permute-start | bytes 6291464 | tf_op jit(solution)/shard_map/ppermute | solution.py:69
  51.9 46.4 %collective-permute-start.2 = (bf16[2,256,2048]{2,1,0:T(8,128)(2,1)}, bf16[2,256,2048]{2,1,0:T(8,128)(2,1)}, u32[]{:S(2)}, u32[]{:S(2)}) collective-permute-start(bf16[2,256,2048]{2,1,0:T(8,128)(2,1)} %maximum_select_fusion.5), channel_id=1, source_target_pairs={{0,8},{8,0},{16,24},{24,16},{1,9},{9,1},{17,25},{25,17},{2,10},{10... | collective-permute-start | bytes 6291464 | tf_op jit(solution)/shard_map/ppermute | solution.py:69
  121.2 331.2 %reduce-scatter.3.cloned.1.call-start = ((), (), s32[]{:S(2)}) async-start(), calls=%async_computation.5 | async-start | bytes 18874368 | tf_op jit(solution)/shard_map/reduce_scatter | solution.py:132
  227.1 309.4 %reduce-scatter.5.cloned.1.call-start = ((), (), s32[]{:S(2)}) async-start(), calls=%async_computation.6 | async-start | bytes 9437184 | tf_op jit(solution)/shard_map/reduce_scatter | solution.py:132
  266.8 44.6 %copy-start.4 = (bf16[2,2,256,2048]{3,2,1,0:T(8,128)(2,1)S(1)}, bf16[2,2,256,2048]{3,2,1,0:T(8,128)(2,1)}, u32[]{:S(2)}) copy-start(bf16[2,2,256,2048]{3,2,1,0:T(8,128)(2,1)} %copy-done.3) | copy-start | bytes 12582916
  369.7 219.2 %all-gather.11.cloned.1.call-start = ((), (), s32[]{:S(2)}) async-start(), calls=%async_computation.7 | async-start | bytes 5242880 | tf_op jit(solution)/shard_map/all_gather | solution.py:83
  374.0 26.0 %collective-permute-start.4 = (bf16[2,256,1024]{2,1,0:T(8,128)(2,1)S(1)}, bf16[2,256,1024]{2,1,0:T(8,128)(2,1)S(1)}, u32[]{:S(2)}, u32[]{:S(2)}) collective-permute-start(bf16[2,256,1024]{2,1,0:T(8,128)(2,1)S(1)} %dynamic-slice_bitcast_fusion.3), channel_id=1, source_target_pairs={{0,16},{8,24},{16,0},{24,8},{1,17},{9,25},{17,1},{25,9},{2,18},{10... | collective-permute-start | bytes 3145736 | tf_op jit(solution)/shard_map/ppermute | solution.py:99
  376.0 26.1 %collective-permute-start.5 = (bf16[2,256,1024]{2,1,0:T(8,128)(2,1)S(1)}, bf16[2,256,1024]{2,1,0:T(8,128)(2,1)S(1)}, u32[]{:S(2)}, u32[]{:S(2)}) collective-permute-start(bf16[2,256,1024]{2,1,0:T(8,128)(2,1)S(1)} %dynamic-slice_bitcast_fusion.2), channel_id=1, source_target_pairs={{0,8},{8,0},{16,24},{24,16},{1,9},{9,1},{17,25},{25,17},{2,10},{10... | collective-permute-start | bytes 3145736 | tf_op jit(solution)/shard_map/ppermute | solution.py:99
  378.3 46.3 %collective-permute-start.9 = (bf16[2,256,1024]{2,1,0:T(8,128)(2,1)S(1)}, bf16[2,256,1024]{2,1,0:T(8,128)(2,1)S(1)}, u32[]{:S(2)}, u32[]{:S(2)}) collective-permute-start(bf16[2,256,1024]{2,1,0:T(8,128)(2,1)S(1)} %dynamic-slice_bitcast_fusion), channel_id=1, source_target_pairs={{0,8},{8,0},{16,24},{24,16},{1,9},{9,1},{17,25},{25,17},{2,10},{10... | collective-permute-start | bytes 3145736 | tf_op jit(solution)/shard_map/ppermute | solution.py:99
  379.0 43.5 %collective-permute-start.8 = (bf16[2,256,1024]{2,1,0:T(8,128)(2,1)S(1)}, bf16[2,256,1024]{2,1,0:T(8,128)(2,1)S(1)}, u32[]{:S(2)}, u32[]{:S(2)}) collective-permute-start(bf16[2,256,1024]{2,1,0:T(8,128)(2,1)S(1)} %dynamic-slice_bitcast_fusion.1), channel_id=1, source_target_pairs={{0,16},{8,24},{16,0},{24,8},{1,17},{9,25},{17,1},{25,9},{2,18},{10... | collective-permute-start | bytes 3145736 | tf_op jit(solution)/shard_map/ppermute | solution.py:99
  402.6 35.8 %collective-permute-start.7 = (bf16[256,1024]{1,0:T(8,128)(2,1)S(1)}, bf16[256,1024]{1,0:T(8,128)(2,1)}, u32[]{:S(2)}, u32[]{:S(2)}) collective-permute-start(bf16[256,1024]{1,0:T(8,128)(2,1)S(1)} %dynamic-slice_bitcast_fusion.6), channel_id=1, source_target_pairs={{0,16},{8,24},{16,0},{24,8},{1,17},{9,25},{17,1},{25,9},{2,18},{10... | collective-permute-start | bytes 1572872 | tf_op jit(solution)/shard_map/ppermute | solution.py:99
  407.5 28.4 %collective-permute-start.6 = (bf16[256,1024]{1,0:T(8,128)(2,1)}, bf16[256,1024]{1,0:T(8,128)(2,1)}, u32[]{:S(2)}, u32[]{:S(2)}) collective-permute-start(bf16[256,1024]{1,0:T(8,128)(2,1)} %dynamic-slice_bitcast_fusion.7), channel_id=1, source_target_pairs={{0,8},{8,0},{16,24},{24,16},{1,9},{9,1},{17,25},{25,17},{2,10},{10... | collective-permute-start | bytes 1572872 | tf_op jit(solution)/shard_map/ppermute | solution.py:99
  425.1 23.6 %collective-permute-start.11 = (bf16[256,1024]{1,0:T(8,128)(2,1)S(1)}, bf16[256,1024]{1,0:T(8,128)(2,1)}, u32[]{:S(2)}, u32[]{:S(2)}) collective-permute-start(bf16[256,1024]{1,0:T(8,128)(2,1)S(1)} %dynamic-slice_bitcast_fusion.4), channel_id=1, source_target_pairs={{0,16},{8,24},{16,0},{24,8},{1,17},{9,25},{17,1},{25,9},{2,18},{10... | collective-permute-start | bytes 1572872 | tf_op jit(solution)/shard_map/ppermute | solution.py:99
  430.0 16.2 %collective-permute-start.10 = (bf16[256,1024]{1,0:T(8,128)(2,1)}, bf16[256,1024]{1,0:T(8,128)(2,1)}, u32[]{:S(2)}, u32[]{:S(2)}) collective-permute-start(bf16[256,1024]{1,0:T(8,128)(2,1)} %dynamic-slice_bitcast_fusion.5), channel_id=1, source_target_pairs={{0,8},{8,0},{16,24},{24,16},{1,9},{9,1},{17,25},{25,17},{2,10},{10... | collective-permute-start | bytes 1572872 | tf_op jit(solution)/shard_map/ppermute | solution.py:99
  455.3 24.2 %collective-permute-start.18 = (bf16[1,256,2048]{2,1,0:T(8,128)(2,1)S(1)}, bf16[1,256,2048]{2,1,0:T(8,128)(2,1)S(1)}, u32[]{:S(2)}, u32[]{:S(2)}) collective-permute-start(bf16[1,256,2048]{2,1,0:T(8,128)(2,1)S(1)} %get-tuple-element.44), channel_id=1, source_target_pairs={{0,8},{8,0},{16,24},{24,16},{1,9},{9,1},{17,25},{25,17},{2,10},{10... | collective-permute-start | bytes 3145736 | tf_op jit(solution)/shard_map/ppermute | solution.py:69
  456.8 24.6 %collective-permute-start.19 = (bf16[1,256,2048]{2,1,0:T(8,128)(2,1)S(1)}, bf16[1,256,2048]{2,1,0:T(8,128)(2,1)S(1)}, u32[]{:S(2)}, u32[]{:S(2)}) collective-permute-start(bf16[1,256,2048]{2,1,0:T(8,128)(2,1)S(1)} %get-tuple-element.45), channel_id=1, source_target_pairs={{0,16},{8,24},{16,0},{24,8},{1,17},{9,25},{17,1},{25,9},{2,18},{10... | collective-permute-start | bytes 3145736 | tf_op jit(solution)/shard_map/ppermute | solution.py:69
  483.1 46.1 %collective-permute-start.20 = (bf16[2,256,2048]{2,1,0:T(8,128)(2,1)}, bf16[2,256,2048]{2,1,0:T(8,128)(2,1)}, u32[]{:S(2)}, u32[]{:S(2)}) collective-permute-start(bf16[2,256,2048]{2,1,0:T(8,128)(2,1)} %maximum_select_fusion.8), channel_id=1, source_target_pairs={{0,8},{8,0},{16,24},{24,16},{1,9},{9,1},{17,25},{25,17},{2,10},{10... | collective-permute-start | bytes 6291464 | tf_op jit(solution)/shard_map/ppermute | solution.py:69
  488.1 45.8 %collective-permute-start.21 = (bf16[2,256,2048]{2,1,0:T(8,128)(2,1)}, bf16[2,256,2048]{2,1,0:T(8,128)(2,1)}, u32[]{:S(2)}, u32[]{:S(2)}) collective-permute-start(bf16[2,256,2048]{2,1,0:T(8,128)(2,1)} %maximum_select_fusion.9), channel_id=1, source_target_pairs={{0,16},{8,24},{16,0},{24,8},{1,17},{9,25},{17,1},{25,9},{2,18},{10... | collective-permute-start | bytes 6291464 | tf_op jit(solution)/shard_map/ppermute | solution.py:69
  491.3 74.9 %copy-start.10 = (bf16[1,256,2048]{2,1,0:T(8,128)(2,1)S(1)}, bf16[1,256,2048]{2,1,0:T(8,128)(2,1)}, u32[]{:S(2)}) copy-start(bf16[1,256,2048]{2,1,0:T(8,128)(2,1)} %copy-done.9) | copy-start | bytes 3145732
  491.5 1.9 collective-permute-start.12
  538.8 27.5 %copy-start.12 = (bf16[1,256,2048]{2,1,0:T(8,128)(2,1)S(1)}, bf16[1,256,2048]{2,1,0:T(8,128)(2,1)}, u32[]{:S(2)}) copy-start(bf16[1,256,2048]{2,1,0:T(8,128)(2,1)} %copy-done.11) | copy-start | bytes 3145732
  538.9 2.8 collective-permute-start.13
  541.7 5.5 collective-permute-start.14
  542.3 6.2 %collective-permute-start.16 = (f32[1,2560]{1,0:T(1,128)S(1)}, f32[1,2560]{1,0:T(1,128)S(1)}, u32[]{:S(2)}, u32[]{:S(2)}) collective-permute-start(f32[1,2560]{1,0:T(1,128)S(1)} %fusion.22), channel_id=1, source_target_pairs={{0,2},{1,3},{2,4},{3,5},{8,10},{9,11},{10,12},{11,13},{16,18},{17,... | collective-permute-start | bytes 30728 | tf_op jit(solution)/shard_map/ppermute | solution.py:119
  548.6 7.1 %collective-permute-start.15 = (f32[1,2560]{1,0:T(1,128)S(1)}, f32[1,2560]{1,0:T(1,128)S(1)}, u32[]{:S(2)}, u32[]{:S(2)}) collective-permute-start(f32[1,2560]{1,0:T(1,128)S(1)} %get-tuple-element.61), channel_id=1, source_target_pairs={{2,0},{3,1},{4,2},{5,3},{6,4},{7,5},{10,8},{11,9},{12,10},{13,11},... | collective-permute-start | bytes 30728 | tf_op jit(solution)/shard_map/ppermute | solution.py:119
  549.9 7.1 %collective-permute-start.17 = (f32[1,2560]{1,0:T(1,128)S(1)}, f32[1,2560]{1,0:T(1,128)S(1)}, u32[]{:S(2)}, u32[]{:S(2)}) collective-permute-start(f32[1,2560]{1,0:T(1,128)S(1)} %get-tuple-element.62), channel_id=1, source_target_pairs={{0,2},{1,3},{2,4},{3,5},{4,6},{5,7},{8,10},{9,11},{10,12},{11,13},... | collective-permute-start | bytes 30728 | tf_op jit(solution)/shard_map/ppermute | solution.py:119
  566.2 33.3 %copy-start.29 = (f32[256]{0:T(256)}, f32[256]{0:T(256)S(1)}, u32[]{:S(2)}) copy-start(f32[256]{0:T(256)S(1)} %get-tuple-element.96) | copy-start | bytes 3076
  (32 other events, 147.7 us)
Sparse Core Ops, SparseCore 0:
  11.8 154.4 all-gather.6
  168.5 80.2 all-gather.8
  251.2 166.7 reduce-scatter.2
  420.8 87.9 reduce-scatter.4
  539.0 49.8 all-gather.10
